TPU v7x, 128 devices: a whole 4x4x4 slice. The times are simulated.
128 devices in a mesh: slab: 16 (over x, y), coil: 8 (over z, core).
Axes of the slice: x: 4, y: 4, z: 4, core: 2. Of those that a mesh axis runs over, the one named last changes fastest.
Arguments:
- samples: bfloat16 [8, 131072, 128], P('coil', 'slab'), may hold values from -6 to 6
- sample_pos: bfloat16 [131072, 64], P('slab'), may hold values from 0 to 64
- block_count: int32 [131072], P('slab'), may hold values from 16 to 64
- grid_block: int32 [131072], P('slab'), may hold values from 0 to 16383
- block_slab: int32 [131072, 1], P('slab'), may hold values from 0 to 15, as said below
- sensitivity: bfloat16 [8, 256, 16, 512], P(None, 'slab', 'coil'), may hold values from -3 to 3
Outputs:
- image: float32 [256, 16, 512], P('slab', 'coil')
Inputs may be any that keep to these rules, and one draw needn't show every extreme that they name: `block_slab`: within the rows of one device no slab is named more than 1280 times; one slab, the same for every device, is named exactly 1280 times by every device.
All inputs are finite; a program needn't handle non-finite values.
Results may differ from a plain program's by a relative error of at most 0.02.
The roundings to bfloat16 on the way count: a program that leaves them out, or rounds other values in their place, can miss the bound.
Values may be sent and summed in bfloat16 or wider, within the bound.
No kernel may reach another device: no remote copies, remote signals or barrier semaphores. Data moves between devices by JAX's collectives and lax.ppermute only.
A program may use at most 128 MiB of HBM per device.

v0:
```python
import math

import jax
import jax.numpy as jnp
from jax import lax
from jax.sharding import PartitionSpec as P

KX = 256


kernel_half = 2.5


def block_weights(positions, counts):
    cell_mid = jnp.arange(positions.shape[-1], dtype=jnp.int32).astype(jnp.float32) + 0.5
    offset = (positions.astype(jnp.float32)[..., :, None] - cell_mid) / kernel_half
    bump = jnp.maximum(1.0 - offset * offset, 0.0)
    live = jnp.arange(positions.shape[-1], dtype=jnp.int32)[:, None] < counts[..., None, None]
    return jnp.where(live, bump * bump, 0.0).astype(jnp.bfloat16)


def twiddle(first, second, length):
    phase = (first * second % length).astype(jnp.float32) * (2.0 * math.pi / length)
    scale = 1.0 / math.sqrt(length)
    return (jnp.cos(phase) * scale, jnp.sin(phase) * scale)


def choose(part_in, part_out, cosine, sine):
    upper = jnp.where(part_out == 0, cosine, sine)
    lower = jnp.where(part_out == 0, -sine, cosine)
    return jnp.where(part_in == 0, upper, lower).astype(jnp.bfloat16)


def across_table(kx_len, rows_out):
    index_in = jnp.arange(2 * kx_len, dtype=jnp.int32)
    segment = index_in // 128
    part_in = index_in // 64 % 2
    cell_at = segment * 64 + index_in % 64
    index_out = jnp.arange(2 * rows_out, dtype=jnp.int32)
    part_out = index_out // rows_out
    row_at = (kx_len - rows_out) // 2 + index_out % rows_out
    cosine, sine = twiddle(cell_at[:, None], row_at[None, :], kx_len)
    return choose(part_in[:, None], part_out[None, :], cosine, sine)


def square_table(length):
    index_in = jnp.arange(2 * length, dtype=jnp.int32)
    index_out = jnp.arange(2 * length, dtype=jnp.int32)
    cosine, sine = twiddle((index_in // 2)[:, None], (index_out % length)[None, :], length)
    return choose((index_in % 2)[:, None], (index_out // length)[None, :], cosine, sine)


def depth_table(positions, freqs, length):
    cosine, sine = twiddle(positions[:, None], freqs[None, :], length)
    upper = jnp.stack([cosine, -sine], axis=-1)
    lower = jnp.stack([sine, cosine], axis=-1)
    return jnp.stack([upper, lower], axis=1).astype(jnp.bfloat16)


def conj_sum(coil_maps, coil_images, half):
    map_re = coil_maps[..., :half].astype(jnp.float32)
    map_im = coil_maps[..., half:].astype(jnp.float32)
    img_re = coil_images[..., :half].astype(jnp.float32)
    img_im = coil_images[..., half:].astype(jnp.float32)
    real_part = jnp.sum(map_re * img_re + map_im * img_im, axis=1)
    imag_part = jnp.sum(map_re * img_im - map_im * img_re, axis=1)
    return jnp.concatenate([real_part, imag_part], axis=-1)


def grid_samples(values, positions, counts):
    row_total = values.shape[0]
    group_len = math.gcd(row_total, 1024)
    coil_count = values.shape[1] // 128

    def one_group(pieces):
        group_vals, group_pos, group_cnt = pieces
        weights = block_weights(group_pos, group_cnt)
        shaped = group_vals.reshape(group_len, coil_count, 2, 64)
        result = jnp.einsum("mij,mcpi->mcpj", weights, shaped, preferred_element_type=jnp.float32)
        return result.reshape(group_len, coil_count * 128).astype(jnp.bfloat16)

    grouped = (
        values.reshape(row_total // group_len, group_len, values.shape[1]),
        positions.reshape(row_total // group_len, group_len, positions.shape[1]),
        counts.reshape(row_total // group_len, group_len),
    )
    return lax.map(one_group, grouped).reshape(row_total, values.shape[1])


def pack_rows(block_slab, slab_total, capacity, members):
    dest_slab = block_slab[:, 0]
    onehot = (dest_slab[:, None] == jnp.arange(slab_total, dtype=jnp.int32)[None, :]).astype(
        jnp.int32
    )
    before = jnp.cumsum(onehot, axis=0) - onehot
    rank_row = jnp.sum(before * onehot, axis=1)
    slot_index = dest_slab * capacity + rank_row
    packed = []
    for member in members:
        buffer = (
            jnp.zeros((slab_total * capacity,) + member.shape[1:], member.dtype)
            .at[slot_index]
            .set(member)
        )
        packed.append(buffer.reshape((slab_total, capacity) + member.shape[1:]))
    return tuple(packed)


def per_device(samples, sample_pos, block_count, grid_block, block_slab, sensitivity):
    slab_total = lax.axis_size("slab")
    coils_here = samples.shape[0]
    blocks_here = samples.shape[1]
    capacity = 5 * blocks_here // (2 * slab_total)
    planes = sensitivity.shape[1]
    width_rows = sensitivity.shape[2] * lax.axis_size("coil")
    depth_len = planes * slab_total
    freq_len = sensitivity.shape[3] // 2
    seg_count = KX // 64
    values = jnp.transpose(samples, (1, 0, 2)).reshape(blocks_here, coils_here * 128)
    block_meta = jnp.stack([block_count, grid_block], axis=1)
    sent_values, sent_pos, sent_meta = pack_rows(
        block_slab, slab_total, capacity, (values, sample_pos, block_meta)
    )
    slot_vals = lax.all_to_all(sent_values, "slab", split_axis=0, concat_axis=0, tiled=True)
    slot_pos = lax.all_to_all(sent_pos, "slab", split_axis=0, concat_axis=0, tiled=True)
    slot_meta = lax.all_to_all(sent_meta, "slab", split_axis=0, concat_axis=0, tiled=True)
    leading = slot_vals.shape[:2]
    gridded = grid_samples(
        slot_vals.reshape(-1, slot_vals.shape[2]),
        slot_pos.reshape(-1, slot_pos.shape[2]),
        slot_meta[:, :, 0].reshape(-1),
    )
    cell_rows = gridded.reshape(leading + (gridded.shape[1],))
    segment_of = slot_meta[:, :, 1]
    grid_rows = planes * freq_len * seg_count
    cell_wide = lax.optimization_barrier(cell_rows).astype(jnp.float32)
    kspace = (
        jnp.zeros((grid_rows, cell_rows.shape[2]), jnp.float32)
        .at[segment_of.reshape(-1)]
        .add(cell_wide.reshape(-1, cell_rows.shape[2]))
    )
    kspace = kspace.astype(jnp.bfloat16).reshape(planes * freq_len, seg_count, coils_here, 128)
    across = across_table(KX, width_rows).reshape(seg_count, 128, 2 * width_rows)
    x_rows = jnp.einsum("rscf,sfn->rcn", kspace, across, preferred_element_type=jnp.float32).astype(
        jnp.bfloat16
    )
    x_rows = x_rows.reshape(planes, freq_len, coils_here, 2, width_rows)
    y_table = square_table(freq_len).reshape(freq_len, 2, 2 * freq_len)
    y_planes = jnp.einsum(
        "zkcqx,kqn->zcxn", x_rows, y_table, preferred_element_type=jnp.float32
    ).astype(jnp.bfloat16)
    shaped = y_planes.reshape(planes, coils_here, width_rows, 2, freq_len)
    own_planes = lax.axis_index("slab") * planes + jnp.arange(planes, dtype=jnp.int32)
    table = depth_table(
        jnp.arange(lax.axis_size("slab") * planes, dtype=jnp.int32), own_planes, depth_len
    )
    result = jnp.einsum("zpkq,kcxqy->zcxpy", table, shaped, preferred_element_type=jnp.float32)
    coil_image = lax.psum_scatter(
        result.reshape(lax.axis_size("slab") * planes, coils_here, width_rows, 2 * freq_len).astype(
            jnp.bfloat16
        ),
        "slab",
        scatter_dimension=0,
        tiled=True,
    )
    coil_index = lax.axis_index("coil")
    own_maps = lax.dynamic_slice_in_dim(
        lax.all_gather(sensitivity, "coil", axis=2, tiled=True),
        coil_index * coils_here,
        coils_here,
        0,
    )
    partial_sum = conj_sum(jnp.swapaxes(own_maps, 0, 1), coil_image, freq_len)
    image = lax.psum_scatter(
        partial_sum.astype(jnp.bfloat16), "coil", scatter_dimension=1, tiled=True
    ).astype(jnp.float32)
    return image


def solution(mesh):
    return jax.shard_map(
        per_device,
        mesh=mesh,
        in_specs=(
            P("coil", "slab", None),
            P("slab", None),
            P("slab"),
            P("slab"),
            P("slab", None),
            P(None, "slab", "coil", None),
        ),
        out_specs=P("slab", "coil", None),
        check_vma=False,
    )
```

profile of v0, /device:TPU:0, one launch (start us, length us, event | category | flops | bytes accessed | tf_op | source)
XLA Modules:
  0.0 1139.5 jit_solution(82848419456415012)
XLA Ops:
  8.3 4.8 reduce-window.6
  14.1 1.2 fusion.26
  16.9 2.8 copy.45
  19.7 25.5 %scatter_custom_fusion = s32[20480,2]{1,0:T(8,128)} fusion(s32[8192]{0:T(1024)S(1)} %bitcast.115, s32[8192,2]{1,0:T(8,128)} %copy.45, s32[]{:T(128)} %constant.199.clone.1), kind=kCustom, calls=%fused_computation.20 | custom fusion | bytes 164352 | tf_op jit(solution)/shard_map/scatter | solution.py:103
  45.1 6.7 copy.46
  51.9 7.1 all-to-all-start
  59.0 1.8 copy.47
  60.8 24.6 %scatter_custom_fusion.2 = bf16[20480,64]{1,0:T(8,128)(2,1)} fusion(s32[8192]{0:T(1024)S(1)} %bitcast.116, bf16[8192,64]{1,0:T(8,128)(2,1)} %copy.47, bf16[]{:T(256)} %constant.205.clone.1), kind=kCustom, calls=%fused_computation.26 | custom fusion | bytes 2621952 | tf_op jit(solution)/shard_map/scatter | solution.py:103
  85.4 6.2 copy.48
  91.5 7.3 all-to-all-start.2
  99.8 24.1 %scatter_custom_fusion.1 = bf16[20480,128]{1,0:T(8,128)(2,1)} fusion(s32[8192]{0:T(1024)S(1)} %bitcast.117, bf16[]{:T(256)} %constant.205.clone.1, bf16[1,8192,128]{2,1,0:T(8,128)(2,1)S(1)} %copy-done), kind=kCustom, calls=%fused_computation.28 | custom fusion | bytes 7340034 | tf_op jit(solution)/shard_map/scatter | solution.py:103
  124.2 10.6 all-to-all-done.2
  134.8 4.6 all-to-all-start.1
  139.8 6.0 copy.61
  145.8 56.8 %all-to-all-done.1 = bf16[16,1280,128]{2,1,0:T(8,128)(2,1)} async-done(((bf16[16,1280,128]{2,1,0:T(8,128)(2,1)}), bf16[16,1280,128]{2,1,0:T(8,128)(2,1)}, u32[]{:S(2)}, u32[]{:S(2)}) %all-to-all-start.1) | async-done | bytes 5242912 | tf_op jit(solution)/shard_map/all_to_all | solution.py:124
  202.6 663.4 %while.10 = (s32[]{:T(128)}, bf16[20,1024,128]{2,1,0:T(8,128)(2,1)}, bf16[20,1024,128]{2,1,0:T(8,128)(2,1)}, s32[20,1024]{1,0:T(8,128)S(1)}, bf16[20,1024,64]{2,1,0:T(8,128)(2,1)}, /*index=5*/s32[]{:T(128)}) while((s32[]{:T(128)}, bf16[20,1024,128]{2,1,0:T(8,128)(2,1)}, bf16[20,1024,128]{2,1,0:T(8,128)(2,1)}, s32[20,1024]{1,0:T(8,128)S(1)}, ...), condition=%wide.region_7.8_spmd, body=%wide.region_6.7_spmd.sunk | while | flops 50593920 | bytes 4469841 | solution.py:87
  204.1 1.0 bitcast_convert_fusion.3
  205.4 29.1 %fusion.101 = bf16[1024,2,64]{2,1,0:T(2,128)(2,1)S(1)} fusion(bf16[1024,2,64]{2,1,0:T(2,128)(2,1)S(1)} %copy.82, f32[64]{0:T(128)S(1)} %convert_add_fusion.2, f32[1024,64]{1,0:T(8,128)S(1)} %bitcast_convert_fusion.3, pred[1024,64]{1,0:T(8,128)(4,1)S(1)} %iota_compare_fusion.4), kind=kOutput, calls=%fused_computation.7.clone.2 | convolution fusion | flops 50462720 | bytes 852224 | tf_op jit(solution)/shard_map/while/body/eval_jaxpr/mij,mcpi->mcpj/dot_general | solution.py:79
  238.5 29.1 %fusion.101 = bf16[1024,2,64]{2,1,0:T(2,128)(2,1)S(1)} fusion(bf16[1024,2,64]{2,1,0:T(2,128)(2,1)S(1)} %copy.82, f32[64]{0:T(128)S(1)} %convert_add_fusion.2, f32[1024,64]{1,0:T(8,128)S(1)} %bitcast_convert_fusion.3, pred[1024,64]{1,0:T(8,128)(4,1)S(1)} %iota_compare_fusion.4), kind=kOutput, calls=%fused_computation.7.clone.2 | convolution fusion | flops 50462720 | bytes 852224 | tf_op jit(solution)/shard_map/while/body/eval_jaxpr/mij,mcpi->mcpj/dot_general | solution.py:79
  271.7 29.1 %fusion.101 = bf16[1024,2,64]{2,1,0:T(2,128)(2,1)S(1)} fusion(bf16[1024,2,64]{2,1,0:T(2,128)(2,1)S(1)} %copy.82, f32[64]{0:T(128)S(1)} %convert_add_fusion.2, f32[1024,64]{1,0:T(8,128)S(1)} %bitcast_convert_fusion.3, pred[1024,64]{1,0:T(8,128)(4,1)S(1)} %iota_compare_fusion.4), kind=kOutput, calls=%fused_computation.7.clone.2 | convolution fusion | flops 50462720 | bytes 852224 | tf_op jit(solution)/shard_map/while/body/eval_jaxpr/mij,mcpi->mcpj/dot_general | solution.py:79
  304.9 29.1 %fusion.101 = bf16[1024,2,64]{2,1,0:T(2,128)(2,1)S(1)} fusion(bf16[1024,2,64]{2,1,0:T(2,128)(2,1)S(1)} %copy.82, f32[64]{0:T(128)S(1)} %convert_add_fusion.2, f32[1024,64]{1,0:T(8,128)S(1)} %bitcast_convert_fusion.3, pred[1024,64]{1,0:T(8,128)(4,1)S(1)} %iota_compare_fusion.4), kind=kOutput, calls=%fused_computation.7.clone.2 | convolution fusion | flops 50462720 | bytes 852224 | tf_op jit(solution)/shard_map/while/body/eval_jaxpr/mij,mcpi->mcpj/dot_general | solution.py:79
  338.0 29.1 %fusion.101 = bf16[1024,2,64]{2,1,0:T(2,128)(2,1)S(1)} fusion(bf16[1024,2,64]{2,1,0:T(2,128)(2,1)S(1)} %copy.82, f32[64]{0:T(128)S(1)} %convert_add_fusion.2, f32[1024,64]{1,0:T(8,128)S(1)} %bitcast_convert_fusion.3, pred[1024,64]{1,0:T(8,128)(4,1)S(1)} %iota_compare_fusion.4), kind=kOutput, calls=%fused_computation.7.clone.2 | convolution fusion | flops 50462720 | bytes 852224 | tf_op jit(solution)/shard_map/while/body/eval_jaxpr/mij,mcpi->mcpj/dot_general | solution.py:79
  370.0 1.0 bitcast_convert_fusion.3
  371.2 29.1 %fusion.101 = bf16[1024,2,64]{2,1,0:T(2,128)(2,1)S(1)} fusion(bf16[1024,2,64]{2,1,0:T(2,128)(2,1)S(1)} %copy.82, f32[64]{0:T(128)S(1)} %convert_add_fusion.2, f32[1024,64]{1,0:T(8,128)S(1)} %bitcast_convert_fusion.3, pred[1024,64]{1,0:T(8,128)(4,1)S(1)} %iota_compare_fusion.4), kind=kOutput, calls=%fused_computation.7.clone.2 | convolution fusion | flops 50462720 | bytes 852224 | tf_op jit(solution)/shard_map/while/body/eval_jaxpr/mij,mcpi->mcpj/dot_general | solution.py:79
  404.4 29.1 %fusion.101 = bf16[1024,2,64]{2,1,0:T(2,128)(2,1)S(1)} fusion(bf16[1024,2,64]{2,1,0:T(2,128)(2,1)S(1)} %copy.82, f32[64]{0:T(128)S(1)} %convert_add_fusion.2, f32[1024,64]{1,0:T(8,128)S(1)} %bitcast_convert_fusion.3, pred[1024,64]{1,0:T(8,128)(4,1)S(1)} %iota_compare_fusion.4), kind=kOutput, calls=%fused_computation.7.clone.2 | convolution fusion | flops 50462720 | bytes 852224 | tf_op jit(solution)/shard_map/while/body/eval_jaxpr/mij,mcpi->mcpj/dot_general | solution.py:79
  437.5 29.1 %fusion.101 = bf16[1024,2,64]{2,1,0:T(2,128)(2,1)S(1)} fusion(bf16[1024,2,64]{2,1,0:T(2,128)(2,1)S(1)} %copy.82, f32[64]{0:T(128)S(1)} %convert_add_fusion.2, f32[1024,64]{1,0:T(8,128)S(1)} %bitcast_convert_fusion.3, pred[1024,64]{1,0:T(8,128)(4,1)S(1)} %iota_compare_fusion.4), kind=kOutput, calls=%fused_computation.7.clone.2 | convolution fusion | flops 50462720 | bytes 852224 | tf_op jit(solution)/shard_map/while/body/eval_jaxpr/mij,mcpi->mcpj/dot_general | solution.py:79
  470.7 29.1 %fusion.101 = bf16[1024,2,64]{2,1,0:T(2,128)(2,1)S(1)} fusion(bf16[1024,2,64]{2,1,0:T(2,128)(2,1)S(1)} %copy.82, f32[64]{0:T(128)S(1)} %convert_add_fusion.2, f32[1024,64]{1,0:T(8,128)S(1)} %bitcast_convert_fusion.3, pred[1024,64]{1,0:T(8,128)(4,1)S(1)} %iota_compare_fusion.4), kind=kOutput, calls=%fused_computation.7.clone.2 | convolution fusion | flops 50462720 | bytes 852224 | tf_op jit(solution)/shard_map/while/body/eval_jaxpr/mij,mcpi->mcpj/dot_general | solution.py:79
  503.9 29.1 %fusion.101 = bf16[1024,2,64]{2,1,0:T(2,128)(2,1)S(1)} fusion(bf16[1024,2,64]{2,1,0:T(2,128)(2,1)S(1)} %copy.82, f32[64]{0:T(128)S(1)} %convert_add_fusion.2, f32[1024,64]{1,0:T(8,128)S(1)} %bitcast_convert_fusion.3, pred[1024,64]{1,0:T(8,128)(4,1)S(1)} %iota_compare_fusion.4), kind=kOutput, calls=%fused_computation.7.clone.2 | convolution fusion | flops 50462720 | bytes 852224 | tf_op jit(solution)/shard_map/while/body/eval_jaxpr/mij,mcpi->mcpj/dot_general | solution.py:79
  537.0 29.1 %fusion.101 = bf16[1024,2,64]{2,1,0:T(2,128)(2,1)S(1)} fusion(bf16[1024,2,64]{2,1,0:T(2,128)(2,1)S(1)} %copy.82, f32[64]{0:T(128)S(1)} %convert_add_fusion.2, f32[1024,64]{1,0:T(8,128)S(1)} %bitcast_convert_fusion.3, pred[1024,64]{1,0:T(8,128)(4,1)S(1)} %iota_compare_fusion.4), kind=kOutput, calls=%fused_computation.7.clone.2 | convolution fusion | flops 50462720 | bytes 852224 | tf_op jit(solution)/shard_map/while/body/eval_jaxpr/mij,mcpi->mcpj/dot_general | solution.py:79
  570.2 29.1 %fusion.101 = bf16[1024,2,64]{2,1,0:T(2,128)(2,1)S(1)} fusion(bf16[1024,2,64]{2,1,0:T(2,128)(2,1)S(1)} %copy.82, f32[64]{0:T(128)S(1)} %convert_add_fusion.2, f32[1024,64]{1,0:T(8,128)S(1)} %bitcast_convert_fusion.3, pred[1024,64]{1,0:T(8,128)(4,1)S(1)} %iota_compare_fusion.4), kind=kOutput, calls=%fused_computation.7.clone.2 | convolution fusion | flops 50462720 | bytes 852224 | tf_op jit(solution)/shard_map/while/body/eval_jaxpr/mij,mcpi->mcpj/dot_general | solution.py:79
  603.4 29.1 %fusion.101 = bf16[1024,2,64]{2,1,0:T(2,128)(2,1)S(1)} fusion(bf16[1024,2,64]{2,1,0:T(2,128)(2,1)S(1)} %copy.82, f32[64]{0:T(128)S(1)} %convert_add_fusion.2, f32[1024,64]{1,0:T(8,128)S(1)} %bitcast_convert_fusion.3, pred[1024,64]{1,0:T(8,128)(4,1)S(1)} %iota_compare_fusion.4), kind=kOutput, calls=%fused_computation.7.clone.2 | convolution fusion | flops 50462720 | bytes 852224 | tf_op jit(solution)/shard_map/while/body/eval_jaxpr/mij,mcpi->mcpj/dot_general | solution.py:79
  636.6 29.1 %fusion.101 = bf16[1024,2,64]{2,1,0:T(2,128)(2,1)S(1)} fusion(bf16[1024,2,64]{2,1,0:T(2,128)(2,1)S(1)} %copy.82, f32[64]{0:T(128)S(1)} %convert_add_fusion.2, f32[1024,64]{1,0:T(8,128)S(1)} %bitcast_convert_fusion.3, pred[1024,64]{1,0:T(8,128)(4,1)S(1)} %iota_compare_fusion.4), kind=kOutput, calls=%fused_computation.7.clone.2 | convolution fusion | flops 50462720 | bytes 852224 | tf_op jit(solution)/shard_map/while/body/eval_jaxpr/mij,mcpi->mcpj/dot_general | solution.py:79
  669.7 29.1 %fusion.101 = bf16[1024,2,64]{2,1,0:T(2,128)(2,1)S(1)} fusion(bf16[1024,2,64]{2,1,0:T(2,128)(2,1)S(1)} %copy.82, f32[64]{0:T(128)S(1)} %convert_add_fusion.2, f32[1024,64]{1,0:T(8,128)S(1)} %bitcast_convert_fusion.3, pred[1024,64]{1,0:T(8,128)(4,1)S(1)} %iota_compare_fusion.4), kind=kOutput, calls=%fused_computation.7.clone.2 | convolution fusion | flops 50462720 | bytes 852224 | tf_op jit(solution)/shard_map/while/body/eval_jaxpr/mij,mcpi->mcpj/dot_general | solution.py:79
  702.9 29.1 %fusion.101 = bf16[1024,2,64]{2,1,0:T(2,128)(2,1)S(1)} fusion(bf16[1024,2,64]{2,1,0:T(2,128)(2,1)S(1)} %copy.82, f32[64]{0:T(128)S(1)} %convert_add_fusion.2, f32[1024,64]{1,0:T(8,128)S(1)} %bitcast_convert_fusion.3, pred[1024,64]{1,0:T(8,128)(4,1)S(1)} %iota_compare_fusion.4), kind=kOutput, calls=%fused_computation.7.clone.2 | convolution fusion | flops 50462720 | bytes 852224 | tf_op jit(solution)/shard_map/while/body/eval_jaxpr/mij,mcpi->mcpj/dot_general | solution.py:79
  736.0 29.1 %fusion.101 = bf16[1024,2,64]{2,1,0:T(2,128)(2,1)S(1)} fusion(bf16[1024,2,64]{2,1,0:T(2,128)(2,1)S(1)} %copy.82, f32[64]{0:T(128)S(1)} %convert_add_fusion.2, f32[1024,64]{1,0:T(8,128)S(1)} %bitcast_convert_fusion.3, pred[1024,64]{1,0:T(8,128)(4,1)S(1)} %iota_compare_fusion.4), kind=kOutput, calls=%fused_computation.7.clone.2 | convolution fusion | flops 50462720 | bytes 852224 | tf_op jit(solution)/shard_map/while/body/eval_jaxpr/mij,mcpi->mcpj/dot_general | solution.py:79
  769.2 29.1 %fusion.101 = bf16[1024,2,64]{2,1,0:T(2,128)(2,1)S(1)} fusion(bf16[1024,2,64]{2,1,0:T(2,128)(2,1)S(1)} %copy.82, f32[64]{0:T(128)S(1)} %convert_add_fusion.2, f32[1024,64]{1,0:T(8,128)S(1)} %bitcast_convert_fusion.3, pred[1024,64]{1,0:T(8,128)(4,1)S(1)} %iota_compare_fusion.4), kind=kOutput, calls=%fused_computation.7.clone.2 | convolution fusion | flops 50462720 | bytes 852224 | tf_op jit(solution)/shard_map/while/body/eval_jaxpr/mij,mcpi->mcpj/dot_general | solution.py:79
  802.4 29.1 %fusion.101 = bf16[1024,2,64]{2,1,0:T(2,128)(2,1)S(1)} fusion(bf16[1024,2,64]{2,1,0:T(2,128)(2,1)S(1)} %copy.82, f32[64]{0:T(128)S(1)} %convert_add_fusion.2, f32[1024,64]{1,0:T(8,128)S(1)} %bitcast_convert_fusion.3, pred[1024,64]{1,0:T(8,128)(4,1)S(1)} %iota_compare_fusion.4), kind=kOutput, calls=%fused_computation.7.clone.2 | convolution fusion | flops 50462720 | bytes 852224 | tf_op jit(solution)/shard_map/while/body/eval_jaxpr/mij,mcpi->mcpj/dot_general | solution.py:79
  835.6 29.1 %fusion.101 = bf16[1024,2,64]{2,1,0:T(2,128)(2,1)S(1)} fusion(bf16[1024,2,64]{2,1,0:T(2,128)(2,1)S(1)} %copy.82, f32[64]{0:T(128)S(1)} %convert_add_fusion.2, f32[1024,64]{1,0:T(8,128)S(1)} %bitcast_convert_fusion.3, pred[1024,64]{1,0:T(8,128)(4,1)S(1)} %iota_compare_fusion.4), kind=kOutput, calls=%fused_computation.7.clone.2 | convolution fusion | flops 50462720 | bytes 852224 | tf_op jit(solution)/shard_map/while/body/eval_jaxpr/mij,mcpi->mcpj/dot_general | solution.py:79
  866.0 133.3 %scatter_custom_fusion.3 = f32[16384,128]{1,0:T(8,128)} fusion(s32[20480]{0:T(1024)S(1)} %bitcast.113, bf16[20480,128]{1,0:T(8,128)(2,1)} %bitcast.102, f32[]{:T(128)} %constant.201.clone.1), kind=kCustom, calls=%fused_computation.17 | custom fusion | flops 5242880 | bytes 13631492 | tf_op jit(solution)/shard_map/scatter-add | solution.py:140
  999.2 3.7 convert_element_type.134
  1002.9 1.6 fusion.10
  1004.6 4.7 fusion.18
  1009.4 3.3 bitcast_convert_fusion.1
  1012.6 6.6 copy.56
  1020.3 78.4 %reduce-scatter.3.cloned.1.call-done = bf16[16,1,16,512]{3,0,2,1:T(8,128)(2,1)} async-done(((bf16[256,1,16,512]{3,0,2,1:T(8,128)(2,1)}), bf16[16,1,16,512]{3,0,2,1:T(8,128)(2,1)}) %reduce-scatter.3.cloned.1.call-update) | async-done | bytes 262160 | tf_op jit(solution)/shard_map/reduce_scatter | solution.py:158
  1098.7 1.1 fusion.44
  1100.5 30.1 %reduce-scatter.5.cloned.1.call-done = bf16[16,2,512]{2,0,1:T(8,128)(2,1)} async-done(((bf16[16,16,512]{2,0,1:T(8,128)(2,1)}), bf16[16,2,512]{2,0,1:T(8,128)(2,1)}) %reduce-scatter.5.cloned.1.call-update) | async-done | bytes 32784 | tf_op jit(solution)/shard_map/reduce_scatter | solution.py:174
  1130.6 1.4 copy.57
  (240 shorter events, 85.1 us)
Async XLA Ops:
  7.4 92.5 %copy-start = (bf16[1,8192,128]{2,1,0:T(8,128)(2,1)S(1)}, bf16[1,8192,128]{2,1,0:T(8,128)(2,1)}, u32[]{:S(2)}) copy-start(bf16[1,8192,128]{2,1,0:T(8,128)(2,1)} %param.8) | copy-start | bytes 6291460
  45.1 13.8 %copy-start.2 = (bf16[8192,64]{0,1:T(8,128)(2,1)S(1)}, bf16[8192,64]{0,1:T(8,128)(2,1)}, u32[]{:S(2)}) copy-start(bf16[8192,64]{0,1:T(8,128)(2,1)} %param.9) | copy-start | bytes 3145732
  51.9 39.7 %all-to-all-start = ((s32[16,1280,2]{1,2,0:T(2,128)}), s32[16,1280,2]{1,2,0:T(2,128)S(1)}, u32[]{:S(2)}, u32[]{:S(2)}) async-start(s32[16,1280,2]{1,2,0:T(2,128)} %copy.46), calls=%async_computation | async-start | bytes 327680 | tf_op jit(solution)/shard_map/all_to_all | solution.py:126
  85.3 13.7 %copy-start.3 = (bf16[8,16,2,512]{3,2,1,0:T(2,128)(2,1)S(1)}, bf16[8,16,2,512]{3,2,1,0:T(2,128)(2,1)}, u32[]{:S(2)}) copy-start(bf16[8,16,2,512]{3,2,1,0:T(2,128)(2,1)} %param.13) | copy-start | bytes 786436
  91.5 43.2 %all-to-all-start.2 = ((bf16[16,1280,64]{1,2,0:T(8,128)(2,1)}), bf16[16,1280,64]{1,2,0:T(8,128)(2,1)}, u32[]{:S(2)}, u32[]{:S(2)}) async-start(bf16[16,1280,64]{1,2,0:T(8,128)(2,1)} %copy.48), calls=%async_computation.2 | async-start | bytes 5242880 | tf_op jit(solution)/shard_map/all_to_all | solution.py:125
  98.8 920.5 %all-gather.2.cloned.1.call-start = ((), (), s32[]{:S(2)}) async-start(), calls=%async_computation.5 | async-start | bytes 2359296 | tf_op jit(solution)/shard_map/all_gather | solution.py:168
  134.8 67.8 %all-to-all-start.1 = ((bf16[16,1280,128]{2,1,0:T(8,128)(2,1)}), bf16[16,1280,128]{2,1,0:T(8,128)(2,1)}, u32[]{:S(2)}, u32[]{:S(2)}) async-start(bf16[16,1280,128]{2,1,0:T(8,128)(2,1)} %bitcast.98), calls=%async_computation.1 | async-start | bytes 10485760 | tf_op jit(solution)/shard_map/all_to_all | solution.py:124
  139.4 959.3 %reduce-scatter.3.cloned.1.call-start = ((), (), s32[]{:S(2)}) async-start(), calls=%async_computation.6 | async-start | bytes 4456448 | tf_op jit(solution)/shard_map/reduce_scatter | solution.py:158
  1012.6 119.4 %copy-start.1 = (bf16[1,8192,128]{2,1,0:T(8,128)(2,1)S(1)}, bf16[1,8192,128]{2,1,0:T(8,128)(2,1)}, u32[]{:S(2)}) copy-start(bf16[1,8192,128]{2,1,0:T(8,128)(2,1)} %param.8) | copy-start | bytes 6291460
  1019.2 111.4 %reduce-scatter.5.cloned.1.call-start = ((), (), s32[]{:S(2)}) async-start(), calls=%async_computation.7 | async-start | bytes 294912 | tf_op jit(solution)/shard_map/reduce_scatter | solution.py:174
Sparse Core Ops, SparseCore 0:
  101.4 27.8 all-gather.1
  1100.6 29.9 reduce-scatter.4
Sparse Core Ops, SparseCore 1:
  1019.3 79.3 reduce-scatter.2
where the time goes:
time: 1140 us
  matrix products  592 us (52%)
  waiting for transfers between devices  176 us (15%)
  other arithmetic  172 us (15%)
  local copies, waits for them, and re-layouts  164 us (14%)
  starting transfers between devices  19.3 us (2%)
  between operations  15.1 us (1%)
    dot_general x20, matrix products, one_group(): jnp.einsum('mij,mcpi->mcpj', weights, shaped, preferred_element_type=jnp....  582 us
    scatter-add x1, other arithmetic, per_device(): kspace = jnp.zeros((grid_rows, cell_rows.shape[2]), jnp.float32).at[segme...  133 us
    reduce_scatter x1, waiting for transfers between devices, per_device(): lax.psum_scatter(result.reshape(lax.axis_size('slab') * planes, coils_her...  78.4 us
    scatter x3, local copies, waits for them, and re-layouts, pack_rows(): buffer = jnp.zeros((slab_total * capacity,) + member.shape[1:], member.dt...  74.1 us
    all_to_all x1, waiting for transfers between devices, per_device(): lax.all_to_all(sent_values, 'slab', split_axis=0, concat_axis=0, tiled=True)  56.8 us
    reduce_scatter x1, waiting for transfers between devices, per_device(): lax.psum_scatter(partial_sum.astype(jnp.bfloat16), 'coil', scatter_dimens...  30.1 us
  transfers between devices with their start and end apart: 6, of which 4 were waited for; matrix products, arithmetic and copies ran while one was open for 77% of the time, Pallas kernels for 0%

commit v1 on v0

v1 whole, which is shorter than its diff:
```python
import functools
import math

import jax
import jax.numpy as jnp
import numpy as np
from jax import lax
from jax.experimental import pallas as pl
from jax.experimental.pallas import tpu as pltpu
from jax.sharding import PartitionSpec as P

KX = 256
KY = 256
Z = 256
XW = 16
CELLS = 64
STEP = 512
GATHER = 2048
NT = (((1,), (1,)), ((), ()))


def twiddle(first, second, length):
    phase = (first * second % length).astype(np.float32) * np.float32(2.0 * math.pi / length)
    scale = 1.0 / math.sqrt(length)
    return np.cos(phase) * scale, np.sin(phase) * scale


def across_table():
    cell = np.arange(CELLS)
    rows = (KX - XW) // 2 + np.arange(XW)
    table = np.zeros((KX // CELLS, XW, 2, 2, 2, CELLS), np.float32)
    for s in range(KX // CELLS):
        cosine, sine = twiddle((s * CELLS + cell)[None, :], rows[:, None], KX)
        table[s, :, 0, 0] = cosine[:, None, :]
        table[s, :, 1, 0] = sine[:, None, :]
        table[s, :, 0, 1] = -sine[:, None, :]
        table[s, :, 1, 1] = cosine[:, None, :]
    return table.reshape(KX // CELLS * XW * 2, 4 * CELLS)


def line_table(length):
    index = np.arange(length)
    cosine, sine = twiddle(index[:, None], index[None, :], length)
    return np.block([[cosine, -sine], [sine, cosine]])


def depth_tables(length):
    index = np.arange(length)
    cosine, sine = twiddle(index[:, None], index[None, :], length)
    return np.stack([cosine, sine, -sine])


def grid_kernel(pos_ref, count_ref, seg_ref, samples_ref, table_ref, out_ref, pos_s, g_s):
    tiles = STEP // 32
    sample = lax.broadcasted_iota(jnp.int32, (CELLS, STEP), 0)
    live = sample < count_ref[...]
    pos = jnp.where(live, pos_ref[...].astype(jnp.float32) * 0.4, -100.0)
    pos_s[:, 0:CELLS] = pos.T
    mids = (lax.broadcasted_iota(jnp.int32, (CELLS, 256), 0).astype(jnp.float32) + 0.5) * 0.4
    low = lax.broadcasted_iota(jnp.int32, (8, 128), 1) < 64
    sub = lax.broadcasted_iota(jnp.int32, (32, 128), 0) % 8
    lane_half = lax.broadcasted_iota(jnp.int32, (32, 128), 1) // 64
    keep = lane_half == sub % 2
    group = sub // 2

    def one_tile(t, carry):
        start = pl.multiple_of(t * 32, 32)
        pos_rows = pos_s[pl.ds(start, 32), :]
        halves = []
        for h in range(2):
            even = pos_rows[16 * h : 16 * h + 8]
            odd = pltpu.roll(pos_rows[16 * h + 8 : 16 * h + 16], 64, 1)
            halves.append(jnp.where(low, even, odd))
        row4 = jnp.concatenate(halves, axis=1)
        parts = []
        for nb in range(8):
            offset = row4[nb : nb + 1, :] - mids
            bump = jnp.maximum(1.0 - offset * offset, 0.0)
            parts.append((bump * bump).astype(jnp.bfloat16))
        weights = jnp.concatenate(parts, axis=0)
        vals = samples_ref[pl.ds(start, 32), :].astype(jnp.float32)
        zero = jnp.zeros((8, 128), jnp.float32)
        lhs = []
        for p in range(2):
            for kb in range(4):
                piece = vals[8 * kb : 8 * kb + 8]
                if kb % 2 != p:
                    piece = pltpu.roll(piece, 64, 1)
                piece = jnp.where(low == (kb % 2 == 0), piece, 0.0)
                lhs.append(jnp.concatenate([piece, zero] if kb < 2 else [zero, piece], axis=1))
        lhs = jnp.concatenate(lhs, axis=0).astype(jnp.bfloat16)
        full = lax.dot_general(lhs, weights, NT, preferred_element_type=jnp.float32)
        sides = []
        for p in range(2):
            block = full[32 * p : 32 * p + 32]
            own = jnp.where(group == 0, block[:, 0:128], block[:, 128:256])
            own = jnp.where(group == 2, block[:, 256:384], own)
            own = jnp.where(group == 3, block[:, 384:512], own)
            sides.append(jnp.where(keep, own, 0.0))
        g_s[pl.ds(start, 32), :] = jnp.concatenate(sides, axis=1).astype(jnp.bfloat16)
        return carry

    lax.fori_loop(0, tiles, one_tile, 0, unroll=2)
    every = lax.dot_general(table_ref[...], g_s[...], NT, preferred_element_type=jnp.float32)
    seg = seg_ref[...]
    own = jnp.where(seg == 0, every[0:32], every[32:64])
    own = jnp.where(seg == 2, every[64:96], own)
    own = jnp.where(seg == 3, every[96:128], own)
    out_ref[...] = own.astype(jnp.bfloat16)


def grid_blocks(pos_t, count, seg, samples, table):
    blocks = samples.shape[0]
    return pl.pallas_call(
        grid_kernel,
        grid=(blocks // STEP,),
        in_specs=[
            pl.BlockSpec((CELLS, STEP), lambda i: (0, i)),
            pl.BlockSpec((1, STEP), lambda i: (0, i)),
            pl.BlockSpec((1, STEP), lambda i: (0, i)),
            pl.BlockSpec((STEP, 128), lambda i: (i, 0)),
            pl.BlockSpec((128, 256), lambda i: (0, 0)),
        ],
        out_specs=pl.BlockSpec((32, STEP), lambda i: (0, i)),
        out_shape=jax.ShapeDtypeStruct((32, blocks), jnp.bfloat16),
        scratch_shapes=[pltpu.VMEM((STEP, 128), jnp.float32), pltpu.VMEM((STEP, 256), jnp.bfloat16)],
        compiler_params=pltpu.CompilerParams(vmem_limit_bytes=48 * 1024 * 1024),
        name="grid_blocks",
    )(pos_t, count, seg, samples, table)


def place_kernel(values_ref, index_ref, y_ref, z_ref, out_ref, acc):
    first = (pl.program_id(0) == 0) & (pl.program_id(1) == 0)
    last = (pl.program_id(0) == pl.num_programs(0) - 1) & (pl.program_id(1) == pl.num_programs(1) - 1)

    @pl.when(first)
    def _():
        acc[...] = jnp.zeros_like(acc)

    iota = lax.broadcasted_iota(jnp.int32, (256, GATHER), 0).astype(jnp.float32).astype(jnp.bfloat16)
    depth = index_ref[0, 0:1, :]
    line = index_ref[0, 1:2, :]
    one = jnp.ones((), jnp.bfloat16)
    zero = jnp.zeros((), jnp.bfloat16)
    planes = jnp.where(iota == depth, one, zero)
    hit = iota == line
    for p in range(2):
        spread = jnp.where(hit, values_ref[0, p : p + 1, :], zero)
        acc[256 * p : 256 * p + 256, :] += lax.dot_general(
            spread, planes, NT, preferred_element_type=jnp.float32
        )

    @pl.when(last)
    def _():
        x_rows = acc[...].astype(jnp.bfloat16)
        y_t = jnp.dot(y_ref[...], x_rows, preferred_element_type=jnp.float32).astype(jnp.bfloat16)
        real, imag = y_t[0:256], y_t[256:512]

        def turn(table, side):
            return lax.dot_general(table, side, NT, preferred_element_type=jnp.float32)

        out_ref[:, 0:256] = (turn(z_ref[0], real) + turn(z_ref[2], imag)).astype(jnp.bfloat16)
        out_ref[:, 256:512] = (turn(z_ref[1], real) + turn(z_ref[0], imag)).astype(jnp.bfloat16)


def place_blocks(values, index, y_table, z_tables):
    sources, _, blocks = values.shape
    return pl.pallas_call(
        place_kernel,
        grid=(sources, blocks // GATHER),
        in_specs=[
            pl.BlockSpec((1, 2, GATHER), lambda i, j: (i, 0, j)),
            pl.BlockSpec((1, 2, GATHER), lambda i, j: (i, 0, j)),
            pl.BlockSpec((512, 512), lambda i, j: (0, 0)),
            pl.BlockSpec((3, 256, 256), lambda i, j: (0, 0, 0)),
        ],
        out_specs=pl.BlockSpec((256, 512), lambda i, j: (0, 0)),
        out_shape=jax.ShapeDtypeStruct((256, 512), jnp.bfloat16),
        scratch_shapes=[pltpu.VMEM((512, 256), jnp.float32)],
        compiler_params=pltpu.CompilerParams(vmem_limit_bytes=48 * 1024 * 1024),
        name="place_blocks",
    )(values, index, y_table, z_tables)


def per_device(samples, sample_pos, block_count, grid_block, block_slab, sensitivity):
    slabs = lax.axis_size("slab")
    groups = lax.axis_size("coil")
    blocks = samples.shape[1]
    planes = sensitivity.shape[1]
    coils = sensitivity.shape[0]
    width = sensitivity.shape[2]
    row = block_slab[:, 0] * (planes * KY * 4) + grid_block
    index = jnp.stack([row // (KY * 4), row // 4 % KY]).astype(jnp.bfloat16)
    index = lax.all_gather(index, "slab", axis=0)
    moved = grid_blocks(
        sample_pos.T,
        block_count[None],
        (grid_block % 4)[None],
        samples[0],
        jnp.asarray(across_table(), jnp.bfloat16),
    )
    moved = moved.reshape(groups, 2 * width, blocks)
    moved = lax.all_to_all(moved, "coil", split_axis=0, concat_axis=0, tiled=True)
    moved = moved.reshape(slabs, 2, blocks)
    moved = lax.all_to_all(moved, "slab", split_axis=0, concat_axis=0, tiled=True)
    whole = place_blocks(
        moved,
        index,
        jnp.asarray(line_table(KY), jnp.bfloat16),
        jnp.asarray(depth_tables(Z), jnp.bfloat16),
    )
    whole = whole.reshape(slabs, planes, 2 * KY)
    own = lax.all_to_all(whole, "slab", split_axis=0, concat_axis=0, tiled=True)
    own = jnp.swapaxes(own.reshape(coils, width, planes, 2 * KY), 1, 2).astype(jnp.float32)
    maps = sensitivity.astype(jnp.float32)
    map_re, map_im = maps[..., :KY], maps[..., KY:]
    img_re, img_im = own[..., :KY], own[..., KY:]
    real_part = jnp.sum(map_re * img_re + map_im * img_im, axis=0)
    imag_part = jnp.sum(map_re * img_im - map_im * img_re, axis=0)
    return jnp.concatenate([real_part, imag_part], axis=-1)


def solution(mesh):
    return jax.shard_map(
        per_device,
        mesh=mesh,
        in_specs=(
            P("coil", "slab", None),
            P("slab", None),
            P("slab"),
            P("slab"),
            P("slab", None),
            P(None, "slab", "coil", None),
        ),
        out_specs=P("slab", "coil", None),
        check_vma=False,
    )
```

time: 1140 us -> 182 us (0.16)
  matrix products: 592 us -> 0 us
  other arithmetic: 172 us -> 1.89 us
  waiting for transfers between devices: 176 us -> 18.7 us
  local copies, waits for them, and re-layouts: 164 us -> 7.19 us
  Pallas kernels: 0 us -> 109 us
  blocking collectives: 0 us -> 26.4 us
  between operations: 15.1 us -> 0.12 us
    dot_general x23 -> x0, matrix products: 592 us -> none  [the longest x20 582 us: one_group(): jnp.einsum('mij,mcpi->mcpj', weights, shaped, preferred_element_type=jnp....]
    scatter-add x1 -> x0, other arithmetic: 133 us -> none  [per_device(): kspace = jnp.zeros((grid_rows, cell_rows.shape[2]), jnp.float32).at[segme...]
    pallas_call x0 -> x2, Pallas kernels: none -> 109 us  [the longest x1 59.2 us: grid_blocks(): pl.pallas_call(grid_kernel, grid=(blocks // STEP,), in_specs=[pl.BlockSpe...]
    reduce_scatter x2 -> x0, waiting for transfers between devices: 109 us -> none  [the longest x1 78.4 us: per_device(): lax.psum_scatter(result.reshape(lax.axis_size('slab') * planes, coils_her...]
    scatter x3 -> x0, local copies, waits for them, and re-layouts: 74.1 us -> none  [pack_rows(): buffer = jnp.zeros((slab_total * capacity,) + member.shape[1:], member.dt...]
    all_to_all x3, waiting for transfers between devices: 67.4 us -> 18.7 us  [the longest x1 10.3 us: per_device(): lax.all_to_all(moved, 'coil', split_axis=0, concat_axis=0, tiled=True)]
    all_gather x0 -> x1, blocking collectives: none -> 26.4 us  [per_device(): index = lax.all_gather(index, 'slab', axis=0)]
    convert_element_type x22 -> x2, other arithmetic: 24.5 us -> 0.1 us  [the longest x1 0.06 us: per_device(): maps = sensitivity.astype(jnp.float32)]
  transfers between devices with their start and end apart: 6 -> 3, of which waited for: 4 -> 2; matrix products, arithmetic and copies ran while one was open for 77% -> 0% of each run, Pallas kernels for 0% -> 0%
where the time goes in v1:
time: 182 us
  Pallas kernels  109 us (60%)
  blocking collectives  26.4 us (15%)
  waiting for transfers between devices  18.7 us (10%)
  starting transfers between devices  18 us (10%)
  local copies, waits for them, and re-layouts  7.19 us (4%)
  other arithmetic  1.89 us (1%)
    pallas_call x1, Pallas kernels, grid_blocks(): pl.pallas_call(grid_kernel, grid=(blocks // STEP,), in_specs=[pl.BlockSpe...  59.2 us
    pallas_call x1, Pallas kernels, place_blocks(): pl.pallas_call(place_kernel, grid=(sources, blocks // GATHER), in_specs=[...  50 us
    all_gather x1, blocking collectives, per_device(): index = lax.all_gather(index, 'slab', axis=0)  26.4 us
    all_to_all x1, waiting for transfers between devices, per_device(): lax.all_to_all(moved, 'coil', split_axis=0, concat_axis=0, tiled=True)  10.3 us
    all_to_all x1, waiting for transfers between devices, per_device(): own = lax.all_to_all(whole, 'slab', split_axis=0, concat_axis=0, tiled=True)  8.4 us
    all_to_all x1, starting transfers between devices, per_device(): lax.all_to_all(moved, 'slab', split_axis=0, concat_axis=0, tiled=True)  7.17 us
    all_to_all x1, starting transfers between devices, per_device(): lax.all_to_all(moved, 'coil', split_axis=0, concat_axis=0, tiled=True)  5.53 us
    all_to_all x1, starting transfers between devices, per_device(): own = lax.all_to_all(whole, 'slab', split_axis=0, concat_axis=0, tiled=True)  5.31 us
  transfers between devices with their start and end apart: 3, of which 2 were waited for; matrix products, arithmetic and copies ran while one was open for 0% of the time, Pallas kernels for 0%

profile of v1, /device:TPU:0, one launch (start us, length us, event | category | flops | bytes accessed | tf_op | source)
XLA Modules:
  0.0 181.6 jit_solution(4734401418532599115)
XLA Ops:
  0.0 0.8 broadcast_multiply_fusion
  0.8 0.8 fusion.2
  1.6 0.0 copy-start
  1.6 1.6 copy-done
  3.2 0.0 copy-start.1
  3.2 1.2 copy-done.1
  4.4 0.0 copy-start.4
  4.4 0.8 copy-done.4
  5.3 0.0 copy-start.5
  5.3 0.8 copy-done.5
  6.0 59.2 %grid_blocks.1 = bf16[32,8192]{1,0:T(8,128)(2,1)S(1)} custom-call(bf16[64,8192]{1,0:T(8,128)(2,1)S(1)} %bitcast.11, s32[1,8192]{1,0:T(1,128)S(1)} %bitcast.13, s32[1,8192]{1,0:T(1,128)S(1)} %bitcast.12, bf16[8192,128]{1,0:T(8,128)(2,1)S(1)} %bitcast.10, bf16[128,256]{1,0:T(8,128)(2,1)S(1)} %copy-done.4), custom_call_target="tpu_custom_call" | custom-call | tf_op jit(solution)/shard_map/grid_blocks/pallas_call | solution.py:114
  65.3 1.0 reshape.47
  66.2 0.0 copy-start.2
  66.2 0.0 copy-start.3
  66.3 5.5 %all-to-all-start = ((bf16[8,4,8192]{2,1,0:T(4,128)(2,1)}), bf16[8,4,8192]{2,1,0:T(4,128)(2,1)S(1)}, u32[]{:S(2)}, u32[]{:S(2)}) async-start(bf16[8,4,8192]{2,1,0:T(4,128)(2,1)} %reshape.47), calls=%async_computation | async-start | bytes 1048576 | tf_op jit(solution)/shard_map/all_to_all | solution.py:203
  71.8 10.3 %all-to-all-done = bf16[8,4,8192]{2,1,0:T(4,128)(2,1)S(1)} async-done(((bf16[8,4,8192]{2,1,0:T(4,128)(2,1)}), bf16[8,4,8192]{2,1,0:T(4,128)(2,1)S(1)}, u32[]{:S(2)}, u32[]{:S(2)}) %all-to-all-start) | async-done | bytes 524320 | tf_op jit(solution)/shard_map/all_to_all | solution.py:203
  82.1 1.1 reshape.48
  83.2 0.0 copy-start.6
  83.2 7.2 %all-to-all-start.1 = ((bf16[16,2,8192]{2,1,0:T(2,128)(2,1)}), bf16[16,2,8192]{2,1,0:T(2,128)(2,1)S(1)}, u32[]{:S(2)}, u32[]{:S(2)}) async-start(bf16[16,2,8192]{2,1,0:T(2,128)(2,1)} %reshape.48), calls=%async_computation.1 | async-start | bytes 1048576 | tf_op jit(solution)/shard_map/all_to_all | solution.py:205
  90.4 0.1 pad_maximum_fusion.1
  90.5 26.4 %all_gather.4.index_ref = bf16[16,2,8192]{2,1,0:T(2,128)(2,1)S(1)} all-gather(bf16[1,2,8192]{2,1,0:T(2,128)(2,1)S(1)} %pad_maximum_fusion.1), channel_id=1, replica_groups=mesh['slab'=16,'coil'=8] {'slab'}, dimensions={0}, use_global_device_ids=true | all-gather | bytes 557056 | tf_op jit(solution)/shard_map/all_gather | solution.py:194
  116.9 0.0 all-to-all-done.1.values_ref
  116.9 0.0 copy-done.2
  116.9 0.0 copy-done.3
  116.9 50.0 %place_blocks.1 = bf16[256,512]{1,0:T(8,128)(2,1)} custom-call(bf16[16,2,8192]{2,1,0:T(2,128)(2,1)S(1)} %all-to-all-done.1.values_ref, bf16[16,2,8192]{2,1,0:T(2,128)(2,1)S(1)} %all_gather.4.index_ref, bf16[512,512]{1,0:T(8,128)(2,1)S(1)} %copy-done.2, bf16[3,256,256]{2,1,0:T(8,128)(2,1)S(1)} %copy-done.3), custom_call_target="tpu_custom_call" | custom-call | tf_op jit(solution)/shard_map/place_blocks/pallas_call | solution.py:168
  166.9 5.3 %all-to-all-start.2 = ((bf16[16,16,512]{2,1,0:T(8,128)(2,1)}), bf16[16,16,512]{2,1,0:T(8,128)(2,1)S(1)}, u32[]{:S(2)}, u32[]{:S(2)}) async-start(bf16[16,16,512]{2,1,0:T(8,128)(2,1)} %bitcast.5), calls=%async_computation.2 | async-start | bytes 524288 | tf_op jit(solution)/shard_map/all_to_all | solution.py:213
  172.2 0.0 copy-done.6
  172.3 0.1 copy_convert_fusion
  172.3 8.4 %all-to-all-done.2 = bf16[16,16,512]{2,1,0:T(8,128)(2,1)S(1)} async-done(((bf16[16,16,512]{2,1,0:T(8,128)(2,1)}), bf16[16,16,512]{2,1,0:T(8,128)(2,1)S(1)}, u32[]{:S(2)}, u32[]{:S(2)}) %all-to-all-start.2) | async-done | bytes 262176 | tf_op jit(solution)/shard_map/all_to_all | solution.py:213
  180.8 0.1 add_reduce_fusion
  180.9 0.7 copy.12
  (4 shorter events, 0.1 us)
Async XLA Ops:
  1.6 1.6 copy-start
  3.2 1.2 copy-start.1
  4.4 0.8 copy-start.4
  5.3 0.8 copy-start.5
  66.2 50.6 %copy-start.2 = (bf16[512,512]{1,0:T(8,128)(2,1)S(1)}, bf16[512,512]{1,0:T(8,128)(2,1)}, u32[]{:S(2)}) copy-start(bf16[512,512]{1,0:T(8,128)(2,1)} %constant.61.clone.y_ref) | copy-start | bytes 1572868
  66.2 50.6 %copy-start.3 = (bf16[3,256,256]{2,1,0:T(8,128)(2,1)S(1)}, bf16[3,256,256]{2,1,0:T(8,128)(2,1)}, u32[]{:S(2)}) copy-start(bf16[3,256,256]{2,1,0:T(8,128)(2,1)} %constant.62.clone.z_ref) | copy-start | bytes 1179652
  66.3 15.9 %all-to-all-start = ((bf16[8,4,8192]{2,1,0:T(4,128)(2,1)}), bf16[8,4,8192]{2,1,0:T(4,128)(2,1)S(1)}, u32[]{:S(2)}, u32[]{:S(2)}) async-start(bf16[8,4,8192]{2,1,0:T(4,128)(2,1)} %reshape.47), calls=%async_computation | async-start | bytes 1048576 | tf_op jit(solution)/shard_map/all_to_all | solution.py:203
  83.2 89.1 %copy-start.6 = (bf16[8,16,2,512]{3,2,1,0:T(2,128)(2,1)S(1)}, bf16[8,16,2,512]{3,2,1,0:T(2,128)(2,1)}, u32[]{:S(2)}) copy-start(bf16[8,16,2,512]{3,2,1,0:T(2,128)(2,1)} %param.14) | copy-start | bytes 786436
  83.2 33.7 %all-to-all-start.1 = ((bf16[16,2,8192]{2,1,0:T(2,128)(2,1)}), bf16[16,2,8192]{2,1,0:T(2,128)(2,1)S(1)}, u32[]{:S(2)}, u32[]{:S(2)}) async-start(bf16[16,2,8192]{2,1,0:T(2,128)(2,1)} %reshape.48), calls=%async_computation.1 | async-start | bytes 1048576 | tf_op jit(solution)/shard_map/all_to_all | solution.py:205
  166.9 13.8 %all-to-all-start.2 = ((bf16[16,16,512]{2,1,0:T(8,128)(2,1)}), bf16[16,16,512]{2,1,0:T(8,128)(2,1)S(1)}, u32[]{:S(2)}, u32[]{:S(2)}) async-start(bf16[16,16,512]{2,1,0:T(8,128)(2,1)} %bitcast.5), calls=%async_computation.2 | async-start | bytes 524288 | tf_op jit(solution)/shard_map/all_to_all | solution.py:213

commit v2 on v1

--- a/solution.py
+++ b/solution.py
@@ -14,8 +14,8 @@
 Z = 256
 XW = 16
 CELLS = 64
-STEP = 512
-GATHER = 2048
+STEP = 1024
+GATHER = 8192
 NT = (((1,), (1,)), ((), ()))
 
 
@@ -100,7 +100,7 @@
         g_s[pl.ds(start, 32), :] = jnp.concatenate(sides, axis=1).astype(jnp.bfloat16)
         return carry
 
-    lax.fori_loop(0, tiles, one_tile, 0, unroll=2)
+    lax.fori_loop(0, tiles, one_tile, 0, unroll=True)
     every = lax.dot_general(table_ref[...], g_s[...], NT, preferred_element_type=jnp.float32)
     seg = seg_ref[...]
     own = jnp.where(seg == 0, every[0:32], every[32:64])
@@ -138,17 +138,15 @@
         acc[...] = jnp.zeros_like(acc)
 
     iota = lax.broadcasted_iota(jnp.int32, (256, GATHER), 0).astype(jnp.float32).astype(jnp.bfloat16)
-    depth = index_ref[0, 0:1, :]
-    line = index_ref[0, 1:2, :]
+    index = index_ref[0].astype(jnp.float32).astype(jnp.bfloat16)
     one = jnp.ones((), jnp.bfloat16)
     zero = jnp.zeros((), jnp.bfloat16)
-    planes = jnp.where(iota == depth, one, zero)
-    hit = iota == line
-    for p in range(2):
-        spread = jnp.where(hit, values_ref[0, p : p + 1, :], zero)
-        acc[256 * p : 256 * p + 256, :] += lax.dot_general(
-            spread, planes, NT, preferred_element_type=jnp.float32
-        )
+    planes = jnp.where(iota == index[0:1], one, zero)
+    hit = iota == index[1:2]
+    spread = [jnp.where(hit, values_ref[0, p : p + 1, :], zero) for p in range(2)]
+    acc[...] += lax.dot_general(
+        jnp.concatenate(spread, axis=0), planes, NT, preferred_element_type=jnp.float32
+    )
 
     @pl.when(last)
     def _():
@@ -190,7 +188,7 @@
     coils = sensitivity.shape[0]
     width = sensitivity.shape[2]
     row = block_slab[:, 0] * (planes * KY * 4) + grid_block
-    index = jnp.stack([row // (KY * 4), row // 4 % KY]).astype(jnp.bfloat16)
+    index = jnp.stack([row // (KY * 4), row // 4 % KY])
     index = lax.all_gather(index, "slab", axis=0)
     moved = grid_blocks(
         sample_pos.T,

time: 182 us -> 142 us (0.78)
  Pallas kernels: 109 us -> 73 us
  starting transfers between devices: 18 us -> 3.53 us
  between operations: 0.12 us -> 13.5 us
  waiting for transfers between devices: 18.7 us -> 8.38 us
  blocking collectives: 26.4 us -> 33.8 us
    all_to_all x0 -> x2, blocking collectives: none -> 33.8 us  [the longest x1 18.1 us: per_device(): lax.all_to_all(moved, 'slab', split_axis=0, concat_axis=0, tiled=True)]
    all_gather x1 -> x0, blocking collectives: 26.4 us -> none  [per_device(): index = lax.all_gather(index, 'slab', axis=0)]
    pallas_call x1, Pallas kernels: 59.2 us -> 33.4 us  [grid_blocks(): pl.pallas_call(grid_kernel, grid=(blocks // STEP,), in_specs=[pl.BlockSpe...]
    all_to_all x2 -> x0, starting transfers between devices: 12.7 us -> none  [the longest x1 7.17 us: per_device(): lax.all_to_all(moved, 'slab', split_axis=0, concat_axis=0, tiled=True)]
    pallas_call x1, Pallas kernels: 50 us -> 39.7 us  [place_blocks(): pl.pallas_call(place_kernel, grid=(sources, blocks // GATHER), in_specs=[...]
    all_to_all x2 -> x0, waiting for transfers between devices: 10.3 us -> none  [the longest x1 10.3 us: per_device(): lax.all_to_all(moved, 'coil', split_axis=0, concat_axis=0, tiled=True)]
    unnamed x14 -> x16, local copies, waits for them, and re-layouts: 4.42 us -> 5.65 us
  transfers between devices with their start and end apart: 3 -> 2, of which waited for: 2 -> 1; matrix products, arithmetic and copies ran while one was open for 0% -> 0% of each run, Pallas kernels for 0% -> 24%
where the time goes in v2:
time: 142 us
  Pallas kernels  73 us (51%)
  blocking collectives  33.8 us (24%)
  between operations  13.5 us (10%)
  waiting for transfers between devices  8.38 us (6%)
  local copies, waits for them, and re-layouts  6.79 us (5%)
  starting transfers between devices  3.53 us (2%)
  other arithmetic  2.48 us (2%)
    pallas_call x1, Pallas kernels, place_blocks(): pl.pallas_call(place_kernel, grid=(sources, blocks // GATHER), in_specs=[...  39.7 us
    pallas_call x1, Pallas kernels, grid_blocks(): pl.pallas_call(grid_kernel, grid=(blocks // STEP,), in_specs=[pl.BlockSpe...  33.4 us
    all_to_all x1, blocking collectives, per_device(): lax.all_to_all(moved, 'slab', split_axis=0, concat_axis=0, tiled=True)  18.1 us
    all_to_all x1, blocking collectives, per_device(): lax.all_to_all(moved, 'coil', split_axis=0, concat_axis=0, tiled=True)  15.7 us
    all_to_all x1, waiting for transfers between devices, per_device(): own = lax.all_to_all(whole, 'slab', split_axis=0, concat_axis=0, tiled=True)  8.36 us
    unnamed x16, local copies, waits for them, and re-layouts  5.65 us
    all_to_all x1, starting transfers between devices, per_device(): own = lax.all_to_all(whole, 'slab', split_axis=0, concat_axis=0, tiled=True)  3.53 us
  transfers between devices with their start and end apart: 2, of which 1 were waited for; matrix products, arithmetic and copies ran while one was open for 0% of the time, Pallas kernels for 24%

profile of v2, /device:TPU:0, one launch (start us, length us, event | category | flops | bytes accessed | tf_op | source)
XLA Modules:
  0.0 141.5 jit_solution(4721172283133785673)
XLA Ops:
  6.5 0.0 all-gather.4.cloned.1.call-start
  6.5 0.8 broadcast_multiply_fusion
  7.3 0.8 add_select_fusion.2
  8.2 0.7 add_bitcast_fusion
  8.8 0.0 all-gather.4.cloned.1.call-update
  8.9 0.0 copy-start
  8.9 1.6 %copy-done = bf16[1,8192,128]{2,1,0:T(8,128)(2,1)S(1)} copy-done((bf16[1,8192,128]{2,1,0:T(8,128)(2,1)S(1)}, bf16[1,8192,128]{2,1,0:T(8,128)(2,1)}, u32[]{:S(2)}) %copy-start) | copy-done | bytes 2097176
  10.5 0.0 copy-start.2
  10.5 1.2 copy-done.2
  11.7 0.0 copy-start.5
  11.7 0.8 copy-done.5
  12.5 0.0 copy-start.6
  12.5 0.8 copy-done.6
  13.3 33.4 %grid_blocks.1 = bf16[32,8192]{1,0:T(8,128)(2,1)S(1)} custom-call(bf16[64,8192]{1,0:T(8,128)(2,1)S(1)} %bitcast.15, s32[1,8192]{1,0:T(1,128)S(1)} %bitcast.17, s32[1,8192]{1,0:T(1,128)S(1)} %bitcast.16, bf16[8192,128]{1,0:T(8,128)(2,1)S(1)} %bitcast.14, bf16[128,256]{1,0:T(8,128)(2,1)S(1)} %copy-done.5), custom_call_target="tpu_custom_call" | custom-call | tf_op jit(solution)/shard_map/grid_blocks/pallas_call | solution.py:114
  46.7 0.0 copy-start.3
  46.7 0.0 copy-start.4
  46.7 0.2 reshape.14
  46.9 15.7 %all_to_all.15 = bf16[8,4,8192]{2,1,0:T(4,128)(2,1)S(1)} all-to-all(bf16[8,4,8192]{2,1,0:T(4,128)(2,1)S(1)} %reshape.14), channel_id=1, replica_groups=mesh['slab'=16,'coil'=8] {'coil'}, dimensions={0} | all-to-all | bytes 1048576 | tf_op jit(solution)/shard_map/all_to_all | solution.py:201
  62.6 0.3 reshape.15
  62.9 0.0 copy-start.7
  62.9 18.1 %all_to_all.16.values_ref = bf16[16,2,8192]{2,1,0:T(2,128)(2,1)S(1)} all-to-all(bf16[16,2,8192]{2,1,0:T(2,128)(2,1)S(1)} %reshape.15), channel_id=1, replica_groups=mesh['slab'=16,'coil'=8] {'slab'}, dimensions={0} | all-to-all | bytes 1048576 | tf_op jit(solution)/shard_map/all_to_all | solution.py:203
  81.0 0.0 all-gather.4.cloned.1.call-done.index_ref
  81.0 0.0 copy-done.3
  81.0 0.0 copy-done.4
  81.0 0.0 copy-start.1
  81.0 1.2 copy-done.1
  82.2 39.7 %place_blocks.1 = bf16[256,512]{1,0:T(8,128)(2,1)} custom-call(bf16[16,2,8192]{2,1,0:T(2,128)(2,1)S(1)} %all_to_all.16.values_ref, s32[16,2,8192]{2,1,0:T(2,128)S(1)} %copy-done.1, bf16[512,512]{1,0:T(8,128)(2,1)S(1)} %copy-done.3, bf16[3,256,256]{2,1,0:T(8,128)(2,1)S(1)} %copy-done.4), custom_call_target="tpu_custom_call" | custom-call | tf_op jit(solution)/shard_map/place_blocks/pallas_call | solution.py:166
  121.9 3.5 %all-to-all-start.2 = ((bf16[16,16,512]{2,1,0:T(8,128)(2,1)}), bf16[16,16,512]{2,1,0:T(8,128)(2,1)S(1)}, u32[]{:S(2)}, u32[]{:S(2)}) async-start(bf16[16,16,512]{2,1,0:T(8,128)(2,1)} %bitcast.8), calls=%async_computation.2 | async-start | bytes 524288 | tf_op jit(solution)/shard_map/all_to_all | solution.py:211
  125.4 0.0 copy-done.7
  125.4 0.1 copy_convert_fusion
  125.5 8.4 %all-to-all-done.2 = bf16[16,16,512]{2,1,0:T(8,128)(2,1)S(1)} async-done(((bf16[16,16,512]{2,1,0:T(8,128)(2,1)}), bf16[16,16,512]{2,1,0:T(8,128)(2,1)S(1)}, u32[]{:S(2)}, u32[]{:S(2)}) %all-to-all-start.2) | async-done | bytes 262176 | tf_op jit(solution)/shard_map/all_to_all | solution.py:211
  133.9 0.1 add_reduce_fusion
  134.0 0.7 copy.12
  (2 shorter events, 0.1 us)
Async XLA Ops:
  6.5 74.4 %all-gather.4.cloned.1.call-start = ((), (), s32[]{:S(2)}) async-start(), calls=%async_computation.3 | async-start | bytes 1114112 | tf_op jit(solution)/shard_map/all_gather | solution.py:192
  8.9 1.6 %copy-start = (bf16[1,8192,128]{2,1,0:T(8,128)(2,1)S(1)}, bf16[1,8192,128]{2,1,0:T(8,128)(2,1)}, u32[]{:S(2)}) copy-start(bf16[1,8192,128]{2,1,0:T(8,128)(2,1)} %param.9) | copy-start | bytes 6291460
  10.5 1.2 copy-start.2
  11.7 0.8 copy-start.5
  12.5 0.8 copy-start.6
  46.7 34.3 %copy-start.3 = (bf16[512,512]{1,0:T(8,128)(2,1)S(1)}, bf16[512,512]{1,0:T(8,128)(2,1)}, u32[]{:S(2)}) copy-start(bf16[512,512]{1,0:T(8,128)(2,1)} %constant.61.clone.y_ref) | copy-start | bytes 1572868
  46.7 34.3 %copy-start.4 = (bf16[3,256,256]{2,1,0:T(8,128)(2,1)S(1)}, bf16[3,256,256]{2,1,0:T(8,128)(2,1)}, u32[]{:S(2)}) copy-start(bf16[3,256,256]{2,1,0:T(8,128)(2,1)} %constant.62.clone.z_ref) | copy-start | bytes 1179652
  62.9 62.6 %copy-start.7 = (bf16[8,16,2,512]{3,2,1,0:T(2,128)(2,1)S(1)}, bf16[8,16,2,512]{3,2,1,0:T(2,128)(2,1)}, u32[]{:S(2)}) copy-start(bf16[8,16,2,512]{3,2,1,0:T(2,128)(2,1)} %param.14) | copy-start | bytes 786436
  81.0 1.2 copy-start.1
  121.9 12.0 %all-to-all-start.2 = ((bf16[16,16,512]{2,1,0:T(8,128)(2,1)}), bf16[16,16,512]{2,1,0:T(8,128)(2,1)S(1)}, u32[]{:S(2)}, u32[]{:S(2)}) async-start(bf16[16,16,512]{2,1,0:T(8,128)(2,1)} %bitcast.8), calls=%async_computation.2 | async-start | bytes 524288 | tf_op jit(solution)/shard_map/all_to_all | solution.py:211
Sparse Core Ops, SparseCore 0:
  9.5 45.0 all-gather.3

commit v3 on v2

--- a/solution.py
+++ b/solution.py
@@ -14,8 +14,9 @@
 Z = 256
 XW = 16
 CELLS = 64
+SLABS = 16
 STEP = 1024
-GATHER = 8192
+TOGETHER = 4
 NT = (((1,), (1,)), ((), ()))
 
 
@@ -50,7 +51,7 @@
     return np.stack([cosine, sine, -sine])
 
 
-def grid_kernel(pos_ref, count_ref, seg_ref, samples_ref, table_ref, out_ref, pos_s, g_s):
+def grid_kernel(pos_ref, count_ref, row_ref, slab_ref, samples_ref, table_ref, out_ref, index_ref, pos_s, g_s):
     tiles = STEP // 32
     sample = lax.broadcasted_iota(jnp.int32, (CELLS, STEP), 0)
     live = sample < count_ref[...]
@@ -102,53 +103,84 @@
 
     lax.fori_loop(0, tiles, one_tile, 0, unroll=True)
     every = lax.dot_general(table_ref[...], g_s[...], NT, preferred_element_type=jnp.float32)
-    seg = seg_ref[...]
+    row = row_ref[...]
+    seg = row % 4
+    plane_rows = KY * KX // CELLS
+    depth = slab_ref[...] * (Z // SLABS) + row // plane_rows
+    line = row // (KX // CELLS) % KY
+    index_ref[...] = jnp.concatenate([depth, line], axis=0).astype(jnp.float32).astype(jnp.bfloat16)
     own = jnp.where(seg == 0, every[0:32], every[32:64])
     own = jnp.where(seg == 2, every[64:96], own)
     own = jnp.where(seg == 3, every[96:128], own)
     out_ref[...] = own.astype(jnp.bfloat16)
 
 
-def grid_blocks(pos_t, count, seg, samples, table):
-    blocks = samples.shape[0]
+def grid_blocks(pos_t, count, row, slab, samples, table, first, blocks):
+    skip = first // STEP
     return pl.pallas_call(
         grid_kernel,
         grid=(blocks // STEP,),
         in_specs=[
-            pl.BlockSpec((CELLS, STEP), lambda i: (0, i)),
-            pl.BlockSpec((1, STEP), lambda i: (0, i)),
-            pl.BlockSpec((1, STEP), lambda i: (0, i)),
-            pl.BlockSpec((STEP, 128), lambda i: (i, 0)),
+            pl.BlockSpec((CELLS, STEP), lambda i: (0, i + skip)),
+            pl.BlockSpec((1, STEP), lambda i: (0, i + skip)),
+            pl.BlockSpec((1, STEP), lambda i: (0, i + skip)),
+            pl.BlockSpec((1, STEP), lambda i: (0, i + skip)),
+            pl.BlockSpec((STEP, 128), lambda i: (i + skip, 0)),
             pl.BlockSpec((128, 256), lambda i: (0, 0)),
         ],
-        out_specs=pl.BlockSpec((32, STEP), lambda i: (0, i)),
-        out_shape=jax.ShapeDtypeStruct((32, blocks), jnp.bfloat16),
+        out_specs=[
+            pl.BlockSpec((2 * XW, STEP), lambda i: (0, i)),
+            pl.BlockSpec((2, STEP), lambda i: (0, i)),
+        ],
+        out_shape=[
+            jax.ShapeDtypeStruct((2 * XW, blocks), jnp.bfloat16),
+            jax.ShapeDtypeStruct((2, blocks), jnp.bfloat16),
+        ],
         scratch_shapes=[pltpu.VMEM((STEP, 128), jnp.float32), pltpu.VMEM((STEP, 256), jnp.bfloat16)],
-        compiler_params=pltpu.CompilerParams(vmem_limit_bytes=48 * 1024 * 1024),
+        compiler_params=pltpu.CompilerParams(vmem_limit_bytes=60 * 1024 * 1024),
+        cost_estimate=pl.CostEstimate(
+            flops=4 * blocks * CELLS * 16 * CELLS, bytes_accessed=8 * blocks * CELLS, transcendentals=0
+        ),
         name="grid_blocks",
-    )(pos_t, count, seg, samples, table)
-
-
-def place_kernel(values_ref, index_ref, y_ref, z_ref, out_ref, acc):
-    first = (pl.program_id(0) == 0) & (pl.program_id(1) == 0)
-    last = (pl.program_id(0) == pl.num_programs(0) - 1) & (pl.program_id(1) == pl.num_programs(1) - 1)
-
-    @pl.when(first)
-    def _():
-        acc[...] = jnp.zeros_like(acc)
-
-    iota = lax.broadcasted_iota(jnp.int32, (256, GATHER), 0).astype(jnp.float32).astype(jnp.bfloat16)
-    index = index_ref[0].astype(jnp.float32).astype(jnp.bfloat16)
+    )(pos_t, count, row, slab, samples, table)
+
+
+def place_step(values_ref, acc):
+    sources, _, length = values_ref.shape
+    iota = lax.broadcasted_iota(jnp.int32, (256, length), 0).astype(jnp.float32).astype(jnp.bfloat16)
     one = jnp.ones((), jnp.bfloat16)
     zero = jnp.zeros((), jnp.bfloat16)
-    planes = jnp.where(iota == index[0:1], one, zero)
-    hit = iota == index[1:2]
-    spread = [jnp.where(hit, values_ref[0, p : p + 1, :], zero) for p in range(2)]
+    planes, spread = [], []
+    for i in range(sources):
+        rows = values_ref[i]
+        planes.append(jnp.where(iota == rows[2:3], one, zero))
+        hit = iota == rows[3:4]
+        both = [jnp.where(hit, rows[p : p + 1], zero) for p in range(2)]
+        spread.append(jnp.concatenate(both, axis=0))
     acc[...] += lax.dot_general(
-        jnp.concatenate(spread, axis=0), planes, NT, preferred_element_type=jnp.float32
-    )
-
-    @pl.when(last)
+        jnp.concatenate(spread, axis=1),
+        jnp.concatenate(planes, axis=1),
+        NT,
+        preferred_element_type=jnp.float32,
+    )
+
+
+def place_first_kernel(values_ref, acc_ref):
+    @pl.when(pl.program_id(0) == 0)
+    def _():
+        acc_ref[...] = jnp.zeros_like(acc_ref)
+
+    place_step(values_ref, acc_ref)
+
+
+def place_last_kernel(values_ref, start_ref, y_ref, z_ref, out_ref, acc):
+    @pl.when(pl.program_id(0) == 0)
+    def _():
+        acc[...] = start_ref[...]
+
+    place_step(values_ref, acc)
+
+    @pl.when(pl.program_id(0) == pl.num_programs(0) - 1)
     def _():
         x_rows = acc[...].astype(jnp.bfloat16)
         y_t = jnp.dot(y_ref[...], x_rows, preferred_element_type=jnp.float32).astype(jnp.bfloat16)
@@ -161,23 +193,45 @@
         out_ref[:, 256:512] = (turn(z_ref[1], real) + turn(z_ref[0], imag)).astype(jnp.bfloat16)
 
 
-def place_blocks(values, index, y_table, z_tables):
+def place_cost(values):
     sources, _, blocks = values.shape
+    return pl.CostEstimate(
+        flops=4 * sources * blocks * KY * Z, bytes_accessed=8 * sources * blocks, transcendentals=0
+    )
+
+
+def place_first(values):
+    sources, rows, blocks = values.shape
     return pl.pallas_call(
-        place_kernel,
-        grid=(sources, blocks // GATHER),
+        place_first_kernel,
+        grid=(sources // TOGETHER,),
+        in_specs=[pl.BlockSpec((TOGETHER, rows, blocks), lambda i: (i, 0, 0))],
+        out_specs=pl.BlockSpec((2 * KY, Z), lambda i: (0, 0)),
+        out_shape=jax.ShapeDtypeStruct((2 * KY, Z), jnp.float32),
+        compiler_params=pltpu.CompilerParams(vmem_limit_bytes=44 * 1024 * 1024),
+        cost_estimate=place_cost(values),
+        name="place_first",
+    )(values)
+
+
+def place_last(values, start, y_table, z_tables):
+    sources, rows, blocks = values.shape
+    return pl.pallas_call(
+        place_last_kernel,
+        grid=(sources // TOGETHER,),
         in_specs=[
-            pl.BlockSpec((1, 2, GATHER), lambda i, j: (i, 0, j)),
-            pl.BlockSpec((1, 2, GATHER), lambda i, j: (i, 0, j)),
-            pl.BlockSpec((512, 512), lambda i, j: (0, 0)),
-            pl.BlockSpec((3, 256, 256), lambda i, j: (0, 0, 0)),
-        ],
-        out_specs=pl.BlockSpec((256, 512), lambda i, j: (0, 0)),
-        out_shape=jax.ShapeDtypeStruct((256, 512), jnp.bfloat16),
-        scratch_shapes=[pltpu.VMEM((512, 256), jnp.float32)],
-        compiler_params=pltpu.CompilerParams(vmem_limit_bytes=48 * 1024 * 1024),
-        name="place_blocks",
-    )(values, index, y_table, z_tables)
+            pl.BlockSpec((TOGETHER, rows, blocks), lambda i: (i, 0, 0)),
+            pl.BlockSpec((2 * KY, Z), lambda i: (0, 0)),
+            pl.BlockSpec((2 * KY, 2 * KY), lambda i: (0, 0)),
+            pl.BlockSpec((3, Z, Z), lambda i: (0, 0, 0)),
+        ],
+        out_specs=pl.BlockSpec((Z, 2 * KY), lambda i: (0, 0)),
+        out_shape=jax.ShapeDtypeStruct((Z, 2 * KY), jnp.bfloat16),
+        scratch_shapes=[pltpu.VMEM((2 * KY, Z), jnp.float32)],
+        compiler_params=pltpu.CompilerParams(vmem_limit_bytes=44 * 1024 * 1024),
+        cost_estimate=place_cost(values),
+        name="place_last",
+    )(values, start, y_table, z_tables)
 
 
 def per_device(samples, sample_pos, block_count, grid_block, block_slab, sensitivity):
@@ -187,28 +241,35 @@
     planes = sensitivity.shape[1]
     coils = sensitivity.shape[0]
     width = sensitivity.shape[2]
-    row = block_slab[:, 0] * (planes * KY * 4) + grid_block
-    index = jnp.stack([row // (KY * 4), row // 4 % KY])
-    index = lax.all_gather(index, "slab", axis=0)
-    moved = grid_blocks(
-        sample_pos.T,
-        block_count[None],
-        (grid_block % 4)[None],
-        samples[0],
-        jnp.asarray(across_table(), jnp.bfloat16),
-    )
-    moved = moved.reshape(groups, 2 * width, blocks)
-    moved = lax.all_to_all(moved, "coil", split_axis=0, concat_axis=0, tiled=True)
-    moved = moved.reshape(slabs, 2, blocks)
-    moved = lax.all_to_all(moved, "slab", split_axis=0, concat_axis=0, tiled=True)
-    whole = place_blocks(
-        moved,
-        index,
+    table = jnp.asarray(across_table(), jnp.bfloat16)
+    half = blocks // 2
+    sent = []
+    for part in range(2):
+        moved, index = grid_blocks(
+            sample_pos.T,
+            block_count[None],
+            grid_block[None],
+            block_slab.reshape(1, blocks),
+            samples[0],
+            table,
+            part * half,
+            half,
+        )
+        index = jnp.broadcast_to(index[None], (slabs, 2, half))
+        sent.append(jnp.concatenate([moved.reshape(slabs, 2, half), index], axis=1))
+    early = lax.all_to_all(sent[0], "slab", split_axis=0, concat_axis=0, tiled=True)
+    early, later = lax.optimization_barrier((early, sent[1]))
+    later = lax.all_to_all(later, "slab", split_axis=0, concat_axis=0, tiled=True)
+    whole = place_last(
+        later,
+        place_first(early),
         jnp.asarray(line_table(KY), jnp.bfloat16),
         jnp.asarray(depth_tables(Z), jnp.bfloat16),
     )
     whole = whole.reshape(slabs, planes, 2 * KY)
     own = lax.all_to_all(whole, "slab", split_axis=0, concat_axis=0, tiled=True)
+    own = own.reshape(groups, width, planes, 2 * KY)
+    own = lax.all_to_all(own, "coil", split_axis=0, concat_axis=0, tiled=True)
     own = jnp.swapaxes(own.reshape(coils, width, planes, 2 * KY), 1, 2).astype(jnp.float32)
     maps = sensitivity.astype(jnp.float32)
     map_re, map_im = maps[..., :KY], maps[..., KY:]

time: 142 us -> 126 us (0.89)
  blocking collectives: 33.8 us -> 15.6 us
  starting transfers between devices: 3.53 us -> 19.7 us
  between operations: 13.5 us -> 0.14 us
  local copies, waits for them, and re-layouts: 6.79 us -> 4.79 us
    all_to_all x2 -> x1, blocking collectives: 33.8 us -> 15.6 us  [per_device(): own = lax.all_to_all(whole, 'slab', split_axis=0, concat_axis=0, tiled=True)]
    all_to_all x1 -> x3, starting transfers between devices: 3.53 us -> 19.7 us  [the longest x1 7.21 us: per_device(): lax.all_to_all(later, 'slab', split_axis=0, concat_axis=0, tiled=True)]
    unnamed x16 -> x6, local copies, waits for them, and re-layouts: 5.65 us -> 0.02 us
    pallas_call x1 -> x2, Pallas kernels: 33.4 us -> 36.9 us  [grid_blocks(): pl.pallas_call(grid_kernel, grid=(blocks // STEP,), in_specs=[pl.BlockSpe...]
    concatenate x0 -> x2, other arithmetic: none -> 2.68 us  [per_device(): sent.append(jnp.concatenate([moved.reshape(slabs, 2, half), index], axis=1))]
    pallas_call x1 -> x2, Pallas kernels: 39.7 us -> 37.2 us  [the longest x1 19 us: place_last(): pl.pallas_call(place_last_kernel, grid=(sources // TOGETHER,), in_specs=[...]
    broadcast_in_dim x0 -> x2, local copies, waits for them, and re-layouts: none -> 1.83 us  [per_device(): index = jnp.broadcast_to(index[None], (slabs, 2, half))]
    reshape x2, local copies, waits for them, and re-layouts: 0.46 us -> 2.26 us  [per_device(): sent.append(jnp.concatenate([moved.reshape(slabs, 2, half), index], axis=1))]
  transfers between devices with their start and end apart: 2 -> 3, of which waited for: 1 -> 1; matrix products, arithmetic and copies ran while one was open for 0% -> 3% of each run, Pallas kernels for 24% -> 29%
where the time goes in v3:
time: 126 us; the launch traced here: 125 us
  Pallas kernels  74.1 us (59%)
  starting transfers between devices  19.7 us (16%)
  blocking collectives  15.6 us (12%)
  waiting for transfers between devices  7.48 us (6%)
  local copies, waits for them, and re-layouts  4.79 us (4%)
  other arithmetic  2.87 us (2%)
    pallas_call x2, Pallas kernels, grid_blocks(): pl.pallas_call(grid_kernel, grid=(blocks // STEP,), in_specs=[pl.BlockSpe...  36.9 us
    pallas_call x1, Pallas kernels, place_last(): pl.pallas_call(place_last_kernel, grid=(sources // TOGETHER,), in_specs=[...  19 us
    pallas_call x1, Pallas kernels, place_first(): pl.pallas_call(place_first_kernel, grid=(sources // TOGETHER,), in_specs=...  18.2 us
    all_to_all x1, blocking collectives, per_device(): own = lax.all_to_all(whole, 'slab', split_axis=0, concat_axis=0, tiled=True)  15.6 us
    all_to_all x1, waiting for transfers between devices, per_device(): own = lax.all_to_all(own, 'coil', split_axis=0, concat_axis=0, tiled=True)  7.47 us
    all_to_all x1, starting transfers between devices, per_device(): lax.all_to_all(later, 'slab', split_axis=0, concat_axis=0, tiled=True)  7.21 us
    all_to_all x1, starting transfers between devices, per_device(): lax.all_to_all(sent[0], 'slab', split_axis=0, concat_axis=0, tiled=True)  7.13 us
    all_to_all x1, starting transfers between devices, per_device(): own = lax.all_to_all(own, 'coil', split_axis=0, concat_axis=0, tiled=True)  5.31 us
  transfers between devices with their start and end apart: 3, of which 1 were waited for; matrix products, arithmetic and copies ran while one was open for 3% of the time, Pallas kernels for 29%

profile of v3, /device:TPU:0, one launch (start us, length us, event | category | flops | bytes accessed | tf_op | source)
XLA Modules:
  0.0 124.6 jit_solution(5396756726947893217)
XLA Ops:
  0.0 18.5 %grid_blocks.2 = (bf16[32,4096]{1,0:T(8,128)(2,1)}, bf16[2,4096]{1,0:T(2,128)(2,1)}) custom-call(bf16[64,8192]{1,0:T(8,128)(2,1)} %bitcast.12, s32[1,8192]{1,0:T(1,128)} %bitcast.14, s32[1,8192]{1,0:T(1,128)} %bitcast.16, s32[1,8192]{1,0:T(1,128)} %bitcast.18, bf16[8192,128]{1,0:T(8,128)(2,1)} %bitcast.10, bf16[128,256]{1,0:T(8,128)(2,1)} %constant.8.clone.table_ref), custom_call_target="tpu_custom_call" | custom-call | flops 1073741824 | bytes 2097152 | tf_op jit(solution)/shard_map/grid_blocks/pallas_call | solution.py:120
  18.5 1.1 reshape.19
  19.6 0.9 broadcast_in_dim.10
  20.5 1.3 %pad_maximum_fusion = bf16[16,4,4096]{2,1,0:T(4,128)(2,1)} fusion(bf16[16,2,4096]{2,1,0:T(2,128)(2,1)S(1)} %broadcast_in_dim.10, bf16[16,2,4096]{2,1,0:T(2,128)(2,1)S(1)} %reshape.19), kind=kLoop, calls=%fused_computation | loop fusion | flops 1048576 | bytes 1048576 | tf_op jit(solution)/shard_map/concatenate | solution.py:259
  21.9 7.1 %all-to-all-start = ((bf16[16,4,4096]{2,1,0:T(4,128)(2,1)}), bf16[16,4,4096]{2,1,0:T(4,128)(2,1)S(1)}, u32[]{:S(2)}, u32[]{:S(2)}) async-start(bf16[16,4,4096]{2,1,0:T(4,128)(2,1)} %pad_maximum_fusion), calls=%async_computation | async-start | bytes 1048576 | tf_op jit(solution)/shard_map/all_to_all | solution.py:260
  29.0 18.4 %grid_blocks.3 = (bf16[32,4096]{1,0:T(8,128)(2,1)}, bf16[2,4096]{1,0:T(2,128)(2,1)}) custom-call(bf16[64,8192]{1,0:T(8,128)(2,1)} %bitcast.13, s32[1,8192]{1,0:T(1,128)} %bitcast.15, s32[1,8192]{1,0:T(1,128)} %bitcast.17, s32[1,8192]{1,0:T(1,128)} %bitcast.19, bf16[8192,128]{1,0:T(8,128)(2,1)} %bitcast.11, bf16[128,256]{1,0:T(8,128)(2,1)} %constant.8.clone.table_ref), custom_call_target="tpu_custom_call" | custom-call | flops 1073741824 | bytes 2097152 | tf_op jit(solution)/shard_map/grid_blocks/pallas_call | solution.py:120
  47.4 1.1 reshape.20
  48.6 0.9 broadcast_in_dim.11
  49.5 1.3 %pad_maximum_fusion.1 = bf16[16,4,4096]{2,1,0:T(4,128)(2,1)} fusion(bf16[16,2,4096]{2,1,0:T(2,128)(2,1)S(1)} %broadcast_in_dim.11, bf16[16,2,4096]{2,1,0:T(2,128)(2,1)S(1)} %reshape.20), kind=kLoop, calls=%fused_computation.1 | loop fusion | flops 1048576 | bytes 1048576 | tf_op jit(solution)/shard_map/concatenate | solution.py:259
  50.9 0.0 all-to-all-done.values_ref
  50.9 7.2 %all-to-all-start.1 = ((bf16[16,4,4096]{2,1,0:T(4,128)(2,1)}), bf16[16,4,4096]{2,1,0:T(4,128)(2,1)S(1)}, u32[]{:S(2)}, u32[]{:S(2)}) async-start(bf16[16,4,4096]{2,1,0:T(4,128)(2,1)} %pad_maximum_fusion.1), calls=%async_computation.1 | async-start | bytes 1048576 | tf_op jit(solution)/shard_map/all_to_all | solution.py:262
  58.1 0.0 copy-start
  58.1 0.0 copy-start.1
  58.1 18.2 %place_first.1.start_ref = f32[512,256]{1,0:T(8,128)S(1)} custom-call(bf16[16,4,4096]{2,1,0:T(4,128)(2,1)S(1)} %all-to-all-done.values_ref), custom_call_target="tpu_custom_call" | custom-call | flops 17179869184 | bytes 524288 | tf_op jit(solution)/shard_map/place_first/pallas_call | solution.py:205
  76.3 0.0 copy-start.2
  76.3 0.0 all-to-all-done.1.values_ref
  76.3 0.0 copy-done
  76.3 0.0 copy-done.1
  76.3 19.0 %place_last.1 = bf16[256,512]{1,0:T(8,128)(2,1)S(1)} custom-call(bf16[16,4,4096]{2,1,0:T(4,128)(2,1)S(1)} %all-to-all-done.1.values_ref, f32[512,256]{1,0:T(8,128)S(1)} %place_first.1.start_ref, bf16[512,512]{1,0:T(8,128)(2,1)S(1)} %copy-done, bf16[3,256,256]{2,1,0:T(8,128)(2,1)S(1)} %copy-done.1), custom_call_target="tpu_custom_call" | custom-call | flops 17179869184 | bytes 524288 | tf_op jit(solution)/shard_map/place_last/pallas_call | solution.py:219
  95.3 15.6 %all_to_all.20 = bf16[16,16,512]{2,1,0:T(8,128)(2,1)} all-to-all(bf16[16,16,512]{2,1,0:T(8,128)(2,1)S(1)} %bitcast.9), channel_id=1, replica_groups=mesh['slab'=16,'coil'=8] {'slab'}, dimensions={0} | all-to-all | bytes 524288 | tf_op jit(solution)/shard_map/all_to_all | solution.py:270
  110.9 5.3 %all-to-all-start.3 = ((bf16[8,2,16,512]{3,2,1,0:T(8,128)(2,1)}), bf16[8,2,16,512]{3,2,1,0:T(8,128)(2,1)S(1)}, u32[]{:S(2)}, u32[]{:S(2)}) async-start(bf16[8,2,16,512]{3,2,1,0:T(8,128)(2,1)} %bitcast.6), calls=%async_computation.3 | async-start | bytes 524288 | tf_op jit(solution)/shard_map/all_to_all | solution.py:272
  116.2 0.0 copy-done.2
  116.2 0.1 copy_convert_fusion
  116.3 7.5 %all-to-all-done.3 = bf16[8,2,16,512]{3,2,1,0:T(8,128)(2,1)S(1)} async-done(((bf16[8,2,16,512]{3,2,1,0:T(8,128)(2,1)}), bf16[8,2,16,512]{3,2,1,0:T(8,128)(2,1)S(1)}, u32[]{:S(2)}, u32[]{:S(2)}) %all-to-all-start.3) | async-done | bytes 262176 | tf_op jit(solution)/shard_map/all_to_all | solution.py:272
  123.8 0.1 add_reduce_fusion
  123.9 0.7 copy.12
  (2 shorter events, 0.1 us)
Async XLA Ops:
  21.9 29.0 %all-to-all-start = ((bf16[16,4,4096]{2,1,0:T(4,128)(2,1)}), bf16[16,4,4096]{2,1,0:T(4,128)(2,1)S(1)}, u32[]{:S(2)}, u32[]{:S(2)}) async-start(bf16[16,4,4096]{2,1,0:T(4,128)(2,1)} %pad_maximum_fusion), calls=%async_computation | async-start | bytes 1048576 | tf_op jit(solution)/shard_map/all_to_all | solution.py:260
  50.9 25.5 %all-to-all-start.1 = ((bf16[16,4,4096]{2,1,0:T(4,128)(2,1)}), bf16[16,4,4096]{2,1,0:T(4,128)(2,1)S(1)}, u32[]{:S(2)}, u32[]{:S(2)}) async-start(bf16[16,4,4096]{2,1,0:T(4,128)(2,1)} %pad_maximum_fusion.1), calls=%async_computation.1 | async-start | bytes 1048576 | tf_op jit(solution)/shard_map/all_to_all | solution.py:262
  58.1 18.2 %copy-start = (bf16[512,512]{1,0:T(8,128)(2,1)S(1)}, bf16[512,512]{1,0:T(8,128)(2,1)}, u32[]{:S(2)}) copy-start(bf16[512,512]{1,0:T(8,128)(2,1)} %constant.9.clone.y_ref) | copy-start | bytes 1572868
  58.1 18.2 %copy-start.1 = (bf16[3,256,256]{2,1,0:T(8,128)(2,1)S(1)}, bf16[3,256,256]{2,1,0:T(8,128)(2,1)}, u32[]{:S(2)}) copy-start(bf16[3,256,256]{2,1,0:T(8,128)(2,1)} %constant.10.clone.z_ref) | copy-start | bytes 1179652
  76.3 39.9 %copy-start.2 = (bf16[8,16,2,512]{3,2,1,0:T(2,128)(2,1)S(1)}, bf16[8,16,2,512]{3,2,1,0:T(2,128)(2,1)}, u32[]{:S(2)}) copy-start(bf16[8,16,2,512]{3,2,1,0:T(2,128)(2,1)} %param.14) | copy-start | bytes 786436
  110.9 12.9 %all-to-all-start.3 = ((bf16[8,2,16,512]{3,2,1,0:T(8,128)(2,1)}), bf16[8,2,16,512]{3,2,1,0:T(8,128)(2,1)S(1)}, u32[]{:S(2)}, u32[]{:S(2)}) async-start(bf16[8,2,16,512]{3,2,1,0:T(8,128)(2,1)} %bitcast.6), calls=%async_computation.3 | async-start | bytes 524288 | tf_op jit(solution)/shard_map/all_to_all | solution.py:272

commit v4 on v3

--- a/solution.py
+++ b/solution.py
@@ -51,7 +51,7 @@
     return np.stack([cosine, sine, -sine])
 
 
-def grid_kernel(pos_ref, count_ref, row_ref, slab_ref, samples_ref, table_ref, out_ref, index_ref, pos_s, g_s):
+def grid_kernel(pos_ref, count_ref, row_ref, slab_ref, samples_ref, table_ref, out_ref, pos_s, g_s):
     tiles = STEP // 32
     sample = lax.broadcasted_iota(jnp.int32, (CELLS, STEP), 0)
     live = sample < count_ref[...]
@@ -108,11 +108,14 @@
     plane_rows = KY * KX // CELLS
     depth = slab_ref[...] * (Z // SLABS) + row // plane_rows
     line = row // (KX // CELLS) % KY
-    index_ref[...] = jnp.concatenate([depth, line], axis=0).astype(jnp.float32).astype(jnp.bfloat16)
+    index = jnp.concatenate([depth, line], axis=0).astype(jnp.float32)
     own = jnp.where(seg == 0, every[0:32], every[32:64])
     own = jnp.where(seg == 2, every[64:96], own)
     own = jnp.where(seg == 3, every[96:128], own)
-    out_ref[...] = own.astype(jnp.bfloat16)
+    sent = jnp.concatenate(
+        [own.reshape(XW, 2, STEP), jnp.broadcast_to(index[None], (XW, 2, STEP))], axis=1
+    )
+    out_ref[...] = sent.astype(jnp.bfloat16)
 
 
 def grid_blocks(pos_t, count, row, slab, samples, table, first, blocks):
@@ -128,14 +131,8 @@
             pl.BlockSpec((STEP, 128), lambda i: (i + skip, 0)),
             pl.BlockSpec((128, 256), lambda i: (0, 0)),
         ],
-        out_specs=[
-            pl.BlockSpec((2 * XW, STEP), lambda i: (0, i)),
-            pl.BlockSpec((2, STEP), lambda i: (0, i)),
-        ],
-        out_shape=[
-            jax.ShapeDtypeStruct((2 * XW, blocks), jnp.bfloat16),
-            jax.ShapeDtypeStruct((2, blocks), jnp.bfloat16),
-        ],
+        out_specs=pl.BlockSpec((XW, 4, STEP), lambda i: (0, 0, i)),
+        out_shape=jax.ShapeDtypeStruct((XW, 4, blocks), jnp.bfloat16),
         scratch_shapes=[pltpu.VMEM((STEP, 128), jnp.float32), pltpu.VMEM((STEP, 256), jnp.bfloat16)],
         compiler_params=pltpu.CompilerParams(vmem_limit_bytes=60 * 1024 * 1024),
         cost_estimate=pl.CostEstimate(
@@ -245,18 +242,18 @@
     half = blocks // 2
     sent = []
     for part in range(2):
-        moved, index = grid_blocks(
-            sample_pos.T,
-            block_count[None],
-            grid_block[None],
-            block_slab.reshape(1, blocks),
-            samples[0],
-            table,
-            part * half,
-            half,
+        sent.append(
+            grid_blocks(
+                sample_pos.T,
+                block_count[None],
+                grid_block[None],
+                block_slab.reshape(1, blocks),
+                samples[0],
+                table,
+                part * half,
+                half,
+            )
         )
-        index = jnp.broadcast_to(index[None], (slabs, 2, half))
-        sent.append(jnp.concatenate([moved.reshape(slabs, 2, half), index], axis=1))
     early = lax.all_to_all(sent[0], "slab", split_axis=0, concat_axis=0, tiled=True)
     early, later = lax.optimization_barrier((early, sent[1]))
     later = lax.all_to_all(later, "slab", split_axis=0, concat_axis=0, tiled=True)

time: 126 us -> 119 us (0.944)
  local copies, waits for them, and re-layouts: 4.79 us -> 0.7 us
  other arithmetic: 2.87 us -> 0.19 us
    concatenate x2 -> x0, other arithmetic: 2.68 us -> none  [per_device(): sent.append(jnp.concatenate([moved.reshape(slabs, 2, half), index], axis=1))]
    reshape x2 -> x0, local copies, waits for them, and re-layouts: 2.26 us -> none  [per_device(): sent.append(jnp.concatenate([moved.reshape(slabs, 2, half), index], axis=1))]
    broadcast_in_dim x2 -> x0, local copies, waits for them, and re-layouts: 1.83 us -> none  [per_device(): index = jnp.broadcast_to(index[None], (slabs, 2, half))]
  transfers between devices with their start and end apart: 3 -> 3, of which waited for: 1 -> 1; matrix products, arithmetic and copies ran while one was open for 3% -> 0% of each run, Pallas kernels for 29% -> 31%
where the time goes in v4:
time: 119 us; the launch traced here: 118 us
  Pallas kernels  74.4 us (63%)
  starting transfers between devices  19.7 us (17%)
  blocking collectives  15.6 us (13%)
  waiting for transfers between devices  7.48 us (6%)
    pallas_call x2, Pallas kernels, grid_blocks(): pl.pallas_call(grid_kernel, grid=(blocks // STEP,), in_specs=[pl.BlockSpe...  37.3 us
    pallas_call x1, Pallas kernels, place_last(): pl.pallas_call(place_last_kernel, grid=(sources // TOGETHER,), in_specs=[...  19 us
    pallas_call x1, Pallas kernels, place_first(): pl.pallas_call(place_first_kernel, grid=(sources // TOGETHER,), in_specs=...  18.2 us
    all_to_all x1, blocking collectives, per_device(): own = lax.all_to_all(whole, 'slab', split_axis=0, concat_axis=0, tiled=True)  15.6 us
    all_to_all x1, waiting for transfers between devices, per_device(): own = lax.all_to_all(own, 'coil', split_axis=0, concat_axis=0, tiled=True)  7.47 us
    all_to_all x1, starting transfers between devices, per_device(): lax.all_to_all(later, 'slab', split_axis=0, concat_axis=0, tiled=True)  7.21 us
    all_to_all x1, starting transfers between devices, per_device(): lax.all_to_all(sent[0], 'slab', split_axis=0, concat_axis=0, tiled=True)  7.12 us
    all_to_all x1, starting transfers between devices, per_device(): own = lax.all_to_all(own, 'coil', split_axis=0, concat_axis=0, tiled=True)  5.32 us
  transfers between devices with their start and end apart: 3, of which 1 were waited for; matrix products, arithmetic and copies ran while one was open for 0% of the time, Pallas kernels for 31%

profile of v4, /device:TPU:0, one launch (start us, length us, event | category | flops | bytes accessed | tf_op | source)
XLA Modules:
  0.0 118.1 jit_solution(581716572396455202)
XLA Ops:
  0.0 18.6 %grid_blocks.2 = bf16[16,4,4096]{2,1,0:T(4,128)(2,1)} custom-call(bf16[64,8192]{1,0:T(8,128)(2,1)} %bitcast.12, s32[1,8192]{1,0:T(1,128)} %bitcast.14, s32[1,8192]{1,0:T(1,128)} %bitcast.16, s32[1,8192]{1,0:T(1,128)} %bitcast.18, bf16[8192,128]{1,0:T(8,128)(2,1)} %bitcast.10, bf16[128,256]{1,0:T(8,128)(2,1)} %constant.8.clone.table_ref), custom_call_target="tpu_custom_call" | custom-call | flops 1073741824 | bytes 2097152 | tf_op jit(solution)/shard_map/grid_blocks/pallas_call | solution.py:123
  18.6 7.1 %all-to-all-start = ((bf16[16,4,4096]{2,1,0:T(4,128)(2,1)}), bf16[16,4,4096]{2,1,0:T(4,128)(2,1)S(1)}, u32[]{:S(2)}, u32[]{:S(2)}) async-start(bf16[16,4,4096]{2,1,0:T(4,128)(2,1)} %grid_blocks.2), calls=%async_computation | async-start | bytes 1048576 | tf_op jit(solution)/shard_map/all_to_all | solution.py:257
  25.8 18.6 %grid_blocks.3 = bf16[16,4,4096]{2,1,0:T(4,128)(2,1)} custom-call(bf16[64,8192]{1,0:T(8,128)(2,1)} %bitcast.13, s32[1,8192]{1,0:T(1,128)} %bitcast.15, s32[1,8192]{1,0:T(1,128)} %bitcast.17, s32[1,8192]{1,0:T(1,128)} %bitcast.19, bf16[8192,128]{1,0:T(8,128)(2,1)} %bitcast.11, bf16[128,256]{1,0:T(8,128)(2,1)} %constant.8.clone.table_ref), custom_call_target="tpu_custom_call" | custom-call | flops 1073741824 | bytes 2097152 | tf_op jit(solution)/shard_map/grid_blocks/pallas_call | solution.py:123
  44.4 0.0 all-to-all-done.values_ref
  44.4 7.2 %all-to-all-start.1 = ((bf16[16,4,4096]{2,1,0:T(4,128)(2,1)}), bf16[16,4,4096]{2,1,0:T(4,128)(2,1)S(1)}, u32[]{:S(2)}, u32[]{:S(2)}) async-start(bf16[16,4,4096]{2,1,0:T(4,128)(2,1)} %grid_blocks.3), calls=%async_computation.1 | async-start | bytes 1048576 | tf_op jit(solution)/shard_map/all_to_all | solution.py:259
  51.6 0.0 copy-start
  51.6 0.0 copy-start.1
  51.6 18.2 %place_first.1.start_ref = f32[512,256]{1,0:T(8,128)S(1)} custom-call(bf16[16,4,4096]{2,1,0:T(4,128)(2,1)S(1)} %all-to-all-done.values_ref), custom_call_target="tpu_custom_call" | custom-call | flops 17179869184 | bytes 524288 | tf_op jit(solution)/shard_map/place_first/pallas_call | solution.py:202
  69.8 0.0 copy-start.2
  69.8 0.0 all-to-all-done.1.values_ref
  69.9 0.0 copy-done
  69.9 0.0 copy-done.1
  69.9 19.0 %place_last.1 = bf16[256,512]{1,0:T(8,128)(2,1)S(1)} custom-call(bf16[16,4,4096]{2,1,0:T(4,128)(2,1)S(1)} %all-to-all-done.1.values_ref, f32[512,256]{1,0:T(8,128)S(1)} %place_first.1.start_ref, bf16[512,512]{1,0:T(8,128)(2,1)S(1)} %copy-done, bf16[3,256,256]{2,1,0:T(8,128)(2,1)S(1)} %copy-done.1), custom_call_target="tpu_custom_call" | custom-call | flops 17179869184 | bytes 524288 | tf_op jit(solution)/shard_map/place_last/pallas_call | solution.py:216
  88.9 15.6 %all_to_all.20 = bf16[16,16,512]{2,1,0:T(8,128)(2,1)} all-to-all(bf16[16,16,512]{2,1,0:T(8,128)(2,1)S(1)} %bitcast.9), channel_id=1, replica_groups=mesh['slab'=16,'coil'=8] {'slab'}, dimensions={0} | all-to-all | bytes 524288 | tf_op jit(solution)/shard_map/all_to_all | solution.py:267
  104.4 5.3 %all-to-all-start.3 = ((bf16[8,2,16,512]{3,2,1,0:T(8,128)(2,1)}), bf16[8,2,16,512]{3,2,1,0:T(8,128)(2,1)S(1)}, u32[]{:S(2)}, u32[]{:S(2)}) async-start(bf16[8,2,16,512]{3,2,1,0:T(8,128)(2,1)} %bitcast.6), calls=%async_computation.3 | async-start | bytes 524288 | tf_op jit(solution)/shard_map/all_to_all | solution.py:269
  109.8 0.0 copy-done.2
  109.8 0.1 copy_convert_fusion
  109.8 7.5 %all-to-all-done.3 = bf16[8,2,16,512]{3,2,1,0:T(8,128)(2,1)S(1)} async-done(((bf16[8,2,16,512]{3,2,1,0:T(8,128)(2,1)}), bf16[8,2,16,512]{3,2,1,0:T(8,128)(2,1)S(1)}, u32[]{:S(2)}, u32[]{:S(2)}) %all-to-all-start.3) | async-done | bytes 262176 | tf_op jit(solution)/shard_map/all_to_all | solution.py:269
  117.4 0.1 add_reduce_fusion
  117.5 0.7 copy.12
  (2 shorter events, 0.1 us)
Async XLA Ops:
  18.6 25.8 %all-to-all-start = ((bf16[16,4,4096]{2,1,0:T(4,128)(2,1)}), bf16[16,4,4096]{2,1,0:T(4,128)(2,1)S(1)}, u32[]{:S(2)}, u32[]{:S(2)}) async-start(bf16[16,4,4096]{2,1,0:T(4,128)(2,1)} %grid_blocks.2), calls=%async_computation | async-start | bytes 1048576 | tf_op jit(solution)/shard_map/all_to_all | solution.py:257
  44.4 25.4 %all-to-all-start.1 = ((bf16[16,4,4096]{2,1,0:T(4,128)(2,1)}), bf16[16,4,4096]{2,1,0:T(4,128)(2,1)S(1)}, u32[]{:S(2)}, u32[]{:S(2)}) async-start(bf16[16,4,4096]{2,1,0:T(4,128)(2,1)} %grid_blocks.3), calls=%async_computation.1 | async-start | bytes 1048576 | tf_op jit(solution)/shard_map/all_to_all | solution.py:259
  51.6 18.2 %copy-start = (bf16[512,512]{1,0:T(8,128)(2,1)S(1)}, bf16[512,512]{1,0:T(8,128)(2,1)}, u32[]{:S(2)}) copy-start(bf16[512,512]{1,0:T(8,128)(2,1)} %constant.9.clone.y_ref) | copy-start | bytes 1572868
  51.6 18.2 %copy-start.1 = (bf16[3,256,256]{2,1,0:T(8,128)(2,1)S(1)}, bf16[3,256,256]{2,1,0:T(8,128)(2,1)}, u32[]{:S(2)}) copy-start(bf16[3,256,256]{2,1,0:T(8,128)(2,1)} %constant.10.clone.z_ref) | copy-start | bytes 1179652
  69.8 39.9 %copy-start.2 = (bf16[8,16,2,512]{3,2,1,0:T(2,128)(2,1)S(1)}, bf16[8,16,2,512]{3,2,1,0:T(2,128)(2,1)}, u32[]{:S(2)}) copy-start(bf16[8,16,2,512]{3,2,1,0:T(2,128)(2,1)} %param.14) | copy-start | bytes 786436
  104.4 12.9 %all-to-all-start.3 = ((bf16[8,2,16,512]{3,2,1,0:T(8,128)(2,1)}), bf16[8,2,16,512]{3,2,1,0:T(8,128)(2,1)S(1)}, u32[]{:S(2)}, u32[]{:S(2)}) async-start(bf16[8,2,16,512]{3,2,1,0:T(8,128)(2,1)} %bitcast.6), calls=%async_computation.3 | async-start | bytes 524288 | tf_op jit(solution)/shard_map/all_to_all | solution.py:269

commit v5 on v4

--- a/solution.py
+++ b/solution.py
@@ -15,8 +15,8 @@
 XW = 16
 CELLS = 64
 SLABS = 16
-STEP = 1024
-TOGETHER = 4
+STEP = 2048
+TOGETHER = 8
 NT = (((1,), (1,)), ((), ()))
 
 
@@ -205,7 +205,7 @@
         in_specs=[pl.BlockSpec((TOGETHER, rows, blocks), lambda i: (i, 0, 0))],
         out_specs=pl.BlockSpec((2 * KY, Z), lambda i: (0, 0)),
         out_shape=jax.ShapeDtypeStruct((2 * KY, Z), jnp.float32),
-        compiler_params=pltpu.CompilerParams(vmem_limit_bytes=44 * 1024 * 1024),
+        compiler_params=pltpu.CompilerParams(vmem_limit_bytes=50 * 1024 * 1024),
         cost_estimate=place_cost(values),
         name="place_first",
     )(values)
@@ -225,7 +225,7 @@
         out_specs=pl.BlockSpec((Z, 2 * KY), lambda i: (0, 0)),
         out_shape=jax.ShapeDtypeStruct((Z, 2 * KY), jnp.bfloat16),
         scratch_shapes=[pltpu.VMEM((2 * KY, Z), jnp.float32)],
-        compiler_params=pltpu.CompilerParams(vmem_limit_bytes=44 * 1024 * 1024),
+        compiler_params=pltpu.CompilerParams(vmem_limit_bytes=50 * 1024 * 1024),
         cost_estimate=place_cost(values),
         name="place_last",
     )(values, start, y_table, z_tables)

time: 119 us -> 117 us (0.983)
  Pallas kernels: 74.4 us -> 72.4 us
where the time goes in v5:
time: 117 us; the launch traced here: 116 us
  Pallas kernels  72.4 us (62%)
  starting transfers between devices  19.7 us (17%)
  blocking collectives  15.6 us (13%)
  waiting for transfers between devices  7.48 us (6%)
    pallas_call x2, Pallas kernels, grid_blocks(): pl.pallas_call(grid_kernel, grid=(blocks // STEP,), in_specs=[pl.BlockSpe...  36.2 us
    pallas_call x1, Pallas kernels, place_last(): pl.pallas_call(place_last_kernel, grid=(sources // TOGETHER,), in_specs=[...  18.5 us
    pallas_call x1, Pallas kernels, place_first(): pl.pallas_call(place_first_kernel, grid=(sources // TOGETHER,), in_specs=...  17.7 us
    all_to_all x1, blocking collectives, per_device(): own = lax.all_to_all(whole, 'slab', split_axis=0, concat_axis=0, tiled=True)  15.6 us
    all_to_all x1, waiting for transfers between devices, per_device(): own = lax.all_to_all(own, 'coil', split_axis=0, concat_axis=0, tiled=True)  7.47 us
    all_to_all x1, starting transfers between devices, per_device(): lax.all_to_all(later, 'slab', split_axis=0, concat_axis=0, tiled=True)  7.22 us
    all_to_all x1, starting transfers between devices, per_device(): lax.all_to_all(sent[0], 'slab', split_axis=0, concat_axis=0, tiled=True)  7.12 us
    all_to_all x1, starting transfers between devices, per_device(): own = lax.all_to_all(own, 'coil', split_axis=0, concat_axis=0, tiled=True)  5.31 us
  transfers between devices with their start and end apart: 3, of which 1 were waited for; matrix products, arithmetic and copies ran while one was open for 0% of the time, Pallas kernels for 31%

profile of v5, /device:TPU:0, one launch (start us, length us, event | category | flops | bytes accessed | tf_op | source)
XLA Modules:
  0.0 116.1 jit_solution(13217882065481786750)
XLA Ops:
  0.0 18.1 %grid_blocks.2 = bf16[16,4,4096]{2,1,0:T(4,128)(2,1)} custom-call(bf16[64,8192]{1,0:T(8,128)(2,1)} %bitcast.12, s32[1,8192]{1,0:T(1,128)} %bitcast.14, s32[1,8192]{1,0:T(1,128)} %bitcast.16, s32[1,8192]{1,0:T(1,128)} %bitcast.18, bf16[8192,128]{1,0:T(8,128)(2,1)} %bitcast.10, bf16[128,256]{1,0:T(8,128)(2,1)} %constant.8.clone.table_ref), custom_call_target="tpu_custom_call" | custom-call | flops 1073741824 | bytes 2097152 | tf_op jit(solution)/shard_map/grid_blocks/pallas_call | solution.py:123
  18.1 7.1 %all-to-all-start = ((bf16[16,4,4096]{2,1,0:T(4,128)(2,1)}), bf16[16,4,4096]{2,1,0:T(4,128)(2,1)S(1)}, u32[]{:S(2)}, u32[]{:S(2)}) async-start(bf16[16,4,4096]{2,1,0:T(4,128)(2,1)} %grid_blocks.2), calls=%async_computation | async-start | bytes 1048576 | tf_op jit(solution)/shard_map/all_to_all | solution.py:257
  25.2 18.1 %grid_blocks.3 = bf16[16,4,4096]{2,1,0:T(4,128)(2,1)} custom-call(bf16[64,8192]{1,0:T(8,128)(2,1)} %bitcast.13, s32[1,8192]{1,0:T(1,128)} %bitcast.15, s32[1,8192]{1,0:T(1,128)} %bitcast.17, s32[1,8192]{1,0:T(1,128)} %bitcast.19, bf16[8192,128]{1,0:T(8,128)(2,1)} %bitcast.11, bf16[128,256]{1,0:T(8,128)(2,1)} %constant.8.clone.table_ref), custom_call_target="tpu_custom_call" | custom-call | flops 1073741824 | bytes 2097152 | tf_op jit(solution)/shard_map/grid_blocks/pallas_call | solution.py:123
  43.3 0.0 all-to-all-done.values_ref
  43.3 7.2 %all-to-all-start.1 = ((bf16[16,4,4096]{2,1,0:T(4,128)(2,1)}), bf16[16,4,4096]{2,1,0:T(4,128)(2,1)S(1)}, u32[]{:S(2)}, u32[]{:S(2)}) async-start(bf16[16,4,4096]{2,1,0:T(4,128)(2,1)} %grid_blocks.3), calls=%async_computation.1 | async-start | bytes 1048576 | tf_op jit(solution)/shard_map/all_to_all | solution.py:259
  50.5 0.0 copy-start
  50.5 0.0 copy-start.1
  50.5 17.7 %place_first.1.start_ref = f32[512,256]{1,0:T(8,128)S(1)} custom-call(bf16[16,4,4096]{2,1,0:T(4,128)(2,1)S(1)} %all-to-all-done.values_ref), custom_call_target="tpu_custom_call" | custom-call | flops 17179869184 | bytes 524288 | tf_op jit(solution)/shard_map/place_first/pallas_call | solution.py:202
  68.3 0.0 copy-start.2
  68.3 0.0 all-to-all-done.1.values_ref
  68.3 0.0 copy-done
  68.3 0.0 copy-done.1
  68.3 18.5 %place_last.1 = bf16[256,512]{1,0:T(8,128)(2,1)S(1)} custom-call(bf16[16,4,4096]{2,1,0:T(4,128)(2,1)S(1)} %all-to-all-done.1.values_ref, f32[512,256]{1,0:T(8,128)S(1)} %place_first.1.start_ref, bf16[512,512]{1,0:T(8,128)(2,1)S(1)} %copy-done, bf16[3,256,256]{2,1,0:T(8,128)(2,1)S(1)} %copy-done.1), custom_call_target="tpu_custom_call" | custom-call | flops 17179869184 | bytes 524288 | tf_op jit(solution)/shard_map/place_last/pallas_call | solution.py:216
  86.9 15.6 %all_to_all.20 = bf16[16,16,512]{2,1,0:T(8,128)(2,1)} all-to-all(bf16[16,16,512]{2,1,0:T(8,128)(2,1)S(1)} %bitcast.9), channel_id=1, replica_groups=mesh['slab'=16,'coil'=8] {'slab'}, dimensions={0} | all-to-all | bytes 524288 | tf_op jit(solution)/shard_map/all_to_all | solution.py:267
  102.4 5.3 %all-to-all-start.3 = ((bf16[8,2,16,512]{3,2,1,0:T(8,128)(2,1)}), bf16[8,2,16,512]{3,2,1,0:T(8,128)(2,1)S(1)}, u32[]{:S(2)}, u32[]{:S(2)}) async-start(bf16[8,2,16,512]{3,2,1,0:T(8,128)(2,1)} %bitcast.6), calls=%async_computation.3 | async-start | bytes 524288 | tf_op jit(solution)/shard_map/all_to_all | solution.py:269
  107.8 0.0 copy-done.2
  107.8 0.1 copy_convert_fusion
  107.8 7.5 %all-to-all-done.3 = bf16[8,2,16,512]{3,2,1,0:T(8,128)(2,1)S(1)} async-done(((bf16[8,2,16,512]{3,2,1,0:T(8,128)(2,1)}), bf16[8,2,16,512]{3,2,1,0:T(8,128)(2,1)S(1)}, u32[]{:S(2)}, u32[]{:S(2)}) %all-to-all-start.3) | async-done | bytes 262176 | tf_op jit(solution)/shard_map/all_to_all | solution.py:269
  115.4 0.1 add_reduce_fusion
  115.5 0.7 copy.12
  (2 shorter events, 0.1 us)
Async XLA Ops:
  18.1 25.2 %all-to-all-start = ((bf16[16,4,4096]{2,1,0:T(4,128)(2,1)}), bf16[16,4,4096]{2,1,0:T(4,128)(2,1)S(1)}, u32[]{:S(2)}, u32[]{:S(2)}) async-start(bf16[16,4,4096]{2,1,0:T(4,128)(2,1)} %grid_blocks.2), calls=%async_computation | async-start | bytes 1048576 | tf_op jit(solution)/shard_map/all_to_all | solution.py:257
  43.3 25.0 %all-to-all-start.1 = ((bf16[16,4,4096]{2,1,0:T(4,128)(2,1)}), bf16[16,4,4096]{2,1,0:T(4,128)(2,1)S(1)}, u32[]{:S(2)}, u32[]{:S(2)}) async-start(bf16[16,4,4096]{2,1,0:T(4,128)(2,1)} %grid_blocks.3), calls=%async_computation.1 | async-start | bytes 1048576 | tf_op jit(solution)/shard_map/all_to_all | solution.py:259
  50.5 17.8 %copy-start = (bf16[512,512]{1,0:T(8,128)(2,1)S(1)}, bf16[512,512]{1,0:T(8,128)(2,1)}, u32[]{:S(2)}) copy-start(bf16[512,512]{1,0:T(8,128)(2,1)} %constant.9.clone.y_ref) | copy-start | bytes 1572868
  50.5 17.8 %copy-start.1 = (bf16[3,256,256]{2,1,0:T(8,128)(2,1)S(1)}, bf16[3,256,256]{2,1,0:T(8,128)(2,1)}, u32[]{:S(2)}) copy-start(bf16[3,256,256]{2,1,0:T(8,128)(2,1)} %constant.10.clone.z_ref) | copy-start | bytes 1179652
  68.3 39.5 %copy-start.2 = (bf16[8,16,2,512]{3,2,1,0:T(2,128)(2,1)S(1)}, bf16[8,16,2,512]{3,2,1,0:T(2,128)(2,1)}, u32[]{:S(2)}) copy-start(bf16[8,16,2,512]{3,2,1,0:T(2,128)(2,1)} %param.14) | copy-start | bytes 786436
  102.4 12.9 %all-to-all-start.3 = ((bf16[8,2,16,512]{3,2,1,0:T(8,128)(2,1)}), bf16[8,2,16,512]{3,2,1,0:T(8,128)(2,1)S(1)}, u32[]{:S(2)}, u32[]{:S(2)}) async-start(bf16[8,2,16,512]{3,2,1,0:T(8,128)(2,1)} %bitcast.6), calls=%async_computation.3 | async-start | bytes 524288 | tf_op jit(solution)/shard_map/all_to_all | solution.py:269

commit v6 on v5

--- a/solution.py
+++ b/solution.py
@@ -265,11 +265,13 @@
     )
     whole = whole.reshape(slabs, planes, 2 * KY)
     own = lax.all_to_all(whole, "slab", split_axis=0, concat_axis=0, tiled=True)
+    whole, half_maps = lax.optimization_barrier((whole, sensitivity[..., :KY]))
+    map_re = half_maps.astype(jnp.float32)
+    own, map_re, half_maps = lax.optimization_barrier((own, map_re, sensitivity[..., KY:]))
     own = own.reshape(groups, width, planes, 2 * KY)
     own = lax.all_to_all(own, "coil", split_axis=0, concat_axis=0, tiled=True)
+    own, map_im = lax.optimization_barrier((own, half_maps.astype(jnp.float32)))
     own = jnp.swapaxes(own.reshape(coils, width, planes, 2 * KY), 1, 2).astype(jnp.float32)
-    maps = sensitivity.astype(jnp.float32)
-    map_re, map_im = maps[..., :KY], maps[..., KY:]
     img_re, img_im = own[..., :KY], own[..., KY:]
     real_part = jnp.sum(map_re * img_re + map_im * img_im, axis=0)
     imag_part = jnp.sum(map_re * img_im - map_im * img_re, axis=0)

time: 117 us -> 118 us (level)
  blocking collectives: 15.6 us -> 0 us
  waiting for transfers between devices: 7.48 us -> 15.7 us
  starting transfers between devices: 19.7 us -> 26.9 us
    all_to_all x1 -> x0, blocking collectives: 15.6 us -> none  [per_device(): own = lax.all_to_all(whole, 'slab', split_axis=0, concat_axis=0, tiled=True)]
    all_to_all x0 -> x1, waiting for transfers between devices: none -> 8.19 us  [per_device(): own = lax.all_to_all(whole, 'slab', split_axis=0, concat_axis=0, tiled=True)]
    all_to_all x0 -> x1, starting transfers between devices: none -> 7.27 us  [per_device(): own = lax.all_to_all(whole, 'slab', split_axis=0, concat_axis=0, tiled=True)]
  transfers between devices with their start and end apart: 3 -> 4, of which waited for: 1 -> 2; matrix products, arithmetic and copies ran while one was open for 0% -> 0% of each run, Pallas kernels for 31% -> 31%
where the time goes in v6:
time: 118 us; the launch traced here: 117 us
  Pallas kernels  73.1 us (62%)
  starting transfers between devices  26.9 us (23%)
  waiting for transfers between devices  15.7 us (13%)
    pallas_call x2, Pallas kernels, grid_blocks(): pl.pallas_call(grid_kernel, grid=(blocks // STEP,), in_specs=[pl.BlockSpe...  36.1 us
    pallas_call x1, Pallas kernels, place_last(): pl.pallas_call(place_last_kernel, grid=(sources // TOGETHER,), in_specs=[...  19.2 us
    pallas_call x1, Pallas kernels, place_first(): pl.pallas_call(place_first_kernel, grid=(sources // TOGETHER,), in_specs=...  17.7 us
    all_to_all x1, waiting for transfers between devices, per_device(): own = lax.all_to_all(whole, 'slab', split_axis=0, concat_axis=0, tiled=True)  8.19 us
    all_to_all x1, waiting for transfers between devices, per_device(): own = lax.all_to_all(own, 'coil', split_axis=0, concat_axis=0, tiled=True)  7.51 us
    all_to_all x1, starting transfers between devices, per_device(): own = lax.all_to_all(whole, 'slab', split_axis=0, concat_axis=0, tiled=True)  7.27 us
    all_to_all x1, starting transfers between devices, per_device(): lax.all_to_all(later, 'slab', split_axis=0, concat_axis=0, tiled=True)  7.21 us
    all_to_all x1, starting transfers between devices, per_device(): lax.all_to_all(sent[0], 'slab', split_axis=0, concat_axis=0, tiled=True)  7.12 us
  transfers between devices with their start and end apart: 4, of which 2 were waited for; matrix products, arithmetic and copies ran while one was open for 0% of the time, Pallas kernels for 31%

profile of v6, /device:TPU:0, one launch (start us, length us, event | category | flops | bytes accessed | tf_op | source)
XLA Modules:
  0.0 117.0 jit_solution(689984334748293473)
XLA Ops:
  0.0 18.0 %grid_blocks.2 = bf16[16,4,4096]{2,1,0:T(4,128)(2,1)} custom-call(bf16[64,8192]{1,0:T(8,128)(2,1)} %bitcast.11, s32[1,8192]{1,0:T(1,128)} %bitcast.13, s32[1,8192]{1,0:T(1,128)} %bitcast.15, s32[1,8192]{1,0:T(1,128)} %bitcast.17, bf16[8192,128]{1,0:T(8,128)(2,1)} %bitcast.9, bf16[128,256]{1,0:T(8,128)(2,1)} %constant.8.clone.table_ref), custom_call_target="tpu_custom_call" | custom-call | flops 1073741824 | bytes 2097152 | tf_op jit(solution)/shard_map/grid_blocks/pallas_call | solution.py:123
  18.0 7.1 %all-to-all-start = ((bf16[16,4,4096]{2,1,0:T(4,128)(2,1)}), bf16[16,4,4096]{2,1,0:T(4,128)(2,1)S(1)}, u32[]{:S(2)}, u32[]{:S(2)}) async-start(bf16[16,4,4096]{2,1,0:T(4,128)(2,1)} %grid_blocks.2), calls=%async_computation | async-start | bytes 1048576 | tf_op jit(solution)/shard_map/all_to_all | solution.py:257
  25.2 18.1 %grid_blocks.3 = bf16[16,4,4096]{2,1,0:T(4,128)(2,1)} custom-call(bf16[64,8192]{1,0:T(8,128)(2,1)} %bitcast.12, s32[1,8192]{1,0:T(1,128)} %bitcast.14, s32[1,8192]{1,0:T(1,128)} %bitcast.16, s32[1,8192]{1,0:T(1,128)} %bitcast.18, bf16[8192,128]{1,0:T(8,128)(2,1)} %bitcast.10, bf16[128,256]{1,0:T(8,128)(2,1)} %constant.8.clone.table_ref), custom_call_target="tpu_custom_call" | custom-call | flops 1073741824 | bytes 2097152 | tf_op jit(solution)/shard_map/grid_blocks/pallas_call | solution.py:123
  43.3 0.0 all-to-all-done.values_ref
  43.3 7.2 %all-to-all-start.1 = ((bf16[16,4,4096]{2,1,0:T(4,128)(2,1)}), bf16[16,4,4096]{2,1,0:T(4,128)(2,1)S(1)}, u32[]{:S(2)}, u32[]{:S(2)}) async-start(bf16[16,4,4096]{2,1,0:T(4,128)(2,1)} %grid_blocks.3), calls=%async_computation.1 | async-start | bytes 1048576 | tf_op jit(solution)/shard_map/all_to_all | solution.py:259
  50.5 0.0 copy-start
  50.5 0.0 copy-start.1
  50.5 17.7 %place_first.1.start_ref = f32[512,256]{1,0:T(8,128)S(1)} custom-call(bf16[16,4,4096]{2,1,0:T(4,128)(2,1)S(1)} %all-to-all-done.values_ref), custom_call_target="tpu_custom_call" | custom-call | flops 17179869184 | bytes 524288 | tf_op jit(solution)/shard_map/place_first/pallas_call | solution.py:202
  68.3 0.0 copy-start.2
  68.3 0.0 all-to-all-done.1.values_ref
  68.3 0.0 copy-done
  68.3 0.0 copy-done.1
  68.3 19.2 %place_last.1 = bf16[256,512]{1,0:T(8,128)(2,1)} custom-call(bf16[16,4,4096]{2,1,0:T(4,128)(2,1)S(1)} %all-to-all-done.1.values_ref, f32[512,256]{1,0:T(8,128)S(1)} %place_first.1.start_ref, bf16[512,512]{1,0:T(8,128)(2,1)S(1)} %copy-done, bf16[3,256,256]{2,1,0:T(8,128)(2,1)S(1)} %copy-done.1), custom_call_target="tpu_custom_call" | custom-call | flops 17179869184 | bytes 524288 | tf_op jit(solution)/shard_map/place_last/pallas_call | solution.py:216
  87.5 7.3 %all-to-all-start.2 = ((bf16[16,16,512]{2,1,0:T(8,128)(2,1)}), bf16[16,16,512]{2,1,0:T(8,128)(2,1)}, u32[]{:S(2)}, u32[]{:S(2)}) async-start(bf16[16,16,512]{2,1,0:T(8,128)(2,1)} %bitcast.5), calls=%async_computation.2 | async-start | bytes 524288 | tf_op jit(solution)/shard_map/all_to_all | solution.py:267
  94.8 0.0 copy-done.2
  94.8 0.2 fusion
  95.1 8.2 %all-to-all-done.2 = bf16[16,16,512]{2,1,0:T(8,128)(2,1)} async-done(((bf16[16,16,512]{2,1,0:T(8,128)(2,1)}), bf16[16,16,512]{2,1,0:T(8,128)(2,1)}, u32[]{:S(2)}, u32[]{:S(2)}) %all-to-all-start.2) | async-done | bytes 262176 | tf_op jit(solution)/shard_map/all_to_all | solution.py:267
  103.3 5.3 %all-to-all-start.3 = ((bf16[8,2,16,512]{3,2,1,0:T(8,128)(2,1)}), bf16[8,2,16,512]{3,2,1,0:T(8,128)(2,1)S(1)}, u32[]{:S(2)}, u32[]{:S(2)}) async-start(bf16[8,2,16,512]{3,2,1,0:T(8,128)(2,1)} %bitcast.6), calls=%async_computation.3 | async-start | bytes 524288 | tf_op jit(solution)/shard_map/all_to_all | solution.py:272
  108.7 7.5 %all-to-all-done.3 = bf16[8,2,16,512]{3,2,1,0:T(8,128)(2,1)S(1)} async-done(((bf16[8,2,16,512]{3,2,1,0:T(8,128)(2,1)}), bf16[8,2,16,512]{3,2,1,0:T(8,128)(2,1)S(1)}, u32[]{:S(2)}, u32[]{:S(2)}) %all-to-all-start.3) | async-done | bytes 262176 | tf_op jit(solution)/shard_map/all_to_all | solution.py:272
  116.2 0.1 add_reduce_fusion
  116.4 0.7 copy.14
  (6 shorter events, 0.1 us)
Async XLA Ops:
  18.0 25.2 %all-to-all-start = ((bf16[16,4,4096]{2,1,0:T(4,128)(2,1)}), bf16[16,4,4096]{2,1,0:T(4,128)(2,1)S(1)}, u32[]{:S(2)}, u32[]{:S(2)}) async-start(bf16[16,4,4096]{2,1,0:T(4,128)(2,1)} %grid_blocks.2), calls=%async_computation | async-start | bytes 1048576 | tf_op jit(solution)/shard_map/all_to_all | solution.py:257
  43.3 25.0 %all-to-all-start.1 = ((bf16[16,4,4096]{2,1,0:T(4,128)(2,1)}), bf16[16,4,4096]{2,1,0:T(4,128)(2,1)S(1)}, u32[]{:S(2)}, u32[]{:S(2)}) async-start(bf16[16,4,4096]{2,1,0:T(4,128)(2,1)} %grid_blocks.3), calls=%async_computation.1 | async-start | bytes 1048576 | tf_op jit(solution)/shard_map/all_to_all | solution.py:259
  50.5 17.8 %copy-start = (bf16[512,512]{1,0:T(8,128)(2,1)S(1)}, bf16[512,512]{1,0:T(8,128)(2,1)}, u32[]{:S(2)}) copy-start(bf16[512,512]{1,0:T(8,128)(2,1)} %constant.9.clone.y_ref) | copy-start | bytes 1572868
  50.5 17.8 %copy-start.1 = (bf16[3,256,256]{2,1,0:T(8,128)(2,1)S(1)}, bf16[3,256,256]{2,1,0:T(8,128)(2,1)}, u32[]{:S(2)}) copy-start(bf16[3,256,256]{2,1,0:T(8,128)(2,1)} %constant.10.clone.z_ref) | copy-start | bytes 1179652
  68.3 26.5 %copy-start.2 = (bf16[8,16,2,512]{3,2,1,0:T(2,128)(2,1)S(1)}, bf16[8,16,2,512]{3,2,1,0:T(2,128)(2,1)}, u32[]{:S(2)}) copy-start(bf16[8,16,2,512]{3,2,1,0:T(2,128)(2,1)} %param.14) | copy-start | bytes 786436
  87.5 15.8 %all-to-all-start.2 = ((bf16[16,16,512]{2,1,0:T(8,128)(2,1)}), bf16[16,16,512]{2,1,0:T(8,128)(2,1)}, u32[]{:S(2)}, u32[]{:S(2)}) async-start(bf16[16,16,512]{2,1,0:T(8,128)(2,1)} %bitcast.5), calls=%async_computation.2 | async-start | bytes 524288 | tf_op jit(solution)/shard_map/all_to_all | solution.py:267
  103.3 12.9 %all-to-all-start.3 = ((bf16[8,2,16,512]{3,2,1,0:T(8,128)(2,1)}), bf16[8,2,16,512]{3,2,1,0:T(8,128)(2,1)S(1)}, u32[]{:S(2)}, u32[]{:S(2)}) async-start(bf16[8,2,16,512]{3,2,1,0:T(8,128)(2,1)} %bitcast.6), calls=%async_computation.3 | async-start | bytes 524288 | tf_op jit(solution)/shard_map/all_to_all | solution.py:272

commit v7 on v2

v7 whole, which is shorter than its diff:
```python
import functools
import math

import jax
import jax.numpy as jnp
import numpy as np
from jax import lax
from jax.experimental import pallas as pl
from jax.experimental.pallas import tpu as pltpu
from jax.sharding import PartitionSpec as P

KX = 256
KY = 256
Z = 256
XW = 16
CELLS = 64
SLABS = 16
STEP = 2048
NT = (((1,), (1,)), ((), ()))


def twiddle(first, second, length):
    phase = (first * second % length).astype(np.float32) * np.float32(2.0 * math.pi / length)
    scale = 1.0 / math.sqrt(length)
    return np.cos(phase) * scale, np.sin(phase) * scale


def across_table():
    cell = np.arange(CELLS)
    rows = (KX - XW) // 2 + np.arange(XW)
    table = np.zeros((KX // CELLS, 2, CELLS, 2, XW), np.float32)
    for s in range(KX // CELLS):
        cosine, sine = twiddle((s * CELLS + cell)[:, None], rows[None, :], KX)
        table[s, 0, :, 0] = cosine
        table[s, 0, :, 1] = sine
        table[s, 1, :, 0] = -sine
        table[s, 1, :, 1] = cosine
    return table.reshape(2 * KX, 2 * XW)


def line_table(length):
    index = np.arange(length)
    cosine, sine = twiddle(index[:, None], index[None, :], length)
    return np.block([[cosine, -sine], [sine, cosine]])


def depth_tables(length):
    index = np.arange(length)
    cosine, sine = twiddle(index[:, None], index[None, :], length)
    return np.stack([cosine, sine, -sine])


def grid_kernel(pos_ref, count_ref, samples_ref, out_ref, pos_s):
    tiles = STEP // 32
    sample = lax.broadcasted_iota(jnp.int32, (CELLS, STEP), 0)
    live = sample < count_ref[...]
    pos = jnp.where(live, pos_ref[...].astype(jnp.float32) * 0.4, -100.0)
    pos_s[:, 0:CELLS] = pos.T
    mids = (lax.broadcasted_iota(jnp.int32, (CELLS, 256), 0).astype(jnp.float32) + 0.5) * 0.4
    low = lax.broadcasted_iota(jnp.int32, (8, 128), 1) < 64
    sub = lax.broadcasted_iota(jnp.int32, (32, 128), 0) % 8
    lane_half = lax.broadcasted_iota(jnp.int32, (32, 128), 1) // 64
    keep = lane_half == sub % 2
    group = sub // 2

    def one_tile(t, carry):
        start = pl.multiple_of(t * 32, 32)
        pos_rows = pos_s[pl.ds(start, 32), :]
        halves = []
        for h in range(2):
            even = pos_rows[16 * h : 16 * h + 8]
            odd = pltpu.roll(pos_rows[16 * h + 8 : 16 * h + 16], 64, 1)
            halves.append(jnp.where(low, even, odd))
        row4 = jnp.concatenate(halves, axis=1)
        parts = []
        for nb in range(8):
            offset = row4[nb : nb + 1, :] - mids
            bump = jnp.maximum(1.0 - offset * offset, 0.0)
            parts.append((bump * bump).astype(jnp.bfloat16))
        weights = jnp.concatenate(parts, axis=0)
        vals = samples_ref[pl.ds(start, 32), :].astype(jnp.float32)
        zero = jnp.zeros((8, 128), jnp.float32)
        lhs = []
        for p in range(2):
            for kb in range(4):
                piece = vals[8 * kb : 8 * kb + 8]
                if kb % 2 != p:
                    piece = pltpu.roll(piece, 64, 1)
                piece = jnp.where(low == (kb % 2 == 0), piece, 0.0)
                lhs.append(jnp.concatenate([piece, zero] if kb < 2 else [zero, piece], axis=1))
        lhs = jnp.concatenate(lhs, axis=0).astype(jnp.bfloat16)
        full = lax.dot_general(lhs, weights, NT, preferred_element_type=jnp.float32)
        sides = []
        for p in range(2):
            block = full[32 * p : 32 * p + 32]
            own = jnp.where(group == 0, block[:, 0:128], block[:, 128:256])
            own = jnp.where(group == 2, block[:, 256:384], own)
            own = jnp.where(group == 3, block[:, 384:512], own)
            own = jnp.where(keep, own, 0.0)
            sides.append(own + pltpu.roll(own, 64, 1))
        out_ref[pl.ds(start, 32), :] = jnp.where(lane_half == 0, sides[0], sides[1]).astype(jnp.bfloat16)
        return carry

    lax.fori_loop(0, tiles, one_tile, 0, unroll=True)


def grid_blocks(pos_t, count, samples):
    blocks = samples.shape[0]
    return pl.pallas_call(
        grid_kernel,
        grid=(blocks // STEP,),
        in_specs=[
            pl.BlockSpec((CELLS, STEP), lambda i: (0, i)),
            pl.BlockSpec((1, STEP), lambda i: (0, i)),
            pl.BlockSpec((STEP, 128), lambda i: (i, 0)),
        ],
        out_specs=pl.BlockSpec((STEP, 128), lambda i: (i, 0)),
        out_shape=jax.ShapeDtypeStruct((blocks, 128), jnp.bfloat16),
        scratch_shapes=[pltpu.VMEM((STEP, 128), jnp.float32)],
        compiler_params=pltpu.CompilerParams(vmem_limit_bytes=60 * 1024 * 1024),
        name="grid_blocks",
    )(pos_t, count, samples)


def add_kernel(rows_ref, values_ref, out_ref, acc):
    step = pl.program_id(0)
    length = values_ref.shape[0]

    @pl.when(step == 0)
    def _():
        acc[...] = jnp.zeros_like(acc)

    def some(i, carry):
        start = pl.multiple_of(i * 16, 16)
        values = values_ref[pl.ds(start, 16), :].astype(jnp.float32)
        for q in range(16):
            row = rows_ref[step * length + start + q]
            acc[pl.ds(row, 1), :] += values[q : q + 1]
        return carry

    lax.fori_loop(0, length // 16, some, 0, unroll=2)

    @pl.when(step == pl.num_programs(0) - 1)
    def _():
        out_ref[...] = acc[...].astype(jnp.bfloat16)


def add_rows(rows, values, total):
    slots = values.shape[0]
    return pl.pallas_call(
        add_kernel,
        grid_spec=pltpu.PrefetchScalarGridSpec(
            num_scalar_prefetch=1,
            grid=(slots // STEP,),
            in_specs=[pl.BlockSpec((STEP, 128), lambda i, rows: (i, 0))],
            out_specs=pl.BlockSpec((total, 128), lambda i, rows: (0, 0)),
            scratch_shapes=[pltpu.VMEM((total, 128), jnp.float32)],
        ),
        out_shape=jax.ShapeDtypeStruct((total, 128), jnp.bfloat16),
        compiler_params=pltpu.CompilerParams(vmem_limit_bytes=48 * 1024 * 1024),
        name="add_rows",
    )(rows, values)


def slots_of(slab, slabs, capacity):
    hot = slab[:, None] == jnp.arange(slabs, dtype=jnp.int32)[None, :]
    chunks = hot.reshape(-1, 128, slabs).astype(jnp.float32)
    inner = jnp.asarray(np.tril(np.ones((128, 128)), -1), jnp.float32)
    outer = jnp.asarray(np.tril(np.ones((chunks.shape[0], chunks.shape[0])), -1), jnp.float32)
    exact = lax.Precision.HIGHEST
    before = jnp.einsum("ij,cjs->cis", inner, chunks, precision=exact)
    before += jnp.einsum("cd,ds->cs", outer, jnp.sum(chunks, axis=1), precision=exact)[:, None]
    rank = jnp.sum(before * chunks, axis=2).reshape(-1)
    return slab * capacity + (rank + 0.5).astype(jnp.int32)


def per_device(samples, sample_pos, block_count, grid_block, block_slab, sensitivity):
    slabs = lax.axis_size("slab")
    groups = lax.axis_size("coil")
    blocks = samples.shape[1]
    planes = sensitivity.shape[1]
    coils = sensitivity.shape[0]
    width = sensitivity.shape[2]
    capacity = 5 * blocks // (2 * slabs)
    slot = slots_of(block_slab[:, 0], slabs, capacity)
    target = jnp.zeros((slabs * capacity,), jnp.int32).at[slot].set(grid_block)
    target = target.reshape(slabs, capacity // 128, 128)
    target = lax.all_to_all(target, "slab", split_axis=0, concat_axis=0, tiled=True)
    gridded = grid_blocks(sample_pos.T, block_count[None], samples[0])
    packed = jnp.zeros((slabs * capacity, 128), jnp.bfloat16).at[slot].set(gridded)
    packed = packed.reshape(slabs, capacity, 128)
    packed = lax.all_to_all(packed, "slab", split_axis=0, concat_axis=0, tiled=True)
    kspace = add_rows(target.reshape(-1), packed.reshape(-1, 128), planes * KY * KX // CELLS)
    x_rows = jnp.dot(
        kspace.reshape(planes * KY, 2 * KX),
        jnp.asarray(across_table(), jnp.bfloat16),
        preferred_element_type=jnp.float32,
    ).astype(jnp.bfloat16)
    y_planes = jnp.einsum(
        "zkqx,qkn->zxn",
        x_rows.reshape(planes, KY, 2, XW),
        jnp.asarray(line_table(KY).T.reshape(2, KY, 2 * KY), jnp.bfloat16),
        preferred_element_type=jnp.float32,
    ).astype(jnp.bfloat16)
    lines = lax.all_to_all(y_planes, "slab", split_axis=1, concat_axis=0, tiled=True)
    lines = lines.reshape(Z, 2, KY)
    turns = jnp.asarray(depth_tables(Z), jnp.bfloat16)
    turns = jnp.stack([jnp.stack([turns[0], turns[2]]), jnp.stack([turns[1], turns[0]])])
    whole = jnp.einsum("pqzk,kqy->zpy", turns, lines, preferred_element_type=jnp.float32)
    whole = whole.astype(jnp.bfloat16).reshape(slabs, planes, 2 * KY)
    own = lax.all_to_all(whole, "slab", split_axis=0, concat_axis=0, tiled=True)
    whole, half_maps = lax.optimization_barrier((whole, sensitivity[..., :KY]))
    map_re = half_maps.astype(jnp.float32)
    own, map_re, half_maps = lax.optimization_barrier((own, map_re, sensitivity[..., KY:]))
    own = own.reshape(groups, width, planes, 2 * KY)
    own = lax.all_to_all(own, "coil", split_axis=0, concat_axis=0, tiled=True)
    own, map_im = lax.optimization_barrier((own, half_maps.astype(jnp.float32)))
    own = jnp.swapaxes(own.reshape(coils, width, planes, 2 * KY), 1, 2).astype(jnp.float32)
    img_re, img_im = own[..., :KY], own[..., KY:]
    real_part = jnp.sum(map_re * img_re + map_im * img_im, axis=0)
    imag_part = jnp.sum(map_re * img_im - map_im * img_re, axis=0)
    return jnp.concatenate([real_part, imag_part], axis=-1)


def solution(mesh):
    return jax.shard_map(
        per_device,
        mesh=mesh,
        in_specs=(
            P("coil", "slab", None),
            P("slab", None),
            P("slab"),
            P("slab"),
            P("slab", None),
            P(None, "slab", "coil", None),
        ),
        out_specs=P("slab", "coil", None),
        check_vma=False,
    )
```

time: 142 us -> 371 us (2.61)
  waiting for transfers between devices: 8.38 us -> 96 us
  Pallas kernels: 73 us -> 153 us
  local copies, waits for them, and re-layouts: 6.79 us -> 67.8 us
  starting transfers between devices: 3.53 us -> 23.8 us
  blocking collectives: 33.8 us -> 19.5 us
  between operations: 13.5 us -> 0.25 us
  matrix products: 0 us -> 6.41 us
    all_to_all x0 -> x3, waiting for transfers between devices: none -> 87.8 us  [the longest x1 80.2 us: per_device(): lax.all_to_all(packed, 'slab', split_axis=0, concat_axis=0, tiled=True)]
    pallas_call x1, Pallas kernels: 39.7 us -> 120 us  [add_rows(): pl.pallas_call(add_kernel, grid_spec=pltpu.PrefetchScalarGridSpec(num_sca...]
    scatter x0 -> x2, local copies, waits for them, and re-layouts: none -> 55.2 us  [the longest x1 30.7 us: per_device(): target = jnp.zeros((slabs * capacity,), jnp.int32).at[slot].set(grid_block)]
    all_to_all x0 -> x3, starting transfers between devices: none -> 19.6 us  [the longest x1 7.27 us: per_device(): lax.all_to_all(packed, 'slab', split_axis=0, concat_axis=0, tiled=True)]
    all_to_all x2 -> x1, blocking collectives: 33.8 us -> 19.5 us  [per_device(): lax.all_to_all(y_planes, 'slab', split_axis=1, concat_axis=0, tiled=True)]
    reshape x2 -> x6, local copies, waits for them, and re-layouts: 0.46 us -> 9.34 us  [the longest x1 7.57 us: per_device(): kspace.reshape(planes * KY, 2 * KX)]
    dot_general x0 -> x5, matrix products: none -> 6.41 us  [the longest x1 3.57 us: per_device(): jnp.dot(kspace.reshape(planes * KY, 2 * KX), jnp.asarray(across_table(),...]
  transfers between devices with their start and end apart: 2 -> 4, of which waited for: 1 -> 3; matrix products, arithmetic and copies ran while one was open for 0% -> 7% of each run, Pallas kernels for 24% -> 9%
where the time goes in v7:
time: 371 us; the launch traced here: 369 us
  Pallas kernels  153 us (41%)
  waiting for transfers between devices  96 us (26%)
  local copies, waits for them, and re-layouts  67.8 us (18%)
  starting transfers between devices  23.8 us (6%)
  blocking collectives  19.5 us (5%)
  matrix products  6.41 us (2%)
    pallas_call x1, Pallas kernels, add_rows(): pl.pallas_call(add_kernel, grid_spec=pltpu.PrefetchScalarGridSpec(num_sca...  120 us
    all_to_all x1, waiting for transfers between devices, per_device(): lax.all_to_all(packed, 'slab', split_axis=0, concat_axis=0, tiled=True)  80.2 us
    pallas_call x1, Pallas kernels, grid_blocks(): pl.pallas_call(grid_kernel, grid=(blocks // STEP,), in_specs=[pl.BlockSpe...  33.9 us
    scatter x1, local copies, waits for them, and re-layouts, per_device(): target = jnp.zeros((slabs * capacity,), jnp.int32).at[slot].set(grid_block)  30.7 us
    scatter x1, local copies, waits for them, and re-layouts, per_device(): jnp.zeros((slabs * capacity, 128), jnp.bfloat16).at[slot].set(gridded)  24.6 us
    all_to_all x1, blocking collectives, per_device(): lax.all_to_all(y_planes, 'slab', split_axis=1, concat_axis=0, tiled=True)  19.5 us
    all_to_all x1, waiting for transfers between devices, per_device(): own = lax.all_to_all(whole, 'slab', split_axis=0, concat_axis=0, tiled=True)  8.21 us
    reshape x1, local copies, waits for them, and re-layouts, per_device(): kspace.reshape(planes * KY, 2 * KX)  7.57 us
  transfers between devices with their start and end apart: 4, of which 3 were waited for; matrix products, arithmetic and copies ran while one was open for 7% of the time, Pallas kernels for 9%

profile of v7, /device:TPU:0, one launch (start us, length us, event | category | flops | bytes accessed | tf_op | source)
XLA Modules:
  0.0 369.2 jit_solution(17291752614802677458)
XLA Ops:
  0.0 1.0 convert_reduce_fusion
  1.0 0.9 fusion.14
  1.9 1.3 fusion.6
  3.2 0.8 compare_select_fusion
  4.0 30.7 %scatter_custom_fusion = s32[20480]{0:T(1024)S(1)} fusion(s32[8192]{0:T(1024)S(1)} %bitcast.65, s32[8192]{0:T(1024)} %param.14, s32[]{:T(128)} %constant.11.clone.1), kind=kCustom, calls=%fused_computation.24 | custom fusion | bytes 82432 | tf_op jit(solution)/shard_map/scatter | solution.py:186
  34.7 0.7 reshape.55
  35.4 7.1 %all-to-all-start = ((s32[16,10,128]{2,1,0:T(8,128)}), s32[16,10,128]{2,1,0:T(8,128)S(1)}, u32[]{:S(2)}, u32[]{:S(2)}) async-start(s32[16,10,128]{2,1,0:T(8,128)} %reshape.55), calls=%async_computation | async-start | bytes 262144 | tf_op jit(solution)/shard_map/all_to_all | solution.py:188
  42.5 33.9 %grid_blocks.1 = bf16[8192,128]{1,0:T(8,128)(2,1)} custom-call(bf16[64,8192]{1,0:T(8,128)(2,1)} %bitcast.57, s32[1,8192]{1,0:T(1,128)} %bitcast.64, bf16[8192,128]{1,0:T(8,128)(2,1)} %bitcast.56), custom_call_target="tpu_custom_call" | custom-call | tf_op jit(solution)/shard_map/grid_blocks/pallas_call | solution.py:109
  76.4 24.6 %scatter_custom_fusion.1 = bf16[20480,128]{1,0:T(8,128)(2,1)} fusion(s32[8192]{0:T(1024)S(1)} %bitcast.66, bf16[8192,128]{1,0:T(8,128)(2,1)} %grid_blocks.1, bf16[]{:T(256)} %constant.10.clone.1), kind=kCustom, calls=%fused_computation.3 | custom fusion | bytes 5243392 | tf_op jit(solution)/shard_map/scatter | solution.py:190
  101.0 0.0 all-to-all-done
  101.0 7.3 %all-to-all-start.1 = ((bf16[16,1280,128]{2,1,0:T(8,128)(2,1)}), bf16[16,1280,128]{2,1,0:T(8,128)(2,1)}, u32[]{:S(2)}, u32[]{:S(2)}) async-start(bf16[16,1280,128]{2,1,0:T(8,128)(2,1)} %bitcast.55), calls=%async_computation.1 | async-start | bytes 10485760 | tf_op jit(solution)/shard_map/all_to_all | solution.py:192
  108.3 80.2 %all-to-all-done.1 = bf16[16,1280,128]{2,1,0:T(8,128)(2,1)} async-done(((bf16[16,1280,128]{2,1,0:T(8,128)(2,1)}), bf16[16,1280,128]{2,1,0:T(8,128)(2,1)}, u32[]{:S(2)}, u32[]{:S(2)}) %all-to-all-start.1) | async-done | bytes 5242912 | tf_op jit(solution)/shard_map/all_to_all | solution.py:192
  188.5 119.5 %add_rows.1 = bf16[16384,128]{1,0:T(8,128)(2,1)S(1)} custom-call(s32[20480]{0:T(1024)S(1)} %reshape.56.rows_ref, bf16[20480,128]{1,0:T(8,128)(2,1)} %bitcast.9.values_ref), custom_call_target="tpu_custom_call" | custom-call | tf_op jit(solution)/shard_map/add_rows/pallas_call | solution.py:150
  308.1 0.0 copy-start
  308.1 1.9 copy-done
  310.0 0.0 copy-start.4
  310.0 7.6 %reshape.59 = bf16[4096,512]{1,0:T(8,128)(2,1)} reshape(bf16[16384,128]{1,0:T(8,128)(2,1)} %copy-done) | data formatting | bytes 8388608 | tf_op jit(solution)/shard_map/reshape | solution.py:195
  317.6 0.0 copy-done.4
  317.6 0.0 copy-start.2
  317.6 0.0 copy-start.1
  317.6 3.6 convolution_convert_fusion
  321.1 0.0 copy-start.3
  321.2 0.1 copy.34
  321.2 0.0 copy-done.2
  321.2 0.3 fusion.4
  321.6 0.2 copy.23
  321.7 19.5 %all_to_all.35 = bf16[16,16,512]{2,0,1:T(8,128)(2,1)S(1)} all-to-all(bf16[16,16,512]{2,0,1:T(8,128)(2,1)S(1)} %copy.23), channel_id=1, replica_groups=mesh['slab'=16,'coil'=8] {'slab'}, dimensions={1} | all-to-all | bytes 524288 | tf_op jit(solution)/shard_map/all_to_all | solution.py:205
  341.3 0.1 reshape.61
  341.3 0.2 copy.24
  341.5 0.0 copy-done.1
  341.5 0.3 fusion.7
  341.9 0.2 copy.25
  342.0 0.9 reshape.62
  342.9 4.2 %all-to-all-start.3 = ((bf16[16,16,512]{2,1,0:T(8,128)(2,1)}), bf16[16,16,512]{2,1,0:T(8,128)(2,1)}, u32[]{:S(2)}, u32[]{:S(2)}) async-start(bf16[16,16,512]{2,1,0:T(8,128)(2,1)} %reshape.62), calls=%async_computation.3 | async-start | bytes 524288 | tf_op jit(solution)/shard_map/all_to_all | solution.py:211
  347.1 0.0 copy-done.3
  347.1 0.2 fusion.13
  347.4 8.2 %all-to-all-done.3 = bf16[16,16,512]{2,1,0:T(8,128)(2,1)} async-done(((bf16[16,16,512]{2,1,0:T(8,128)(2,1)}), bf16[16,16,512]{2,1,0:T(8,128)(2,1)}, u32[]{:S(2)}, u32[]{:S(2)}) %all-to-all-start.3) | async-done | bytes 262176 | tf_op jit(solution)/shard_map/all_to_all | solution.py:211
  355.6 5.3 %all-to-all-start.4 = ((bf16[8,2,16,512]{3,2,1,0:T(8,128)(2,1)}), bf16[8,2,16,512]{3,2,1,0:T(8,128)(2,1)S(1)}, u32[]{:S(2)}, u32[]{:S(2)}) async-start(bf16[8,2,16,512]{3,2,1,0:T(8,128)(2,1)} %bitcast.19), calls=%async_computation.4 | async-start | bytes 524288 | tf_op jit(solution)/shard_map/all_to_all | solution.py:216
  360.9 7.5 %all-to-all-done.4 = bf16[8,2,16,512]{3,2,1,0:T(8,128)(2,1)S(1)} async-done(((bf16[8,2,16,512]{3,2,1,0:T(8,128)(2,1)}), bf16[8,2,16,512]{3,2,1,0:T(8,128)(2,1)S(1)}, u32[]{:S(2)}, u32[]{:S(2)}) %all-to-all-start.4) | async-done | bytes 262176 | tf_op jit(solution)/shard_map/all_to_all | solution.py:216
  368.5 0.1 add_reduce_fusion
  368.6 0.7 copy.28
  (8 shorter events, 0.1 us)
Async XLA Ops:
  35.4 65.6 %all-to-all-start = ((s32[16,10,128]{2,1,0:T(8,128)}), s32[16,10,128]{2,1,0:T(8,128)S(1)}, u32[]{:S(2)}, u32[]{:S(2)}) async-start(s32[16,10,128]{2,1,0:T(8,128)} %reshape.55), calls=%async_computation | async-start | bytes 262144 | tf_op jit(solution)/shard_map/all_to_all | solution.py:188
  101.0 87.5 %all-to-all-start.1 = ((bf16[16,1280,128]{2,1,0:T(8,128)(2,1)}), bf16[16,1280,128]{2,1,0:T(8,128)(2,1)}, u32[]{:S(2)}, u32[]{:S(2)}) async-start(bf16[16,1280,128]{2,1,0:T(8,128)(2,1)} %bitcast.55), calls=%async_computation.1 | async-start | bytes 10485760 | tf_op jit(solution)/shard_map/all_to_all | solution.py:192
  308.1 1.9 copy-start
  310.0 7.6 %copy-start.4 = (bf16[512,32]{1,0:T(8,128)(2,1)S(1)}, bf16[512,32]{1,0:T(8,128)(2,1)}, u32[]{:S(2)}) copy-start(bf16[512,32]{1,0:T(8,128)(2,1)} %constant.26.clone) | copy-start | bytes 98308
  317.6 3.7 copy-start.2
  317.6 23.9 %copy-start.1 = (bf16[2,2,256,256]{3,2,1,0:T(8,128)(2,1)S(1)}, bf16[2,2,256,256]{3,2,1,0:T(8,128)(2,1)}, u32[]{:S(2)}) copy-start(bf16[2,2,256,256]{3,2,1,0:T(8,128)(2,1)} %constant.38) | copy-start | bytes 1572868
  321.1 26.0 %copy-start.3 = (bf16[8,16,2,512]{3,2,1,0:T(2,128)(2,1)S(1)}, bf16[8,16,2,512]{3,2,1,0:T(2,128)(2,1)}, u32[]{:S(2)}) copy-start(bf16[8,16,2,512]{3,2,1,0:T(2,128)(2,1)} %param.16) | copy-start | bytes 786436
  342.9 12.7 %all-to-all-start.3 = ((bf16[16,16,512]{2,1,0:T(8,128)(2,1)}), bf16[16,16,512]{2,1,0:T(8,128)(2,1)}, u32[]{:S(2)}, u32[]{:S(2)}) async-start(bf16[16,16,512]{2,1,0:T(8,128)(2,1)} %reshape.62), calls=%async_computation.3 | async-start | bytes 524288 | tf_op jit(solution)/shard_map/all_to_all | solution.py:211
  355.6 12.8 %all-to-all-start.4 = ((bf16[8,2,16,512]{3,2,1,0:T(8,128)(2,1)}), bf16[8,2,16,512]{3,2,1,0:T(8,128)(2,1)S(1)}, u32[]{:S(2)}, u32[]{:S(2)}) async-start(bf16[8,2,16,512]{3,2,1,0:T(8,128)(2,1)} %bitcast.19), calls=%async_computation.4 | async-start | bytes 524288 | tf_op jit(solution)/shard_map/all_to_all | solution.py:216

commit v8 on v7

--- a/solution.py
+++ b/solution.py
@@ -16,6 +16,8 @@
 CELLS = 64
 SLABS = 16
 STEP = 2048
+ADDED = 1024
+LANES = 4
 NT = (((1,), (1,)), ((), ()))
 
 
@@ -122,44 +124,97 @@
     )(pos_t, count, samples)
 
 
-def add_kernel(rows_ref, values_ref, out_ref, acc):
-    step = pl.program_id(0)
-    length = values_ref.shape[0]
-
-    @pl.when(step == 0)
-    def _():
-        acc[...] = jnp.zeros_like(acc)
+def pack_kernel(slot_ref, row_ref, zeros_ref, values_ref, out_ref, target_ref, wide):
+    pltpu.sync_copy(zeros_ref, target_ref)
+    wide[...] = jnp.zeros_like(wide)
 
     def some(i, carry):
         start = pl.multiple_of(i * 16, 16)
         values = values_ref[pl.ds(start, 16), :].astype(jnp.float32)
         for q in range(16):
-            row = rows_ref[step * length + start + q]
-            acc[pl.ds(row, 1), :] += values[q : q + 1]
+            slot = slot_ref[start + q]
+            wide[pl.ds(slot, 1), :] = values[q : q + 1]
+            target_ref[slot] = row_ref[start + q]
         return carry
 
-    lax.fori_loop(0, length // 16, some, 0, unroll=2)
+    lax.fori_loop(0, values_ref.shape[0] // 16, some, 0, unroll=2)
+    out_ref[...] = wide[...].astype(jnp.bfloat16)
+
+
+def pack_rows(slot, row, values, slots):
+    blocks = values.shape[0]
+    return pl.pallas_call(
+        pack_kernel,
+        grid_spec=pltpu.PrefetchScalarGridSpec(
+            num_scalar_prefetch=2,
+            grid=(1,),
+            in_specs=[
+                pl.BlockSpec(memory_space=pl.ANY),
+                pl.BlockSpec((blocks, 128), lambda i, slot, row: (0, 0)),
+            ],
+            out_specs=[
+                pl.BlockSpec((slots, 128), lambda i, slot, row: (0, 0)),
+                pl.BlockSpec(memory_space=pltpu.SMEM),
+            ],
+            scratch_shapes=[pltpu.VMEM((slots, 128), jnp.float32)],
+        ),
+        out_shape=[
+            jax.ShapeDtypeStruct((slots, 128), jnp.bfloat16),
+            jax.ShapeDtypeStruct((slots,), jnp.int32),
+        ],
+        compiler_params=pltpu.CompilerParams(vmem_limit_bytes=48 * 1024 * 1024),
+        name="pack_rows",
+    )(slot, row, jnp.zeros((slots,), jnp.int32), values)
+
+
+def add_kernel(rows_ref, *refs):
+    values_refs, out_ref, accs = refs[:LANES], refs[LANES], refs[LANES + 1 :]
+    step = pl.program_id(0)
+    length = values_refs[0].shape[0]
+    share = length * pl.num_programs(0)
+
+    @pl.when(step == 0)
+    def _():
+        for acc in accs:
+            acc[...] = jnp.zeros_like(acc)
+
+    def some(i, carry):
+        start = pl.multiple_of(i * 16, 16)
+        values = [ref[pl.ds(start, 16), :].astype(jnp.float32) for ref in values_refs]
+        for q in range(16):
+            for n in range(LANES):
+                row = rows_ref[n * share + step * length + start + q]
+                accs[n][pl.ds(row, 1), :] += values[n][q : q + 1]
+        return carry
+
+    lax.fori_loop(0, length // 16, some, 0)
 
     @pl.when(step == pl.num_programs(0) - 1)
     def _():
-        out_ref[...] = acc[...].astype(jnp.bfloat16)
+        total = accs[0][...]
+        for acc in accs[1:]:
+            total = total + acc[...]
+        out_ref[...] = total.astype(jnp.bfloat16)
 
 
 def add_rows(rows, values, total):
     slots = values.shape[0]
+    steps = slots // LANES // ADDED
     return pl.pallas_call(
         add_kernel,
         grid_spec=pltpu.PrefetchScalarGridSpec(
             num_scalar_prefetch=1,
-            grid=(slots // STEP,),
-            in_specs=[pl.BlockSpec((STEP, 128), lambda i, rows: (i, 0))],
+            grid=(steps,),
+            in_specs=[
+                pl.BlockSpec((ADDED, 128), lambda i, rows, n=n: (n * steps + i, 0)) for n in range(LANES)
+            ],
             out_specs=pl.BlockSpec((total, 128), lambda i, rows: (0, 0)),
-            scratch_shapes=[pltpu.VMEM((total, 128), jnp.float32)],
+            scratch_shapes=[pltpu.VMEM((total, 128), jnp.float32)] * LANES,
         ),
         out_shape=jax.ShapeDtypeStruct((total, 128), jnp.bfloat16),
-        compiler_params=pltpu.CompilerParams(vmem_limit_bytes=48 * 1024 * 1024),
+        compiler_params=pltpu.CompilerParams(vmem_limit_bytes=58 * 1024 * 1024),
         name="add_rows",
-    )(rows, values)
+    )(rows, *[values] * LANES)
 
 
 def slots_of(slab, slabs, capacity):
@@ -183,13 +238,12 @@
     width = sensitivity.shape[2]
     capacity = 5 * blocks // (2 * slabs)
     slot = slots_of(block_slab[:, 0], slabs, capacity)
-    target = jnp.zeros((slabs * capacity,), jnp.int32).at[slot].set(grid_block)
+    gridded = grid_blocks(sample_pos.T, block_count[None], samples[0])
+    packed, target = pack_rows(slot, grid_block, gridded, slabs * capacity)
+    packed = packed.reshape(slabs, capacity, 128)
+    packed = lax.all_to_all(packed, "slab", split_axis=0, concat_axis=0, tiled=True)
     target = target.reshape(slabs, capacity // 128, 128)
     target = lax.all_to_all(target, "slab", split_axis=0, concat_axis=0, tiled=True)
-    gridded = grid_blocks(sample_pos.T, block_count[None], samples[0])
-    packed = jnp.zeros((slabs * capacity, 128), jnp.bfloat16).at[slot].set(gridded)
-    packed = packed.reshape(slabs, capacity, 128)
-    packed = lax.all_to_all(packed, "slab", split_axis=0, concat_axis=0, tiled=True)
     kspace = add_rows(target.reshape(-1), packed.reshape(-1, 128), planes * KY * KX // CELLS)
     x_rows = jnp.dot(
         kspace.reshape(planes * KY, 2 * KX),

time: 371 us -> 260 us (0.70)
  Pallas kernels: 153 us -> 93.4 us
  local copies, waits for them, and re-layouts: 67.8 us -> 12.2 us
  blocking collectives: 19.5 us -> 39.1 us
  starting transfers between devices: 23.8 us -> 14.3 us
  waiting for transfers between devices: 96 us -> 90.8 us
    pallas_call x1, Pallas kernels: 120 us -> 37.3 us  [add_rows(): pl.pallas_call(add_kernel, grid_spec=pltpu.PrefetchScalarGridSpec(num_sca...]
    scatter x2 -> x0, local copies, waits for them, and re-layouts: 55.2 us -> none  [the longest x1 30.7 us: per_device(): target = jnp.zeros((slabs * capacity,), jnp.int32).at[slot].set(grid_block)]
    pallas_call x0 -> x1, Pallas kernels: none -> 22.2 us  [pack_rows(): pl.pallas_call(pack_kernel, grid_spec=pltpu.PrefetchScalarGridSpec(num_sc...]
    all_to_all x0 -> x1, blocking collectives: none -> 14.8 us  [per_device(): lax.all_to_all(target, 'slab', split_axis=0, concat_axis=0, tiled=True)]
    all_to_all x1 -> x0, starting transfers between devices: 7.12 us -> none  [per_device(): lax.all_to_all(target, 'slab', split_axis=0, concat_axis=0, tiled=True)]
    all_to_all x1, waiting for transfers between devices: 80.2 us -> 75.1 us  [per_device(): lax.all_to_all(packed, 'slab', split_axis=0, concat_axis=0, tiled=True)]
    all_to_all x1, blocking collectives: 19.5 us -> 24.4 us  [per_device(): lax.all_to_all(y_planes, 'slab', split_axis=1, concat_axis=0, tiled=True)]
  transfers between devices with their start and end apart: 4 -> 3, of which waited for: 3 -> 3; matrix products, arithmetic and copies ran while one was open for 7% -> 0% of each run, Pallas kernels for 9% -> 0%
where the time goes in v8:
time: 260 us; the launch traced here: 258 us
  Pallas kernels  93.4 us (36%)
  waiting for transfers between devices  90.8 us (35%)
  blocking collectives  39.1 us (15%)
  starting transfers between devices  14.3 us (6%)
  local copies, waits for them, and re-layouts  12.2 us (5%)
  matrix products  6.41 us (2%)
    all_to_all x1, waiting for transfers between devices, per_device(): lax.all_to_all(packed, 'slab', split_axis=0, concat_axis=0, tiled=True)  75.1 us
    pallas_call x1, Pallas kernels, add_rows(): pl.pallas_call(add_kernel, grid_spec=pltpu.PrefetchScalarGridSpec(num_sca...  37.3 us
    pallas_call x1, Pallas kernels, grid_blocks(): pl.pallas_call(grid_kernel, grid=(blocks // STEP,), in_specs=[pl.BlockSpe...  33.9 us
    all_to_all x1, blocking collectives, per_device(): lax.all_to_all(y_planes, 'slab', split_axis=1, concat_axis=0, tiled=True)  24.4 us
    pallas_call x1, Pallas kernels, pack_rows(): pl.pallas_call(pack_kernel, grid_spec=pltpu.PrefetchScalarGridSpec(num_sc...  22.2 us
    all_to_all x1, blocking collectives, per_device(): lax.all_to_all(target, 'slab', split_axis=0, concat_axis=0, tiled=True)  14.8 us
    all_to_all x1, waiting for transfers between devices, per_device(): own = lax.all_to_all(whole, 'slab', split_axis=0, concat_axis=0, tiled=True)  8.21 us
    reshape x1, local copies, waits for them, and re-layouts, per_device(): kspace.reshape(planes * KY, 2 * KX)  7.54 us
  transfers between devices with their start and end apart: 3, of which 3 were waited for; matrix products, arithmetic and copies ran while one was open for 0% of the time, Pallas kernels for 0%

profile of v8, /device:TPU:0, one launch (start us, length us, event | category | flops | bytes accessed | tf_op | source)
XLA Modules:
  0.0 258.4 jit_solution(9727971278738784372)
XLA Ops:
  0.0 0.0 copy-start.1
  0.0 0.8 broadcast_multiply_fusion
  0.8 1.0 convert_reduce_fusion
  1.8 0.9 fusion.10
  2.7 1.3 fusion.4
  4.0 33.9 %grid_blocks.1.values_ref = bf16[8192,128]{1,0:T(8,128)(2,1)} custom-call(bf16[64,8192]{1,0:T(8,128)(2,1)} %bitcast.58, s32[1,8192]{1,0:T(1,128)} %bitcast.65, bf16[8192,128]{1,0:T(8,128)(2,1)} %bitcast.57), custom_call_target="tpu_custom_call" | custom-call | tf_op jit(solution)/shard_map/grid_blocks/pallas_call | solution.py:111
  37.9 0.0 copy-done.1
  37.9 0.0 copy-start
  37.9 1.6 copy-done
  39.5 22.2 %pack_rows.1 = (bf16[20480,128]{1,0:T(8,128)(2,1)}, s32[20480]{0:T(1024)S(1)}) custom-call(s32[8192]{0:T(1024)S(1)} %bitcast_add_fusion.slot_ref, s32[8192]{0:T(1024)S(1)} %copy-done.1, s32[20480]{0:T(1024)S(1)} %broadcast_in_dim.8.zeros_ref, bf16[8192,128]{1,0:T(8,128)(2,1)S(1)} %copy-done), custom_call_target="tpu_custom_call" | custom-call | tf_op jit(solution)/shard_map/pack_rows/pallas_call | solution.py:146
  61.8 14.8 %all_to_all.35 = s32[16,10,128]{2,1,0:T(8,128)S(1)} all-to-all(s32[16,10,128]{2,1,0:T(8,128)S(1)} %reshape.44), channel_id=1, replica_groups=mesh['slab'=16,'coil'=8] {'slab'}, dimensions={0} | all-to-all | bytes 163840 | tf_op jit(solution)/shard_map/all_to_all | solution.py:246
  76.5 4.8 %all-to-all-start.1 = ((bf16[16,1280,128]{2,1,0:T(8,128)(2,1)}), bf16[16,1280,128]{2,1,0:T(8,128)(2,1)}, u32[]{:S(2)}, u32[]{:S(2)}) async-start(bf16[16,1280,128]{2,1,0:T(8,128)(2,1)} %bitcast.56), calls=%async_computation.1 | async-start | bytes 10485760 | tf_op jit(solution)/shard_map/all_to_all | solution.py:244
  81.3 0.6 reshape.45.rows_ref
  81.9 75.1 %all-to-all-done.1 = bf16[16,1280,128]{2,1,0:T(8,128)(2,1)} async-done(((bf16[16,1280,128]{2,1,0:T(8,128)(2,1)}), bf16[16,1280,128]{2,1,0:T(8,128)(2,1)}, u32[]{:S(2)}, u32[]{:S(2)}) %all-to-all-start.1) | async-done | bytes 5242912 | tf_op jit(solution)/shard_map/all_to_all | solution.py:244
  157.0 37.3 %add_rows.1 = bf16[16384,128]{1,0:T(8,128)(2,1)} custom-call(s32[20480]{0:T(1024)} %reshape.45.rows_ref, bf16[20480,128]{1,0:T(8,128)(2,1)} %bitcast.9.refs_0_.refs_1_.refs_2_.refs_3_, bf16[20480,128]{1,0:T(8,128)(2,1)} %bitcast.9.refs_0_.refs_1_.refs_2_.refs_3_, bf16[20480,128]{1,0:T(8,128)(2,1)} %bitcast.9.refs_0_.refs_1_.refs_2_.refs_3_, ...), custom_call_target="tpu_custom_call" | custom-call | tf_op jit(solution)/shard_map/add_rows/pallas_call | solution.py:203
  194.4 0.0 copy-start.5
  194.4 7.5 %reshape.48 = bf16[4096,512]{1,0:T(8,128)(2,1)} reshape(bf16[16384,128]{1,0:T(8,128)(2,1)} %add_rows.1) | data formatting | bytes 8388608 | tf_op jit(solution)/shard_map/reshape | solution.py:249
  201.9 0.0 copy-done.5
  201.9 0.0 copy-start.3
  201.9 0.0 copy-start.2
  201.9 3.6 %convolution_convert_fusion = bf16[4096,32]{0,1:T(8,128)(2,1)S(1)} fusion(bf16[4096,512]{1,0:T(8,128)(2,1)} %reshape.48, bf16[512,32]{1,0:T(8,128)(2,1)S(1)} %copy-done.5), kind=kOutput, calls=%fused_computation | convolution fusion | flops 134348800 | bytes 4489216 | tf_op jit(solution)/shard_map/dot_general | solution.py:248
  205.5 0.0 copy-start.4
  205.5 0.1 copy.34
  205.6 0.0 copy-done.3
  205.6 0.3 fusion.2
  205.9 0.2 copy.23
  206.0 24.4 %all_to_all.36 = bf16[16,16,512]{2,0,1:T(8,128)(2,1)S(1)} all-to-all(bf16[16,16,512]{2,0,1:T(8,128)(2,1)S(1)} %copy.23), channel_id=1, replica_groups=mesh['slab'=16,'coil'=8] {'slab'}, dimensions={1} | all-to-all | bytes 524288 | tf_op jit(solution)/shard_map/all_to_all | solution.py:259
  230.4 0.1 reshape.50
  230.5 0.2 copy.24
  230.7 0.0 copy-done.2
  230.7 0.3 fusion.5
  231.0 0.2 copy.25
  231.2 0.9 reshape.51
  232.1 4.2 %all-to-all-start.3 = ((bf16[16,16,512]{2,1,0:T(8,128)(2,1)}), bf16[16,16,512]{2,1,0:T(8,128)(2,1)}, u32[]{:S(2)}, u32[]{:S(2)}) async-start(bf16[16,16,512]{2,1,0:T(8,128)(2,1)} %reshape.51), calls=%async_computation.3 | async-start | bytes 524288 | tf_op jit(solution)/shard_map/all_to_all | solution.py:265
  236.3 0.0 copy-done.4
  236.3 0.2 fusion.9
  236.5 8.2 %all-to-all-done.3 = bf16[16,16,512]{2,1,0:T(8,128)(2,1)} async-done(((bf16[16,16,512]{2,1,0:T(8,128)(2,1)}), bf16[16,16,512]{2,1,0:T(8,128)(2,1)}, u32[]{:S(2)}, u32[]{:S(2)}) %all-to-all-start.3) | async-done | bytes 262176 | tf_op jit(solution)/shard_map/all_to_all | solution.py:265
  244.7 5.3 %all-to-all-start.4 = ((bf16[8,2,16,512]{3,2,1,0:T(8,128)(2,1)}), bf16[8,2,16,512]{3,2,1,0:T(8,128)(2,1)S(1)}, u32[]{:S(2)}, u32[]{:S(2)}) async-start(bf16[8,2,16,512]{3,2,1,0:T(8,128)(2,1)} %bitcast.19), calls=%async_computation.4 | async-start | bytes 524288 | tf_op jit(solution)/shard_map/all_to_all | solution.py:270
  250.1 7.5 %all-to-all-done.4 = bf16[8,2,16,512]{3,2,1,0:T(8,128)(2,1)S(1)} async-done(((bf16[8,2,16,512]{3,2,1,0:T(8,128)(2,1)}), bf16[8,2,16,512]{3,2,1,0:T(8,128)(2,1)S(1)}, u32[]{:S(2)}, u32[]{:S(2)}) %all-to-all-start.4) | async-done | bytes 262176 | tf_op jit(solution)/shard_map/all_to_all | solution.py:270
  257.7 0.1 add_reduce_fusion
  257.8 0.7 copy.28
  (9 shorter events, 0.2 us)
Async XLA Ops:
  0.0 37.9 %copy-start.1 = (s32[8192]{0:T(1024)S(1)}, s32[8192]{0:T(1024)}, u32[]{:S(2)}) copy-start(s32[8192]{0:T(1024)} %row_ref.1) | copy-start | bytes 98308
  37.9 1.6 copy-start
  76.5 80.5 %all-to-all-start.1 = ((bf16[16,1280,128]{2,1,0:T(8,128)(2,1)}), bf16[16,1280,128]{2,1,0:T(8,128)(2,1)}, u32[]{:S(2)}, u32[]{:S(2)}) async-start(bf16[16,1280,128]{2,1,0:T(8,128)(2,1)} %bitcast.56), calls=%async_computation.1 | async-start | bytes 10485760 | tf_op jit(solution)/shard_map/all_to_all | solution.py:244
  194.4 7.5 %copy-start.5 = (bf16[512,32]{1,0:T(8,128)(2,1)S(1)}, bf16[512,32]{1,0:T(8,128)(2,1)}, u32[]{:S(2)}) copy-start(bf16[512,32]{1,0:T(8,128)(2,1)} %constant.21.clone) | copy-start | bytes 98308
  201.9 3.7 %copy-start.3 = (bf16[2,256,512,1]{2,1,0,3:T(8,128)(2,1)S(1)}, bf16[2,256,512,1]{2,1,0,3:T(8,128)(2,1)}, u32[]{:S(2)}) copy-start(bf16[2,256,512,1]{2,1,0,3:T(8,128)(2,1)} %constant.35) | copy-start | bytes 1572868
  201.9 28.7 %copy-start.2 = (bf16[2,2,256,256]{3,2,1,0:T(8,128)(2,1)S(1)}, bf16[2,2,256,256]{3,2,1,0:T(8,128)(2,1)}, u32[]{:S(2)}) copy-start(bf16[2,2,256,256]{3,2,1,0:T(8,128)(2,1)} %constant.33) | copy-start | bytes 1572868
  205.5 30.8 %copy-start.4 = (bf16[8,16,2,512]{3,2,1,0:T(2,128)(2,1)S(1)}, bf16[8,16,2,512]{3,2,1,0:T(2,128)(2,1)}, u32[]{:S(2)}) copy-start(bf16[8,16,2,512]{3,2,1,0:T(2,128)(2,1)} %param.16) | copy-start | bytes 786436
  232.1 12.7 %all-to-all-start.3 = ((bf16[16,16,512]{2,1,0:T(8,128)(2,1)}), bf16[16,16,512]{2,1,0:T(8,128)(2,1)}, u32[]{:S(2)}, u32[]{:S(2)}) async-start(bf16[16,16,512]{2,1,0:T(8,128)(2,1)} %reshape.51), calls=%async_computation.3 | async-start | bytes 524288 | tf_op jit(solution)/shard_map/all_to_all | solution.py:265
  244.7 12.9 %all-to-all-start.4 = ((bf16[8,2,16,512]{3,2,1,0:T(8,128)(2,1)}), bf16[8,2,16,512]{3,2,1,0:T(8,128)(2,1)S(1)}, u32[]{:S(2)}, u32[]{:S(2)}) async-start(bf16[8,2,16,512]{3,2,1,0:T(8,128)(2,1)} %bitcast.19), calls=%async_computation.4 | async-start | bytes 524288 | tf_op jit(solution)/shard_map/all_to_all | solution.py:270

commit v9 on v8

--- a/solution.py
+++ b/solution.py
@@ -168,7 +168,8 @@
 
 
 def add_kernel(rows_ref, *refs):
-    values_refs, out_ref, accs = refs[:LANES], refs[LANES], refs[LANES + 1 :]
+    values_refs, table_ref, out_ref, accs = refs[:LANES], refs[LANES], refs[LANES + 1], refs[LANES + 2 :]
+    segments = KX // CELLS
     step = pl.program_id(0)
     length = values_refs[0].shape[0]
     share = length * pl.num_programs(0)
@@ -191,13 +192,19 @@
 
     @pl.when(step == pl.num_programs(0) - 1)
     def _():
-        total = accs[0][...]
-        for acc in accs[1:]:
-            total = total + acc[...]
-        out_ref[...] = total.astype(jnp.bfloat16)
-
-
-def add_rows(rows, values, total):
+        x_rows = None
+        for n in range(segments):
+            every = pl.ds(n, out_ref.shape[0], stride=segments)
+            total = accs[0][every, :]
+            for acc in accs[1:]:
+                total = total + acc[every, :]
+            kspace = total.astype(jnp.bfloat16)
+            term = jnp.dot(kspace, table_ref[n], preferred_element_type=jnp.float32)
+            x_rows = term if x_rows is None else x_rows + term
+        out_ref[...] = x_rows.astype(jnp.bfloat16)
+
+
+def add_rows(rows, values, table, total):
     slots = values.shape[0]
     steps = slots // LANES // ADDED
     return pl.pallas_call(
@@ -207,14 +214,15 @@
             grid=(steps,),
             in_specs=[
                 pl.BlockSpec((ADDED, 128), lambda i, rows, n=n: (n * steps + i, 0)) for n in range(LANES)
-            ],
-            out_specs=pl.BlockSpec((total, 128), lambda i, rows: (0, 0)),
+            ]
+            + [pl.BlockSpec(table.shape, lambda i, rows: (0, 0, 0))],
+            out_specs=pl.BlockSpec((total // table.shape[0], table.shape[2]), lambda i, rows: (0, 0)),
             scratch_shapes=[pltpu.VMEM((total, 128), jnp.float32)] * LANES,
         ),
-        out_shape=jax.ShapeDtypeStruct((total, 128), jnp.bfloat16),
+        out_shape=jax.ShapeDtypeStruct((total // table.shape[0], table.shape[2]), jnp.bfloat16),
         compiler_params=pltpu.CompilerParams(vmem_limit_bytes=58 * 1024 * 1024),
         name="add_rows",
-    )(rows, *[values] * LANES)
+    )(rows, *[values] * LANES, table)
 
 
 def slots_of(slab, slabs, capacity):
@@ -244,12 +252,10 @@
     packed = lax.all_to_all(packed, "slab", split_axis=0, concat_axis=0, tiled=True)
     target = target.reshape(slabs, capacity // 128, 128)
     target = lax.all_to_all(target, "slab", split_axis=0, concat_axis=0, tiled=True)
-    kspace = add_rows(target.reshape(-1), packed.reshape(-1, 128), planes * KY * KX // CELLS)
-    x_rows = jnp.dot(
-        kspace.reshape(planes * KY, 2 * KX),
-        jnp.asarray(across_table(), jnp.bfloat16),
-        preferred_element_type=jnp.float32,
-    ).astype(jnp.bfloat16)
+    table = jnp.asarray(across_table().reshape(KX // CELLS, 2 * CELLS, 2 * XW), jnp.bfloat16)
+    x_rows = add_rows(
+        target.reshape(-1), packed.reshape(-1, 128), table, planes * KY * KX // CELLS
+    )
     y_planes = jnp.einsum(
         "zkqx,qkn->zxn",
         x_rows.reshape(planes, KY, 2, XW),

time: 260 us -> 250 us (0.962)
  blocking collectives: 39.1 us -> 30.5 us
  Pallas kernels: 93.4 us -> 102 us
  local copies, waits for them, and re-layouts: 12.2 us -> 6.23 us
  matrix products: 6.41 us -> 2.85 us
    all_to_all x1, blocking collectives: 24.4 us -> 15.7 us  [per_device(): lax.all_to_all(y_planes, 'slab', split_axis=1, concat_axis=0, tiled=True)]
    pallas_call x1, Pallas kernels: 37.3 us -> 46 us  [add_rows(): pl.pallas_call(add_kernel, grid_spec=pltpu.PrefetchScalarGridSpec(num_sca...]
    reshape x1 -> x0, local copies, waits for them, and re-layouts: 7.54 us -> none  [per_device(): kspace.reshape(planes * KY, 2 * KX)]
    dot_general x1 -> x0, matrix products: 3.57 us -> none  [per_device(): jnp.dot(kspace.reshape(planes * KY, 2 * KX), jnp.asarray(across_table(),...]
where the time goes in v9:
time: 250 us; the launch traced here: 249 us
  Pallas kernels  102 us (41%)
  waiting for transfers between devices  90.8 us (36%)
  blocking collectives  30.5 us (12%)
  starting transfers between devices  14.3 us (6%)
  local copies, waits for them, and re-layouts  6.23 us (2%)
  matrix products  2.85 us (1%)
    all_to_all x1, waiting for transfers between devices, per_device(): lax.all_to_all(packed, 'slab', split_axis=0, concat_axis=0, tiled=True)  75.1 us
    pallas_call x1, Pallas kernels, add_rows(): pl.pallas_call(add_kernel, grid_spec=pltpu.PrefetchScalarGridSpec(num_sca...  46 us
    pallas_call x1, Pallas kernels, grid_blocks(): pl.pallas_call(grid_kernel, grid=(blocks // STEP,), in_specs=[pl.BlockSpe...  33.9 us
    pallas_call x1, Pallas kernels, pack_rows(): pl.pallas_call(pack_kernel, grid_spec=pltpu.PrefetchScalarGridSpec(num_sc...  22.2 us
    all_to_all x1, blocking collectives, per_device(): lax.all_to_all(y_planes, 'slab', split_axis=1, concat_axis=0, tiled=True)  15.7 us
    all_to_all x1, blocking collectives, per_device(): lax.all_to_all(target, 'slab', split_axis=0, concat_axis=0, tiled=True)  14.8 us
    all_to_all x1, waiting for transfers between devices, per_device(): own = lax.all_to_all(whole, 'slab', split_axis=0, concat_axis=0, tiled=True)  8.21 us
    all_to_all x1, waiting for transfers between devices, per_device(): own = lax.all_to_all(own, 'coil', split_axis=0, concat_axis=0, tiled=True)  7.51 us
  transfers between devices with their start and end apart: 3, of which 3 were waited for; matrix products, arithmetic and copies ran while one was open for 0% of the time, Pallas kernels for 0%

profile of v9, /device:TPU:0, one launch (start us, length us, event | category | flops | bytes accessed | tf_op | source)
XLA Modules:
  0.0 248.9 jit_solution(2602321004790287373)
XLA Ops:
  0.0 0.0 copy-start.1
  0.0 0.8 broadcast_multiply_fusion
  0.8 1.0 convert_reduce_fusion
  1.8 0.9 fusion.10
  2.7 1.3 fusion.4
  4.0 33.9 %grid_blocks.1.values_ref = bf16[8192,128]{1,0:T(8,128)(2,1)} custom-call(bf16[64,8192]{1,0:T(8,128)(2,1)} %bitcast.56, s32[1,8192]{1,0:T(1,128)} %bitcast.63, bf16[8192,128]{1,0:T(8,128)(2,1)} %bitcast.55), custom_call_target="tpu_custom_call" | custom-call | tf_op jit(solution)/shard_map/grid_blocks/pallas_call | solution.py:111
  37.9 0.0 copy-done.1
  37.9 0.0 copy-start
  37.9 1.6 copy-done
  39.5 22.2 %pack_rows.1 = (bf16[20480,128]{1,0:T(8,128)(2,1)}, s32[20480]{0:T(1024)S(1)}) custom-call(s32[8192]{0:T(1024)S(1)} %bitcast_add_fusion.slot_ref, s32[8192]{0:T(1024)S(1)} %copy-done.1, s32[20480]{0:T(1024)S(1)} %broadcast_in_dim.8.zeros_ref, bf16[8192,128]{1,0:T(8,128)(2,1)S(1)} %copy-done), custom_call_target="tpu_custom_call" | custom-call | tf_op jit(solution)/shard_map/pack_rows/pallas_call | solution.py:146
  61.8 14.8 %all_to_all.35 = s32[16,10,128]{2,1,0:T(8,128)S(1)} all-to-all(s32[16,10,128]{2,1,0:T(8,128)S(1)} %reshape.41), channel_id=1, replica_groups=mesh['slab'=16,'coil'=8] {'slab'}, dimensions={0} | all-to-all | bytes 163840 | tf_op jit(solution)/shard_map/all_to_all | solution.py:254
  76.5 4.8 %all-to-all-start.1 = ((bf16[16,1280,128]{2,1,0:T(8,128)(2,1)}), bf16[16,1280,128]{2,1,0:T(8,128)(2,1)}, u32[]{:S(2)}, u32[]{:S(2)}) async-start(bf16[16,1280,128]{2,1,0:T(8,128)(2,1)} %bitcast.54), calls=%async_computation.1 | async-start | bytes 10485760 | tf_op jit(solution)/shard_map/all_to_all | solution.py:252
  81.3 0.6 reshape.42.rows_ref
  81.9 75.1 %all-to-all-done.1 = bf16[16,1280,128]{2,1,0:T(8,128)(2,1)} async-done(((bf16[16,1280,128]{2,1,0:T(8,128)(2,1)}), bf16[16,1280,128]{2,1,0:T(8,128)(2,1)}, u32[]{:S(2)}, u32[]{:S(2)}) %all-to-all-start.1) | async-done | bytes 5242912 | tf_op jit(solution)/shard_map/all_to_all | solution.py:252
  157.1 0.0 copy-start.3
  157.1 0.0 copy-start.2
  157.1 46.0 %add_rows.1 = bf16[4096,32]{1,0:T(8,128)(2,1)} custom-call(s32[20480]{0:T(1024)} %reshape.42.rows_ref, bf16[20480,128]{1,0:T(8,128)(2,1)} %bitcast.9.refs_0_.refs_1_.refs_2_.refs_3_, bf16[20480,128]{1,0:T(8,128)(2,1)} %bitcast.9.refs_0_.refs_1_.refs_2_.refs_3_, bf16[20480,128]{1,0:T(8,128)(2,1)} %bitcast.9.refs_0_.refs_1_.refs_2_.refs_3_, ...), custom_call_target="tpu_custom_call" | custom-call | tf_op jit(solution)/shard_map/add_rows/pallas_call | solution.py:210
  203.0 0.0 copy-start.4
  203.0 1.6 copy.23
  204.7 0.0 copy-done.3
  204.7 0.3 fusion.2
  205.0 0.2 copy.25
  205.1 15.7 %all_to_all.36 = bf16[16,16,512]{2,0,1:T(8,128)(2,1)S(1)} all-to-all(bf16[16,16,512]{2,0,1:T(8,128)(2,1)S(1)} %copy.25), channel_id=1, replica_groups=mesh['slab'=16,'coil'=8] {'slab'}, dimensions={1} | all-to-all | bytes 524288 | tf_op jit(solution)/shard_map/all_to_all | solution.py:265
  220.8 0.1 reshape.46
  220.9 0.2 copy.26
  221.1 0.0 copy-done.2
  221.1 0.3 fusion.5
  221.4 0.2 copy.27
  221.6 0.9 reshape.47
  222.5 4.2 %all-to-all-start.3 = ((bf16[16,16,512]{2,1,0:T(8,128)(2,1)}), bf16[16,16,512]{2,1,0:T(8,128)(2,1)}, u32[]{:S(2)}, u32[]{:S(2)}) async-start(bf16[16,16,512]{2,1,0:T(8,128)(2,1)} %reshape.47), calls=%async_computation.3 | async-start | bytes 524288 | tf_op jit(solution)/shard_map/all_to_all | solution.py:271
  226.7 0.0 copy-done.4
  226.7 0.2 fusion.9
  227.0 8.2 %all-to-all-done.3 = bf16[16,16,512]{2,1,0:T(8,128)(2,1)} async-done(((bf16[16,16,512]{2,1,0:T(8,128)(2,1)}), bf16[16,16,512]{2,1,0:T(8,128)(2,1)}, u32[]{:S(2)}, u32[]{:S(2)}) %all-to-all-start.3) | async-done | bytes 262176 | tf_op jit(solution)/shard_map/all_to_all | solution.py:271
  235.2 5.3 %all-to-all-start.4 = ((bf16[8,2,16,512]{3,2,1,0:T(8,128)(2,1)}), bf16[8,2,16,512]{3,2,1,0:T(8,128)(2,1)S(1)}, u32[]{:S(2)}, u32[]{:S(2)}) async-start(bf16[8,2,16,512]{3,2,1,0:T(8,128)(2,1)} %bitcast.19), calls=%async_computation.4 | async-start | bytes 524288 | tf_op jit(solution)/shard_map/all_to_all | solution.py:276
  240.5 7.5 %all-to-all-done.4 = bf16[8,2,16,512]{3,2,1,0:T(8,128)(2,1)S(1)} async-done(((bf16[8,2,16,512]{3,2,1,0:T(8,128)(2,1)}), bf16[8,2,16,512]{3,2,1,0:T(8,128)(2,1)S(1)}, u32[]{:S(2)}, u32[]{:S(2)}) %all-to-all-start.4) | async-done | bytes 262176 | tf_op jit(solution)/shard_map/all_to_all | solution.py:276
  248.1 0.1 add_reduce_fusion
  248.2 0.7 copy.30
  (10 shorter events, 0.2 us)
Async XLA Ops:
  0.0 37.9 %copy-start.1 = (s32[8192]{0:T(1024)S(1)}, s32[8192]{0:T(1024)}, u32[]{:S(2)}) copy-start(s32[8192]{0:T(1024)} %row_ref.1) | copy-start | bytes 98308
  37.9 1.6 copy-start
  76.5 80.5 %all-to-all-start.1 = ((bf16[16,1280,128]{2,1,0:T(8,128)(2,1)}), bf16[16,1280,128]{2,1,0:T(8,128)(2,1)}, u32[]{:S(2)}, u32[]{:S(2)}) async-start(bf16[16,1280,128]{2,1,0:T(8,128)(2,1)} %bitcast.54), calls=%async_computation.1 | async-start | bytes 10485760 | tf_op jit(solution)/shard_map/all_to_all | solution.py:252
  157.1 47.6 %copy-start.3 = (bf16[2,256,512,1]{2,1,0,3:T(8,128)(2,1)S(1)}, bf16[2,256,512,1]{2,1,0,3:T(8,128)(2,1)}, u32[]{:S(2)}) copy-start(bf16[2,256,512,1]{2,1,0,3:T(8,128)(2,1)} %constant.35) | copy-start | bytes 1572868
  157.1 64.0 %copy-start.2 = (bf16[2,2,256,256]{3,2,1,0:T(8,128)(2,1)S(1)}, bf16[2,2,256,256]{3,2,1,0:T(8,128)(2,1)}, u32[]{:S(2)}) copy-start(bf16[2,2,256,256]{3,2,1,0:T(8,128)(2,1)} %constant.33) | copy-start | bytes 1572868
  203.0 23.7 %copy-start.4 = (bf16[8,16,2,512]{3,2,1,0:T(2,128)(2,1)S(1)}, bf16[8,16,2,512]{3,2,1,0:T(2,128)(2,1)}, u32[]{:S(2)}) copy-start(bf16[8,16,2,512]{3,2,1,0:T(2,128)(2,1)} %param.16) | copy-start | bytes 786436
  222.5 12.7 %all-to-all-start.3 = ((bf16[16,16,512]{2,1,0:T(8,128)(2,1)}), bf16[16,16,512]{2,1,0:T(8,128)(2,1)}, u32[]{:S(2)}, u32[]{:S(2)}) async-start(bf16[16,16,512]{2,1,0:T(8,128)(2,1)} %reshape.47), calls=%async_computation.3 | async-start | bytes 524288 | tf_op jit(solution)/shard_map/all_to_all | solution.py:271
  235.2 12.9 %all-to-all-start.4 = ((bf16[8,2,16,512]{3,2,1,0:T(8,128)(2,1)}), bf16[8,2,16,512]{3,2,1,0:T(8,128)(2,1)S(1)}, u32[]{:S(2)}, u32[]{:S(2)}) async-start(bf16[8,2,16,512]{3,2,1,0:T(8,128)(2,1)} %bitcast.19), calls=%async_computation.4 | async-start | bytes 524288 | tf_op jit(solution)/shard_map/all_to_all | solution.py:276

commit v10 on v9

--- a/solution.py
+++ b/solution.py
@@ -16,7 +16,6 @@
 CELLS = 64
 SLABS = 16
 STEP = 2048
-ADDED = 1024
 LANES = 4
 NT = (((1,), (1,)), ((), ()))
 
@@ -138,10 +137,15 @@
         return carry
 
     lax.fori_loop(0, values_ref.shape[0] // 16, some, 0, unroll=2)
-    out_ref[...] = wide[...].astype(jnp.bfloat16)
-
-
-def pack_rows(slot, row, values, slots):
+    slabs, padded, _ = out_ref.shape
+    capacity = wide.shape[0] // slabs
+    for k in range(slabs):
+        out_ref[k, 0:capacity, :] = wide[k * capacity : (k + 1) * capacity, :].astype(jnp.bfloat16)
+        out_ref[k, capacity:padded, :] = jnp.zeros((padded - capacity, 128), jnp.bfloat16)
+
+
+def pack_rows(slot, row, values, slabs, capacity, padded):
+    slots = slabs * capacity
     blocks = values.shape[0]
     return pl.pallas_call(
         pack_kernel,
@@ -153,13 +157,13 @@
                 pl.BlockSpec((blocks, 128), lambda i, slot, row: (0, 0)),
             ],
             out_specs=[
-                pl.BlockSpec((slots, 128), lambda i, slot, row: (0, 0)),
+                pl.BlockSpec((slabs, padded, 128), lambda i, slot, row: (0, 0, 0)),
                 pl.BlockSpec(memory_space=pltpu.SMEM),
             ],
             scratch_shapes=[pltpu.VMEM((slots, 128), jnp.float32)],
         ),
         out_shape=[
-            jax.ShapeDtypeStruct((slots, 128), jnp.bfloat16),
+            jax.ShapeDtypeStruct((slabs, padded, 128), jnp.bfloat16),
             jax.ShapeDtypeStruct((slots,), jnp.int32),
         ],
         compiler_params=pltpu.CompilerParams(vmem_limit_bytes=48 * 1024 * 1024),
@@ -171,7 +175,7 @@
     values_refs, table_ref, out_ref, accs = refs[:LANES], refs[LANES], refs[LANES + 1], refs[LANES + 2 :]
     segments = KX // CELLS
     step = pl.program_id(0)
-    length = values_refs[0].shape[0]
+    length = values_refs[0].shape[1]
     share = length * pl.num_programs(0)
 
     @pl.when(step == 0)
@@ -181,7 +185,7 @@
 
     def some(i, carry):
         start = pl.multiple_of(i * 16, 16)
-        values = [ref[pl.ds(start, 16), :].astype(jnp.float32) for ref in values_refs]
+        values = [ref[0, pl.ds(start, 16), :].astype(jnp.float32) for ref in values_refs]
         for q in range(16):
             for n in range(LANES):
                 row = rows_ref[n * share + step * length + start + q]
@@ -205,15 +209,15 @@
 
 
 def add_rows(rows, values, table, total):
-    slots = values.shape[0]
-    steps = slots // LANES // ADDED
+    steps = values.shape[0] // LANES
+    length = rows.shape[0] // values.shape[0]
     return pl.pallas_call(
         add_kernel,
         grid_spec=pltpu.PrefetchScalarGridSpec(
             num_scalar_prefetch=1,
             grid=(steps,),
             in_specs=[
-                pl.BlockSpec((ADDED, 128), lambda i, rows, n=n: (n * steps + i, 0)) for n in range(LANES)
+                pl.BlockSpec((1, length, 128), lambda i, rows, n=n: (n * steps + i, 0, 0)) for n in range(LANES)
             ]
             + [pl.BlockSpec(table.shape, lambda i, rows: (0, 0, 0))],
             out_specs=pl.BlockSpec((total // table.shape[0], table.shape[2]), lambda i, rows: (0, 0)),
@@ -247,14 +251,19 @@
     capacity = 5 * blocks // (2 * slabs)
     slot = slots_of(block_slab[:, 0], slabs, capacity)
     gridded = grid_blocks(sample_pos.T, block_count[None], samples[0])
-    packed, target = pack_rows(slot, grid_block, gridded, slabs * capacity)
-    packed = packed.reshape(slabs, capacity, 128)
+    spare = 16 - 2 * (capacity // 128) % 16
+    padded = capacity + 2 * (capacity // 128) + spare
+    packed, target = pack_rows(slot, grid_block, gridded, slabs, capacity, padded)
+    target = target.reshape(slabs, capacity // 128, 128)
+    marks = [target // 128, target % 128, jnp.zeros((slabs, spare, 128), jnp.int32)]
+    marks = jnp.concatenate(marks, axis=1).astype(jnp.bfloat16)
+    packed = lax.dynamic_update_slice(packed, marks, (0, capacity, 0))
     packed = lax.all_to_all(packed, "slab", split_axis=0, concat_axis=0, tiled=True)
-    target = target.reshape(slabs, capacity // 128, 128)
-    target = lax.all_to_all(target, "slab", split_axis=0, concat_axis=0, tiled=True)
+    marks = packed[:, capacity : capacity + 2 * (capacity // 128)].astype(jnp.int32)
+    target = marks[:, : capacity // 128] * 128 + marks[:, capacity // 128 :]
     table = jnp.asarray(across_table().reshape(KX // CELLS, 2 * CELLS, 2 * XW), jnp.bfloat16)
     x_rows = add_rows(
-        target.reshape(-1), packed.reshape(-1, 128), table, planes * KY * KX // CELLS
+        target.reshape(-1), packed, table, planes * KY * KX // CELLS
     )
     y_planes = jnp.einsum(
         "zkqx,qkn->zxn",

time: 250 us -> 227 us (0.908)
  waiting for transfers between devices: 90.8 us -> 15.7 us
  blocking collectives: 30.5 us -> 82.5 us
  starting transfers between devices: 14.3 us -> 9.5 us
    all_to_all x1 -> x0, waiting for transfers between devices: 75.1 us -> none  [per_device(): lax.all_to_all(packed, 'slab', split_axis=0, concat_axis=0, tiled=True)]
    all_to_all x1, blocking collectives: 14.8 us -> 71.2 us  [per_device(): lax.all_to_all(packed, 'slab', split_axis=0, concat_axis=0, tiled=True)]
    all_to_all x1 -> x0, starting transfers between devices: 4.76 us -> none  [per_device(): lax.all_to_all(packed, 'slab', split_axis=0, concat_axis=0, tiled=True)]
    all_to_all x1, blocking collectives: 15.7 us -> 11.2 us  [per_device(): lax.all_to_all(y_planes, 'slab', split_axis=1, concat_axis=0, tiled=True)]
  transfers between devices with their start and end apart: 3 -> 2, of which waited for: 3 -> 2; matrix products, arithmetic and copies ran while one was open for 0% -> 0% of each run, Pallas kernels for 0% -> 0%
where the time goes in v10:
time: 227 us; the launch traced here: 225 us
  Pallas kernels  103 us (45%)
  blocking collectives  82.5 us (36%)
  waiting for transfers between devices  15.7 us (7%)
  starting transfers between devices  9.5 us (4%)
  local copies, waits for them, and re-layouts  8.64 us (4%)
  other arithmetic  2.9 us (1%)
  matrix products  2.85 us (1%)
    all_to_all x1, blocking collectives, per_device(): lax.all_to_all(packed, 'slab', split_axis=0, concat_axis=0, tiled=True)  71.2 us
    pallas_call x1, Pallas kernels, add_rows(): pl.pallas_call(add_kernel, grid_spec=pltpu.PrefetchScalarGridSpec(num_sca...  47 us
    pallas_call x1, Pallas kernels, grid_blocks(): pl.pallas_call(grid_kernel, grid=(blocks // STEP,), in_specs=[pl.BlockSpe...  33.9 us
    pallas_call x1, Pallas kernels, pack_rows(): pl.pallas_call(pack_kernel, grid_spec=pltpu.PrefetchScalarGridSpec(num_sc...  22.2 us
    all_to_all x1, blocking collectives, per_device(): lax.all_to_all(y_planes, 'slab', split_axis=1, concat_axis=0, tiled=True)  11.2 us
    all_to_all x1, waiting for transfers between devices, per_device(): own = lax.all_to_all(whole, 'slab', split_axis=0, concat_axis=0, tiled=True)  8.21 us
    all_to_all x1, waiting for transfers between devices, per_device(): own = lax.all_to_all(own, 'coil', split_axis=0, concat_axis=0, tiled=True)  7.51 us
    all_to_all x1, starting transfers between devices, per_device(): own = lax.all_to_all(own, 'coil', split_axis=0, concat_axis=0, tiled=True)  5.31 us
  transfers between devices with their start and end apart: 2, of which 2 were waited for; matrix products, arithmetic and copies ran while one was open for 0% of the time, Pallas kernels for 0%

profile of v10, /device:TPU:0, one launch (start us, length us, event | category | flops | bytes accessed | tf_op | source)
XLA Modules:
  0.0 225.5 jit_solution(14224980063905342502)
XLA Ops:
  0.0 0.0 copy-start.1
  0.0 0.8 broadcast_multiply_fusion
  0.8 1.0 convert_reduce_fusion
  1.8 0.9 fusion.14
  2.7 1.3 fusion.4
  4.0 33.9 %grid_blocks.1.values_ref = bf16[8192,128]{1,0:T(8,128)(2,1)} custom-call(bf16[64,8192]{1,0:T(8,128)(2,1)} %bitcast.53, s32[1,8192]{1,0:T(1,128)} %bitcast.60, bf16[8192,128]{1,0:T(8,128)(2,1)} %bitcast.52), custom_call_target="tpu_custom_call" | custom-call | tf_op jit(solution)/shard_map/grid_blocks/pallas_call | solution.py:110
  37.9 0.0 copy-done.1
  37.9 0.0 copy-start
  37.9 1.6 copy-done
  39.5 22.2 %pack_rows.1 = (bf16[16,1312,128]{2,1,0:T(8,128)(2,1)}, s32[20480]{0:T(1024)S(1)}) custom-call(s32[8192]{0:T(1024)S(1)} %bitcast_add_fusion.slot_ref, s32[8192]{0:T(1024)S(1)} %copy-done.1, s32[20480]{0:T(1024)S(1)} %broadcast_in_dim.11.zeros_ref, bf16[8192,128]{1,0:T(8,128)(2,1)S(1)} %copy-done), custom_call_target="tpu_custom_call" | custom-call | tf_op jit(solution)/shard_map/pack_rows/pallas_call | solution.py:150
  61.8 0.1 fusion.9
  61.9 0.1 pad.4.clone
  62.0 0.8 maximum_dynamic-update-slice_fusion
  62.8 71.2 %all_to_all.30.refs_0_.refs_1_.refs_2_.refs_3_ = bf16[16,1312,128]{2,1,0:T(8,128)(2,1)S(1)} all-to-all(bf16[16,1312,128]{2,1,0:T(8,128)(2,1)} %maximum_dynamic-update-slice_fusion), channel_id=1, replica_groups=mesh['slab'=16,'coil'=8] {'slab'}, dimensions={0} | all-to-all | bytes 10747904 | tf_op jit(solution)/shard_map/all_to_all | solution.py:261
  134.0 0.0 copy-start.2
  134.0 2.3 %copy-done.2 = bf16[16,1312,128]{2,1,0:T(8,128)(2,1)} copy-done((bf16[16,1312,128]{2,1,0:T(8,128)(2,1)}, bf16[16,1312,128]{2,1,0:T(8,128)(2,1)S(1)}, u32[]{:S(2)}) %copy-start.2) | copy-done | bytes 5373976
  136.4 0.6 reshape.36.rows_ref
  137.0 0.0 copy-start.4
  137.0 0.0 copy-start.3
  137.0 47.0 %add_rows.1 = bf16[4096,32]{1,0:T(8,128)(2,1)} custom-call(s32[20480]{0:T(1024)} %reshape.36.rows_ref, bf16[16,1312,128]{2,1,0:T(8,128)(2,1)} %copy-done.2, bf16[16,1312,128]{2,1,0:T(8,128)(2,1)} %copy-done.2, bf16[16,1312,128]{2,1,0:T(8,128)(2,1)} %copy-done.2, bf16[16,1312,128]{2,1,0:T(8,128)(2,1)} %copy-done.2, bf16[4,128,32]{2,1,0:T(8,128)(2,1)} %constant.54.clone.refs_4_), custom_call_target="tpu_custom_call" | custom-call | tf_op jit(solution)/shard_map/add_rows/pallas_call | solution.py:214
  184.1 0.0 copy-start.5
  184.1 1.6 copy.23
  185.7 0.0 copy-done.4
  185.7 0.3 fusion.2
  186.0 0.2 copy.25
  186.2 11.2 %all_to_all.31 = bf16[16,16,512]{2,0,1:T(8,128)(2,1)S(1)} all-to-all(bf16[16,16,512]{2,0,1:T(8,128)(2,1)S(1)} %copy.25), channel_id=1, replica_groups=mesh['slab'=16,'coil'=8] {'slab'}, dimensions={1} | all-to-all | bytes 524288 | tf_op jit(solution)/shard_map/all_to_all | solution.py:274
  197.4 0.1 reshape.38
  197.5 0.2 copy.26
  197.7 0.0 copy-done.3
  197.7 0.3 fusion.5
  198.0 0.2 copy.27
  198.2 0.9 reshape.39
  199.1 4.2 %all-to-all-start.2 = ((bf16[16,16,512]{2,1,0:T(8,128)(2,1)}), bf16[16,16,512]{2,1,0:T(8,128)(2,1)}, u32[]{:S(2)}, u32[]{:S(2)}) async-start(bf16[16,16,512]{2,1,0:T(8,128)(2,1)} %reshape.39), calls=%async_computation.2 | async-start | bytes 524288 | tf_op jit(solution)/shard_map/all_to_all | solution.py:280
  203.3 0.0 copy-done.5
  203.3 0.2 fusion.13
  203.6 8.2 %all-to-all-done.2 = bf16[16,16,512]{2,1,0:T(8,128)(2,1)} async-done(((bf16[16,16,512]{2,1,0:T(8,128)(2,1)}), bf16[16,16,512]{2,1,0:T(8,128)(2,1)}, u32[]{:S(2)}, u32[]{:S(2)}) %all-to-all-start.2) | async-done | bytes 262176 | tf_op jit(solution)/shard_map/all_to_all | solution.py:280
  211.8 5.3 %all-to-all-start.3 = ((bf16[8,2,16,512]{3,2,1,0:T(8,128)(2,1)}), bf16[8,2,16,512]{3,2,1,0:T(8,128)(2,1)S(1)}, u32[]{:S(2)}, u32[]{:S(2)}) async-start(bf16[8,2,16,512]{3,2,1,0:T(8,128)(2,1)} %bitcast.17), calls=%async_computation.3 | async-start | bytes 524288 | tf_op jit(solution)/shard_map/all_to_all | solution.py:285
  217.1 7.5 %all-to-all-done.3 = bf16[8,2,16,512]{3,2,1,0:T(8,128)(2,1)S(1)} async-done(((bf16[8,2,16,512]{3,2,1,0:T(8,128)(2,1)}), bf16[8,2,16,512]{3,2,1,0:T(8,128)(2,1)S(1)}, u32[]{:S(2)}, u32[]{:S(2)}) %all-to-all-start.3) | async-done | bytes 262176 | tf_op jit(solution)/shard_map/all_to_all | solution.py:285
  224.7 0.1 add_reduce_fusion
  224.8 0.7 copy.30
  (13 shorter events, 0.2 us)
Async XLA Ops:
  0.0 37.9 %copy-start.1 = (s32[8192]{0:T(1024)S(1)}, s32[8192]{0:T(1024)}, u32[]{:S(2)}) copy-start(s32[8192]{0:T(1024)} %row_ref.1) | copy-start | bytes 98308
  37.9 1.6 copy-start
  134.0 2.3 %copy-start.2 = (bf16[16,1312,128]{2,1,0:T(8,128)(2,1)}, bf16[16,1312,128]{2,1,0:T(8,128)(2,1)S(1)}, u32[]{:S(2)}) copy-start(bf16[16,1312,128]{2,1,0:T(8,128)(2,1)S(1)} %all_to_all.30.refs_0_.refs_1_.refs_2_.refs_3_) | copy-start | bytes 16121860
  137.0 48.7 %copy-start.4 = (bf16[2,256,512,1]{2,1,0,3:T(8,128)(2,1)S(1)}, bf16[2,256,512,1]{2,1,0,3:T(8,128)(2,1)}, u32[]{:S(2)}) copy-start(bf16[2,256,512,1]{2,1,0,3:T(8,128)(2,1)} %constant.68) | copy-start | bytes 1572868
  137.0 60.7 %copy-start.3 = (bf16[2,2,256,256]{3,2,1,0:T(8,128)(2,1)S(1)}, bf16[2,2,256,256]{3,2,1,0:T(8,128)(2,1)}, u32[]{:S(2)}) copy-start(bf16[2,2,256,256]{3,2,1,0:T(8,128)(2,1)} %constant.66) | copy-start | bytes 1572868
  184.1 19.2 %copy-start.5 = (bf16[8,16,2,512]{3,2,1,0:T(2,128)(2,1)S(1)}, bf16[8,16,2,512]{3,2,1,0:T(2,128)(2,1)}, u32[]{:S(2)}) copy-start(bf16[8,16,2,512]{3,2,1,0:T(2,128)(2,1)} %param.16) | copy-start | bytes 786436
  199.1 12.7 %all-to-all-start.2 = ((bf16[16,16,512]{2,1,0:T(8,128)(2,1)}), bf16[16,16,512]{2,1,0:T(8,128)(2,1)}, u32[]{:S(2)}, u32[]{:S(2)}) async-start(bf16[16,16,512]{2,1,0:T(8,128)(2,1)} %reshape.39), calls=%async_computation.2 | async-start | bytes 524288 | tf_op jit(solution)/shard_map/all_to_all | solution.py:280
  211.8 12.8 %all-to-all-start.3 = ((bf16[8,2,16,512]{3,2,1,0:T(8,128)(2,1)}), bf16[8,2,16,512]{3,2,1,0:T(8,128)(2,1)S(1)}, u32[]{:S(2)}, u32[]{:S(2)}) async-start(bf16[8,2,16,512]{3,2,1,0:T(8,128)(2,1)} %bitcast.17), calls=%async_computation.3 | async-start | bytes 524288 | tf_op jit(solution)/shard_map/all_to_all | solution.py:285

commit v11 on v10

--- a/solution.py
+++ b/solution.py
@@ -224,7 +224,7 @@
             scratch_shapes=[pltpu.VMEM((total, 128), jnp.float32)] * LANES,
         ),
         out_shape=jax.ShapeDtypeStruct((total // table.shape[0], table.shape[2]), jnp.bfloat16),
-        compiler_params=pltpu.CompilerParams(vmem_limit_bytes=58 * 1024 * 1024),
+        compiler_params=pltpu.CompilerParams(vmem_limit_bytes=42 * 1024 * 1024),
         name="add_rows",
     )(rows, *[values] * LANES, table)
 

time: 227 us -> 225 us (level)
  Pallas kernels: 103 us -> 99.4 us
    pallas_call x1, Pallas kernels: 47 us -> 43.3 us  [add_rows(): pl.pallas_call(add_kernel, grid_spec=pltpu.PrefetchScalarGridSpec(num_sca...]
    unnamed x13 -> x17, local copies, waits for them, and re-layouts: 3.98 us -> 6.51 us
where the time goes in v11:
time: 225 us; the launch traced here: 224 us
  Pallas kernels  99.4 us (44%)
  blocking collectives  83.6 us (37%)
  waiting for transfers between devices  15.7 us (7%)
  starting transfers between devices  9.51 us (4%)
  local copies, waits for them, and re-layouts  9.27 us (4%)
  other arithmetic  2.89 us (1%)
  matrix products  2.85 us (1%)
    all_to_all x1, blocking collectives, per_device(): lax.all_to_all(packed, 'slab', split_axis=0, concat_axis=0, tiled=True)  71.3 us
    pallas_call x1, Pallas kernels, add_rows(): pl.pallas_call(add_kernel, grid_spec=pltpu.PrefetchScalarGridSpec(num_sca...  43.3 us
    pallas_call x1, Pallas kernels, grid_blocks(): pl.pallas_call(grid_kernel, grid=(blocks // STEP,), in_specs=[pl.BlockSpe...  33.9 us
    pallas_call x1, Pallas kernels, pack_rows(): pl.pallas_call(pack_kernel, grid_spec=pltpu.PrefetchScalarGridSpec(num_sc...  22.2 us
    all_to_all x1, blocking collectives, per_device(): lax.all_to_all(y_planes, 'slab', split_axis=1, concat_axis=0, tiled=True)  12.3 us
    all_to_all x1, waiting for transfers between devices, per_device(): own = lax.all_to_all(whole, 'slab', split_axis=0, concat_axis=0, tiled=True)  8.21 us
    all_to_all x1, waiting for transfers between devices, per_device(): own = lax.all_to_all(own, 'coil', split_axis=0, concat_axis=0, tiled=True)  7.51 us
    unnamed x17, local copies, waits for them, and re-layouts  6.51 us
  transfers between devices with their start and end apart: 2, of which 2 were waited for; matrix products, arithmetic and copies ran while one was open for 0% of the time, Pallas kernels for 0%

profile of v11, /device:TPU:0, one launch (start us, length us, event | category | flops | bytes accessed | tf_op | source)
XLA Modules:
  0.0 223.5 jit_solution(2688331434612171330)
XLA Ops:
  0.0 0.0 copy-start.4
  0.0 0.8 broadcast_multiply_fusion
  0.8 1.0 convert_reduce_fusion
  1.8 0.9 fusion.14
  2.7 1.3 fusion.4
  4.0 33.9 %grid_blocks.1.values_ref = bf16[8192,128]{1,0:T(8,128)(2,1)} custom-call(bf16[64,8192]{1,0:T(8,128)(2,1)} %bitcast.53, s32[1,8192]{1,0:T(1,128)} %bitcast.60, bf16[8192,128]{1,0:T(8,128)(2,1)} %bitcast.52), custom_call_target="tpu_custom_call" | custom-call | tf_op jit(solution)/shard_map/grid_blocks/pallas_call | solution.py:110
  37.9 0.0 copy-done.4
  37.9 0.0 copy-start.2
  37.9 1.6 copy-done.2
  39.5 22.2 %pack_rows.1 = (bf16[16,1312,128]{2,1,0:T(8,128)(2,1)}, s32[20480]{0:T(1024)S(1)}) custom-call(s32[8192]{0:T(1024)S(1)} %bitcast_add_fusion.slot_ref, s32[8192]{0:T(1024)S(1)} %copy-done.4, s32[20480]{0:T(1024)S(1)} %broadcast_in_dim.11.zeros_ref, bf16[8192,128]{1,0:T(8,128)(2,1)S(1)} %copy-done.2), custom_call_target="tpu_custom_call" | custom-call | tf_op jit(solution)/shard_map/pack_rows/pallas_call | solution.py:150
  61.8 0.1 fusion.9
  61.9 0.1 pad.4.clone
  62.0 0.8 maximum_dynamic-update-slice_fusion
  62.8 0.0 copy-start.3
  62.8 71.3 %all_to_all.30.refs_0_.refs_1_.refs_2_.refs_3_ = bf16[16,1312,128]{2,1,0:T(8,128)(2,1)S(1)} all-to-all(bf16[16,1312,128]{2,1,0:T(8,128)(2,1)} %maximum_dynamic-update-slice_fusion), channel_id=1, replica_groups=mesh['slab'=16,'coil'=8] {'slab'}, dimensions={0} | all-to-all | bytes 10747904 | tf_op jit(solution)/shard_map/all_to_all | solution.py:261
  134.1 0.0 copy-start
  134.1 2.3 %copy-done = bf16[16,1312,128]{2,1,0:T(8,128)(2,1)} copy-done((bf16[16,1312,128]{2,1,0:T(8,128)(2,1)}, bf16[16,1312,128]{2,1,0:T(8,128)(2,1)S(1)}, u32[]{:S(2)}) %copy-start) | copy-done | bytes 5373976
  136.5 0.0 copy-done.3
  136.5 0.0 copy-start.1
  136.5 2.5 %copy-done.1 = bf16[16,1312,128]{2,1,0:T(8,128)(2,1)S(1)} copy-done((bf16[16,1312,128]{2,1,0:T(8,128)(2,1)S(1)}, bf16[16,1312,128]{2,1,0:T(8,128)(2,1)}, u32[]{:S(2)}) %copy-start.1) | copy-done | bytes 5373976
  139.1 0.0 copy-start.6
  139.1 0.0 copy-start.5
  139.1 43.3 %add_rows.1 = bf16[4096,32]{1,0:T(8,128)(2,1)S(1)} custom-call(s32[20480]{0:T(1024)S(1)} %reshape.36.rows_ref, bf16[16,1312,128]{2,1,0:T(8,128)(2,1)S(1)} %copy-done.1, bf16[16,1312,128]{2,1,0:T(8,128)(2,1)S(1)} %copy-done.1, bf16[16,1312,128]{2,1,0:T(8,128)(2,1)S(1)} %copy-done.1, bf16[16,1312,128]{2,1,0:T(8,128)(2,1)S(1)} %copy-done.1, ...), custom_call_target="tpu_custom_call" | custom-call | tf_op jit(solution)/shard_map/add_rows/pallas_call | solution.py:214
  182.3 0.0 copy-start.7
  182.3 0.3 copy.23
  182.7 0.0 copy-done.6
  182.7 0.3 fusion.2
  183.0 0.2 copy.25
  183.2 12.3 %all_to_all.31 = bf16[16,16,512]{2,0,1:T(8,128)(2,1)S(1)} all-to-all(bf16[16,16,512]{2,0,1:T(8,128)(2,1)S(1)} %copy.25), channel_id=1, replica_groups=mesh['slab'=16,'coil'=8] {'slab'}, dimensions={1} | all-to-all | bytes 524288 | tf_op jit(solution)/shard_map/all_to_all | solution.py:274
  195.5 0.1 reshape.38
  195.6 0.2 copy.26
  195.7 0.0 copy-done.5
  195.7 0.3 fusion.5
  196.1 0.2 copy.27
  196.3 0.9 reshape.39
  197.1 4.2 %all-to-all-start.2 = ((bf16[16,16,512]{2,1,0:T(8,128)(2,1)}), bf16[16,16,512]{2,1,0:T(8,128)(2,1)}, u32[]{:S(2)}, u32[]{:S(2)}) async-start(bf16[16,16,512]{2,1,0:T(8,128)(2,1)} %reshape.39), calls=%async_computation.2 | async-start | bytes 524288 | tf_op jit(solution)/shard_map/all_to_all | solution.py:280
  201.3 0.0 copy-done.7
  201.4 0.2 fusion.13
  201.6 8.2 %all-to-all-done.2 = bf16[16,16,512]{2,1,0:T(8,128)(2,1)} async-done(((bf16[16,16,512]{2,1,0:T(8,128)(2,1)}), bf16[16,16,512]{2,1,0:T(8,128)(2,1)}, u32[]{:S(2)}, u32[]{:S(2)}) %all-to-all-start.2) | async-done | bytes 262176 | tf_op jit(solution)/shard_map/all_to_all | solution.py:280
  209.8 5.3 %all-to-all-start.3 = ((bf16[8,2,16,512]{3,2,1,0:T(8,128)(2,1)}), bf16[8,2,16,512]{3,2,1,0:T(8,128)(2,1)S(1)}, u32[]{:S(2)}, u32[]{:S(2)}) async-start(bf16[8,2,16,512]{3,2,1,0:T(8,128)(2,1)} %bitcast.17), calls=%async_computation.3 | async-start | bytes 524288 | tf_op jit(solution)/shard_map/all_to_all | solution.py:285
  215.2 7.5 %all-to-all-done.3 = bf16[8,2,16,512]{3,2,1,0:T(8,128)(2,1)S(1)} async-done(((bf16[8,2,16,512]{3,2,1,0:T(8,128)(2,1)}), bf16[8,2,16,512]{3,2,1,0:T(8,128)(2,1)S(1)}, u32[]{:S(2)}, u32[]{:S(2)}) %all-to-all-start.3) | async-done | bytes 262176 | tf_op jit(solution)/shard_map/all_to_all | solution.py:285
  222.7 0.1 add_reduce_fusion
  222.9 0.7 copy.30
  (14 shorter events, 0.3 us)
Async XLA Ops:
  0.0 37.9 %copy-start.4 = (s32[8192]{0:T(1024)S(1)}, s32[8192]{0:T(1024)}, u32[]{:S(2)}) copy-start(s32[8192]{0:T(1024)} %row_ref.1) | copy-start | bytes 98308
  37.9 1.6 copy-start.2
  62.8 73.8 %copy-start.3 = (bf16[4,128,32]{2,1,0:T(8,128)(2,1)S(1)}, bf16[4,128,32]{2,1,0:T(8,128)(2,1)}, u32[]{:S(2)}) copy-start(bf16[4,128,32]{2,1,0:T(8,128)(2,1)} %constant.54.clone.refs_4_) | copy-start | bytes 98308
  134.1 2.3 %copy-start = (bf16[16,1312,128]{2,1,0:T(8,128)(2,1)}, bf16[16,1312,128]{2,1,0:T(8,128)(2,1)S(1)}, u32[]{:S(2)}) copy-start(bf16[16,1312,128]{2,1,0:T(8,128)(2,1)S(1)} %all_to_all.30.refs_0_.refs_1_.refs_2_.refs_3_) | copy-start | bytes 16121860
  136.5 2.5 %copy-start.1 = (bf16[16,1312,128]{2,1,0:T(8,128)(2,1)S(1)}, bf16[16,1312,128]{2,1,0:T(8,128)(2,1)}, u32[]{:S(2)}) copy-start(bf16[16,1312,128]{2,1,0:T(8,128)(2,1)} %copy-done) | copy-start | bytes 16121860
  139.1 43.7 %copy-start.6 = (bf16[2,256,512,1]{2,1,0,3:T(8,128)(2,1)S(1)}, bf16[2,256,512,1]{2,1,0,3:T(8,128)(2,1)}, u32[]{:S(2)}) copy-start(bf16[2,256,512,1]{2,1,0,3:T(8,128)(2,1)} %constant.68) | copy-start | bytes 1572868
  139.1 56.7 %copy-start.5 = (bf16[2,2,256,256]{3,2,1,0:T(8,128)(2,1)S(1)}, bf16[2,2,256,256]{3,2,1,0:T(8,128)(2,1)}, u32[]{:S(2)}) copy-start(bf16[2,2,256,256]{3,2,1,0:T(8,128)(2,1)} %constant.66) | copy-start | bytes 1572868
  182.3 19.0 %copy-start.7 = (bf16[8,16,2,512]{3,2,1,0:T(2,128)(2,1)S(1)}, bf16[8,16,2,512]{3,2,1,0:T(2,128)(2,1)}, u32[]{:S(2)}) copy-start(bf16[8,16,2,512]{3,2,1,0:T(2,128)(2,1)} %param.16) | copy-start | bytes 786436
  197.1 12.7 %all-to-all-start.2 = ((bf16[16,16,512]{2,1,0:T(8,128)(2,1)}), bf16[16,16,512]{2,1,0:T(8,128)(2,1)}, u32[]{:S(2)}, u32[]{:S(2)}) async-start(bf16[16,16,512]{2,1,0:T(8,128)(2,1)} %reshape.39), calls=%async_computation.2 | async-start | bytes 524288 | tf_op jit(solution)/shard_map/all_to_all | solution.py:280
  209.8 12.9 %all-to-all-start.3 = ((bf16[8,2,16,512]{3,2,1,0:T(8,128)(2,1)}), bf16[8,2,16,512]{3,2,1,0:T(8,128)(2,1)S(1)}, u32[]{:S(2)}, u32[]{:S(2)}) async-start(bf16[8,2,16,512]{3,2,1,0:T(8,128)(2,1)} %bitcast.17), calls=%async_computation.3 | async-start | bytes 524288 | tf_op jit(solution)/shard_map/all_to_all | solution.py:285
